TPU v7x, 256 devices: a whole 4x4x8 slice. The times are simulated.
256 devices in a mesh: section: 2 (over y_lo), blk: 128 (over y_hi, x, z, core).
Axes of the slice: x: 4, y: 4 (y_hi: 2, y_lo: 2; y = y_hi * 2 + y_lo), z: 8, core: 2. Of those that a mesh axis runs over, the one named last changes fastest.
Arguments:
- traces: bfloat16 [8, 4096, 6144], P('section', 'blk'), may hold values from -8 to 8
- counts: int32 [128], P('blk'), may hold values from 1 to 32, 2560 in all
- taps: float32 [64], replicated, may hold values from -0.75 to 0.75
- masks: int32 [6], replicated, may hold values from 1 to 127, as said below
Outputs:
- cross: bfloat16 [128, 6, 2, 32, 32, 768], P('blk', None, None, None, None, 'section')
Inputs may be any that keep to these rules, and one draw needn't show every extreme that they name: The first counts[b] slots of block b hold its live channels; the counts sum to 2560. The masks are distinct; one round pairs block b with block 127 - b, and one with block b XOR 1.
All inputs are finite; a program needn't handle non-finite values.
Results may differ from a plain program's by a relative error of at most 0.0067.
Values may be sent and summed in bfloat16 or wider, within the bound.
No kernel may reach another device: no remote copies, remote signals or barrier semaphores. Data moves between devices by JAX's collectives and lax.ppermute only.
A program may use at most 128 MiB of HBM per device.

v0:
```python
import math

import jax
import jax.numpy as jnp
from jax import lax
from jax.sharding import PartitionSpec as P

F = 768


def swapped(block, axis, stride):
    count = lax.axis_size(axis)
    route = []
    for low in range(count):
        high = low | 1 << stride
        if high != low and high < count:
            route += [(low, high), (high, low)]
    return lax.ppermute(block, axis, route)


def dft_table(start, count, length):
    times = jnp.arange(count, dtype=jnp.int32) + start
    freqs = jnp.arange(F, dtype=jnp.int32)
    phase = times[:, None] * freqs[None, :] % length
    angle = phase.astype(jnp.float32) * (2.0 * math.pi / length)
    return jnp.concatenate([jnp.cos(angle), -jnp.sin(angle)], axis=1).astype(jnp.bfloat16)


def response(taps, length):
    steps = jnp.arange(taps.shape[0], dtype=jnp.int32)
    freqs = jnp.arange(F, dtype=jnp.int32)
    phase = steps[:, None] * freqs[None, :] % length
    angle = phase.astype(jnp.float32) * (2.0 * math.pi / length)
    real = jnp.dot(taps, jnp.cos(angle), precision=lax.Precision.HIGHEST)
    imag = -jnp.dot(taps, jnp.sin(angle), precision=lax.Precision.HIGHEST)
    return (real, imag)


def clip_rows(signal):
    values = signal.astype(jnp.float32)
    level = jnp.sqrt(jnp.mean(values * values, axis=1, keepdims=True) + 1e-06)
    return jnp.clip(values, -2.5 * level, 2.5 * level).astype(jnp.bfloat16)


def whiten(spectrum, live, real_resp, imag_resp):
    real_part = spectrum[:, :F]
    imag_part = spectrum[:, F:]
    filt_re = real_part * real_resp - imag_part * imag_resp
    filt_im = real_part * imag_resp + imag_part * real_resp
    power = jnp.mean(filt_re * filt_re + filt_im * filt_im, axis=1, keepdims=True) + 1e-06
    scale = live[:, None] / jnp.sqrt(power)
    return jnp.stack([filt_re * scale, filt_im * scale], axis=1).astype(jnp.bfloat16)


def bit_sequence(count):
    return list(range(count))


def partner_of(spectra, mask_value, bits):
    held = spectra
    for bit in bits:
        moved = swapped(held, "blk", bit)
        held = jnp.where(mask_value >> bit & 1 == 1, moved, held)
    return held


def shards(traces, counts, taps, masks):
    segs, cap, length = traces.shape
    real_resp, imag_resp = response(taps, length)
    live_one = (jnp.arange(cap, dtype=jnp.int32) < counts[0]).astype(jnp.float32)
    live = jnp.tile(live_one, segs)
    clipped = clip_rows(traces.reshape(segs * cap, length))
    step = 1024
    spectrum = jnp.zeros((segs * cap, 2 * F), jnp.float32)
    for start in range(0, length, step):
        spectrum = spectrum + jnp.dot(
            clipped[:, start : start + step],
            dft_table(start, step, length),
            preferred_element_type=jnp.float32,
        )
    local_spec = whiten(spectrum, live, real_resp, imag_resp).reshape(segs, cap, 2, F)
    spectra = lax.all_to_all(local_spec, "section", split_axis=3, concat_axis=0, tiled=True)
    total_segs = spectra.shape[0]
    other = jnp.concatenate([spectra[:, :, 1:2], -spectra[:, :, 0:1]], axis=2)
    left = jnp.stack([spectra, other])
    rounds = masks.shape[0]
    bits = bit_sequence(lax.axis_size("blk").bit_length() - 1)
    results = []
    for rnd in range(rounds):
        total = jnp.einsum(
            "asikf,sjkf->aijf",
            left,
            partner_of(spectra, masks[rnd], bits),
            preferred_element_type=jnp.float32,
        )
        results.append((total * (1.0 / total_segs)).astype(jnp.bfloat16))
    return jnp.stack(results)[None]


def solution(mesh):
    return jax.shard_map(
        shards,
        mesh=mesh,
        in_specs=(P("section", "blk", None), P("blk"), P(), P()),
        out_specs=P("blk", None, None, None, None, "section"),
        check_vma=False,
    )
```

profile of v0, /device:TPU:224, one launch (start us, length us, event | category | flops | bytes accessed | tf_op | source)
XLA Modules:
  0.0 623.8 jit_solution(11531116691799523096)
XLA Ops:
  0.0 14.0 %negate_convert_fusion.5 = (bf16[1024,768]{1,0:T(8,128)(2,1)S(1)}, bf16[1024,768]{1,0:T(8,128)(2,1)}) fusion(), kind=kLoop, calls=%fused_computation.88 | loop fusion | flops 9437184 | bytes 3145728 | tf_op jit(solution)/shard_map/convert.16
  17.4 13.7 %cosine_convert_fusion.4 = (bf16[1024,768]{1,0:T(8,128)(2,1)S(1)}, bf16[1024,768]{1,0:T(8,128)(2,1)S(1)}) fusion(s32[1024]{0:T(1024)S(1)} %iota_add_fusion.4), kind=kLoop, calls=%fused_computation.84 | loop fusion | flops 9437184 | bytes 3149824 | tf_op jit(solution)/shard_map/convert.13
  31.1 13.8 %cosine_convert_fusion.3 = (bf16[1024,768]{1,0:T(8,128)(2,1)S(1)}, bf16[1024,768]{1,0:T(8,128)(2,1)S(1)}) fusion(s32[1024]{0:T(1024)S(1)} %iota_add_fusion.3), kind=kLoop, calls=%fused_computation.79 | loop fusion | flops 9437184 | bytes 3149824 | tf_op jit(solution)/shard_map/convert.11
  44.9 13.8 %cosine_convert_fusion.2 = (bf16[1024,768]{1,0:T(8,128)(2,1)S(1)}, bf16[1024,768]{1,0:T(8,128)(2,1)S(1)}) fusion(s32[1024]{0:T(1024)S(1)} %iota_add_fusion.2), kind=kLoop, calls=%fused_computation.74 | loop fusion | flops 9437184 | bytes 3149824 | tf_op jit(solution)/shard_map/convert.9
  58.6 13.8 %cosine_convert_fusion.1 = (bf16[1024,768]{1,0:T(8,128)(2,1)S(1)}, bf16[1024,768]{1,0:T(8,128)(2,1)S(1)}) fusion(s32[1024]{0:T(1024)S(1)} %iota_add_fusion.1), kind=kLoop, calls=%fused_computation.69 | loop fusion | flops 9437184 | bytes 3149824 | tf_op jit(solution)/shard_map/convert.7
  72.4 14.0 %cosine_convert_fusion = (bf16[1024,768]{1,0:T(8,128)(2,1)S(1)}, bf16[1024,768]{1,0:T(8,128)(2,1)S(1)}) fusion(s32[1024]{0:T(1024)S(1)} %iota_add_fusion), kind=kLoop, calls=%fused_computation.64 | loop fusion | flops 9437184 | bytes 3149824 | tf_op jit(solution)/shard_map/convert.5
  94.9 9.3 %all_to_all.18 = bf16[2,2,49152]{2,1,0:T(2,128)(2,1)S(1)} all-to-all(bf16[2,2,49152]{2,1,0:T(2,128)(2,1)S(1)} %reshape.353), channel_id=1, replica_groups=mesh['section'=2,'blk'=128] {'section'}, dimensions={0} | all-to-all | bytes 786432 | tf_op jit(solution)/shard_map/all_to_all | solution.py:82
  157.4 14.2 %collective-permute-done.13 = bf16[8,32,2,384]{3,1,2,0:T(8,128)(2,1)S(1)} collective-permute-done((bf16[8,32,2,384]{3,1,2,0:T(8,128)(2,1)}, bf16[8,32,2,384]{3,1,2,0:T(8,128)(2,1)S(1)}, u32[]{:S(2)}, u32[]{:S(2)}) %collective-permute-start.13) | collective-permute-done | bytes 393248 | tf_op jit(solution)/shard_map/ppermute | solution.py:18
  172.8 15.7 %collective-permute-done.19 = bf16[8,32,2,384]{3,1,2,0:T(8,128)(2,1)S(1)} collective-permute-done((bf16[8,32,2,384]{3,1,2,0:T(8,128)(2,1)}, bf16[8,32,2,384]{3,1,2,0:T(8,128)(2,1)S(1)}, u32[]{:S(2)}, u32[]{:S(2)}) %collective-permute-start.19) | collective-permute-done | bytes 393248 | tf_op jit(solution)/shard_map/ppermute | solution.py:18
  188.6 8.4 %collective-permute-done.25 = bf16[8,32,2,384]{3,1,2,0:T(8,128)(2,1)S(1)} collective-permute-done((bf16[8,32,2,384]{3,1,2,0:T(8,128)(2,1)}, bf16[8,32,2,384]{3,1,2,0:T(8,128)(2,1)S(1)}, u32[]{:S(2)}, u32[]{:S(2)}) %collective-permute-start.25) | collective-permute-done | bytes 393248 | tf_op jit(solution)/shard_map/ppermute | solution.py:18
  197.2 7.9 %collective-permute-done.31 = bf16[8,32,2,384]{3,1,2,0:T(8,128)(2,1)S(1)} collective-permute-done((bf16[8,32,2,384]{3,1,2,0:T(8,128)(2,1)S(1)}, bf16[8,32,2,384]{3,1,2,0:T(8,128)(2,1)S(1)}, u32[]{:S(2)}, u32[]{:S(2)}) %collective-permute-start.31) | collective-permute-done | bytes 393248 | tf_op jit(solution)/shard_map/ppermute | solution.py:18
  209.8 55.2 %collective-permute-done.14 = bf16[8,32,2,384]{3,1,2,0:T(8,128)(2,1)S(1)} collective-permute-done((bf16[8,32,2,384]{3,1,2,0:T(8,128)(2,1)S(1)}, bf16[8,32,2,384]{3,1,2,0:T(8,128)(2,1)S(1)}, u32[]{:S(2)}, u32[]{:S(2)}) %collective-permute-start.14) | collective-permute-done | bytes 393248 | tf_op jit(solution)/shard_map/ppermute | solution.py:18
  265.0 17.0 %collective-permute-done.20 = bf16[8,32,2,384]{3,1,2,0:T(8,128)(2,1)S(1)} collective-permute-done((bf16[8,32,2,384]{3,1,2,0:T(8,128)(2,1)S(1)}, bf16[8,32,2,384]{3,1,2,0:T(8,128)(2,1)S(1)}, u32[]{:S(2)}, u32[]{:S(2)}) %collective-permute-start.20) | collective-permute-done | bytes 393248 | tf_op jit(solution)/shard_map/ppermute | solution.py:18
  282.1 16.9 %collective-permute-done.26 = bf16[8,32,2,384]{3,1,2,0:T(8,128)(2,1)S(1)} collective-permute-done((bf16[8,32,2,384]{3,1,2,0:T(8,128)(2,1)S(1)}, bf16[8,32,2,384]{3,1,2,0:T(8,128)(2,1)S(1)}, u32[]{:S(2)}, u32[]{:S(2)}) %collective-permute-start.26) | collective-permute-done | bytes 393248 | tf_op jit(solution)/shard_map/ppermute | solution.py:18
  299.1 75.4 %collective-permute-done.32 = bf16[8,32,2,384]{3,1,2,0:T(8,128)(2,1)S(1)} collective-permute-done((bf16[8,32,2,384]{3,1,2,0:T(8,128)(2,1)S(1)}, bf16[8,32,2,384]{3,1,2,0:T(8,128)(2,1)S(1)}, u32[]{:S(2)}, u32[]{:S(2)}) %collective-permute-start.32) | collective-permute-done | bytes 393248 | tf_op jit(solution)/shard_map/ppermute | solution.py:18
  384.7 18.9 %collective-permute-done.27 = bf16[8,32,2,384]{3,1,2,0:T(8,128)(2,1)S(1)} collective-permute-done((bf16[8,32,2,384]{3,1,2,0:T(8,128)(2,1)S(1)}, bf16[8,32,2,384]{3,1,2,0:T(8,128)(2,1)S(1)}, u32[]{:S(2)}, u32[]{:S(2)}) %collective-permute-start.27) | collective-permute-done | bytes 393248 | tf_op jit(solution)/shard_map/ppermute | solution.py:18
  437.9 7.5 %collective-permute-done.5 = bf16[8,32,2,384]{3,1,2,0:T(8,128)(2,1)S(1)} collective-permute-done((bf16[8,32,2,384]{3,1,2,0:T(8,128)(2,1)S(1)}, bf16[8,32,2,384]{3,1,2,0:T(8,128)(2,1)S(1)}, u32[]{:S(2)}, u32[]{:S(2)}) %collective-permute-start.5) | collective-permute-done | bytes 393248 | tf_op jit(solution)/shard_map/ppermute | solution.py:18
  446.3 7.6 %collective-permute-done.11 = bf16[8,32,2,384]{3,1,2,0:T(8,128)(2,1)S(1)} collective-permute-done((bf16[8,32,2,384]{3,1,2,0:T(8,128)(2,1)S(1)}, bf16[8,32,2,384]{3,1,2,0:T(8,128)(2,1)S(1)}, u32[]{:S(2)}, u32[]{:S(2)}) %collective-permute-start.11) | collective-permute-done | bytes 393248 | tf_op jit(solution)/shard_map/ppermute | solution.py:18
  522.2 10.4 %copy.68 = bf16[1,2,32,32,384]{4,3,2,1,0:T(8,128)(2,1)} copy(bf16[1,2,32,32,384]{2,3,1,4,0:T(8,128)(2,1)} %fusion.6) | data formatting | bytes 3145728 | tf_op jit(solution)/shard_map/stack | solution.py:97
  532.6 10.4 %copy.69 = bf16[1,2,32,32,384]{4,3,2,1,0:T(8,128)(2,1)} copy(bf16[1,2,32,32,384]{2,3,1,4,0:T(8,128)(2,1)} %fusion.7) | data formatting | bytes 3145728 | tf_op jit(solution)/shard_map/stack | solution.py:97
  543.0 10.5 %copy.70 = bf16[1,2,32,32,384]{4,3,2,1,0:T(8,128)(2,1)} copy(bf16[1,2,32,32,384]{2,3,1,4,0:T(8,128)(2,1)} %fusion.8) | data formatting | bytes 3145728 | tf_op jit(solution)/shard_map/stack | solution.py:97
  562.5 10.4 %copy.71 = bf16[1,2,32,32,384]{4,3,2,1,0:T(8,128)(2,1)} copy(bf16[1,2,32,32,384]{2,3,1,4,0:T(8,128)(2,1)} %fusion.9) | data formatting | bytes 3145728 | tf_op jit(solution)/shard_map/stack | solution.py:97
  583.5 10.5 %copy.72 = bf16[1,2,32,32,384]{4,3,2,1,0:T(8,128)(2,1)} copy(bf16[1,2,32,32,384]{2,3,1,4,0:T(8,128)(2,1)} %fusion.10) | data formatting | bytes 3145728 | tf_op jit(solution)/shard_map/stack | solution.py:97
  606.2 10.0 %copy.73 = bf16[1,2,32,32,384]{4,3,2,1,0:T(8,128)(2,1)S(1)} copy(bf16[1,2,32,32,384]{2,3,1,4,0:T(8,128)(2,1)} %fusion.11) | data formatting | bytes 3145728 | tf_op jit(solution)/shard_map/stack | solution.py:97
  (176 shorter events, 197.0 us)
Async XLA Ops:
  144.2 44.3 %collective-permute-start.19 = (bf16[8,32,2,384]{3,1,2,0:T(8,128)(2,1)}, bf16[8,32,2,384]{3,1,2,0:T(8,128)(2,1)S(1)}, u32[]{:S(2)}, u32[]{:S(2)}) collective-permute-start(bf16[8,32,2,384]{3,1,2,0:T(8,128)(2,1)} %get-tuple-element.9), channel_id=1, source_target_pairs={{0,2},{2,0},{1,3},{3,1},{4,6},{6,4},{5,7},{7,5},{8,10},{10,8},{9,1... | collective-permute-start | bytes 1179656 | tf_op jit(solution)/shard_map/ppermute | solution.py:18
  145.2 51.8 %collective-permute-start.25 = (bf16[8,32,2,384]{3,1,2,0:T(8,128)(2,1)}, bf16[8,32,2,384]{3,1,2,0:T(8,128)(2,1)S(1)}, u32[]{:S(2)}, u32[]{:S(2)}) collective-permute-start(bf16[8,32,2,384]{3,1,2,0:T(8,128)(2,1)} %get-tuple-element.8), channel_id=1, source_target_pairs={{0,2},{2,0},{1,3},{3,1},{4,6},{6,4},{5,7},{7,5},{8,10},{10,8},{9,1... | collective-permute-start | bytes 1179656 | tf_op jit(solution)/shard_map/ppermute | solution.py:18
  146.5 58.6 %collective-permute-start.31 = (bf16[8,32,2,384]{3,1,2,0:T(8,128)(2,1)S(1)}, bf16[8,32,2,384]{3,1,2,0:T(8,128)(2,1)S(1)}, u32[]{:S(2)}, u32[]{:S(2)}) collective-permute-start(bf16[8,32,2,384]{3,1,2,0:T(8,128)(2,1)S(1)} %get-tuple-element.7), channel_id=1, source_target_pairs={{0,2},{2,0},{1,3},{3,1},{4,6},{6,4},{5,7},{7,5},{8,10},{10,8},{9,1... | collective-permute-start | bytes 1179656 | tf_op jit(solution)/shard_map/ppermute | solution.py:18
  154.9 50.2 %collective-permute-start.2 = (bf16[8,32,2,384]{3,1,2,0:T(8,128)(2,1)S(1)}, bf16[8,32,2,384]{3,1,2,0:T(8,128)(2,1)S(1)}, u32[]{:S(2)}, u32[]{:S(2)}) collective-permute-start(bf16[8,32,2,384]{3,1,2,0:T(8,128)(2,1)S(1)} %broadcast_select_fusion.31), channel_id=1, source_target_pairs={{0,4},{4,0},{1,5},{5,1},{2,6},{6,2},{3,7},{7,3},{8,12},{12,8},{9,1... | collective-permute-start | bytes 1179656 | tf_op jit(solution)/shard_map/ppermute | solution.py:18
  171.7 36.5 %collective-permute-start.8 = (bf16[8,32,2,384]{3,1,2,0:T(8,128)(2,1)S(1)}, bf16[8,32,2,384]{3,1,2,0:T(8,128)(2,1)S(1)}, u32[]{:S(2)}, u32[]{:S(2)}) collective-permute-start(bf16[8,32,2,384]{3,1,2,0:T(8,128)(2,1)S(1)} %broadcast_select_fusion.25), channel_id=1, source_target_pairs={{0,4},{4,0},{1,5},{5,1},{2,6},{6,2},{3,7},{7,3},{8,12},{12,8},{9,1... | collective-permute-start | bytes 1179656 | tf_op jit(solution)/shard_map/ppermute | solution.py:18
  188.5 76.4 %collective-permute-start.14 = (bf16[8,32,2,384]{3,1,2,0:T(8,128)(2,1)S(1)}, bf16[8,32,2,384]{3,1,2,0:T(8,128)(2,1)S(1)}, u32[]{:S(2)}, u32[]{:S(2)}) collective-permute-start(bf16[8,32,2,384]{3,1,2,0:T(8,128)(2,1)S(1)} %broadcast_select_fusion.19), channel_id=1, source_target_pairs={{0,4},{4,0},{1,5},{5,1},{2,6},{6,2},{3,7},{7,3},{8,12},{12,8},{9,1... | collective-permute-start | bytes 1179656 | tf_op jit(solution)/shard_map/ppermute | solution.py:18
  197.0 85.0 %collective-permute-start.20 = (bf16[8,32,2,384]{3,1,2,0:T(8,128)(2,1)S(1)}, bf16[8,32,2,384]{3,1,2,0:T(8,128)(2,1)S(1)}, u32[]{:S(2)}, u32[]{:S(2)}) collective-permute-start(bf16[8,32,2,384]{3,1,2,0:T(8,128)(2,1)S(1)} %broadcast_select_fusion.13), channel_id=1, source_target_pairs={{0,4},{4,0},{1,5},{5,1},{2,6},{6,2},{3,7},{7,3},{8,12},{12,8},{9,1... | collective-permute-start | bytes 1179656 | tf_op jit(solution)/shard_map/ppermute | solution.py:18
  205.1 93.9 %collective-permute-start.26 = (bf16[8,32,2,384]{3,1,2,0:T(8,128)(2,1)S(1)}, bf16[8,32,2,384]{3,1,2,0:T(8,128)(2,1)S(1)}, u32[]{:S(2)}, u32[]{:S(2)}) collective-permute-start(bf16[8,32,2,384]{3,1,2,0:T(8,128)(2,1)S(1)} %broadcast_select_fusion.7), channel_id=1, source_target_pairs={{0,4},{4,0},{1,5},{5,1},{2,6},{6,2},{3,7},{7,3},{8,12},{12,8},{9,1... | collective-permute-start | bytes 1179656 | tf_op jit(solution)/shard_map/ppermute | solution.py:18
  205.1 169.3 %collective-permute-start.32 = (bf16[8,32,2,384]{3,1,2,0:T(8,128)(2,1)S(1)}, bf16[8,32,2,384]{3,1,2,0:T(8,128)(2,1)S(1)}, u32[]{:S(2)}, u32[]{:S(2)}) collective-permute-start(bf16[8,32,2,384]{3,1,2,0:T(8,128)(2,1)S(1)} %broadcast_select_fusion.1), channel_id=1, source_target_pairs={{0,4},{4,0},{1,5},{5,1},{2,6},{6,2},{3,7},{7,3},{8,12},{12,8},{9,1... | collective-permute-start | bytes 1179656 | tf_op jit(solution)/shard_map/ppermute | solution.py:18
  208.2 166.3 %collective-permute-start.3 = (bf16[8,32,2,384]{3,1,2,0:T(8,128)(2,1)S(1)}, bf16[8,32,2,384]{3,1,2,0:T(8,128)(2,1)S(1)}, u32[]{:S(2)}, u32[]{:S(2)}) collective-permute-start(bf16[8,32,2,384]{3,1,2,0:T(8,128)(2,1)S(1)} %broadcast_select_fusion.32), channel_id=1, source_target_pairs={{0,8},{8,0},{1,9},{9,1},{2,10},{10,2},{3,11},{11,3},{4,12},{12,4},... | collective-permute-start | bytes 1179656 | tf_op jit(solution)/shard_map/ppermute | solution.py:18
  264.9 115.6 %collective-permute-start.9 = (bf16[8,32,2,384]{3,1,2,0:T(8,128)(2,1)S(1)}, bf16[8,32,2,384]{3,1,2,0:T(8,128)(2,1)S(1)}, u32[]{:S(2)}, u32[]{:S(2)}) collective-permute-start(bf16[8,32,2,384]{3,1,2,0:T(8,128)(2,1)S(1)} %broadcast_select_fusion.26), channel_id=1, source_target_pairs={{0,8},{8,0},{1,9},{9,1},{2,10},{10,2},{3,11},{11,3},{4,12},{12,4},... | collective-permute-start | bytes 1179656 | tf_op jit(solution)/shard_map/ppermute | solution.py:18
  282.0 100.2 %collective-permute-start.15 = (bf16[8,32,2,384]{3,1,2,0:T(8,128)(2,1)S(1)}, bf16[8,32,2,384]{3,1,2,0:T(8,128)(2,1)S(1)}, u32[]{:S(2)}, u32[]{:S(2)}) collective-permute-start(bf16[8,32,2,384]{3,1,2,0:T(8,128)(2,1)S(1)} %broadcast_select_fusion.20), channel_id=1, source_target_pairs={{0,8},{8,0},{1,9},{9,1},{2,10},{10,2},{3,11},{11,3},{4,12},{12,4},... | collective-permute-start | bytes 1179656 | tf_op jit(solution)/shard_map/ppermute | solution.py:18
  299.0 83.9 %collective-permute-start.21 = (bf16[8,32,2,384]{3,1,2,0:T(8,128)(2,1)S(1)}, bf16[8,32,2,384]{3,1,2,0:T(8,128)(2,1)S(1)}, u32[]{:S(2)}, u32[]{:S(2)}) collective-permute-start(bf16[8,32,2,384]{3,1,2,0:T(8,128)(2,1)S(1)} %broadcast_select_fusion.14), channel_id=1, source_target_pairs={{0,8},{8,0},{1,9},{9,1},{2,10},{10,2},{3,11},{11,3},{4,12},{12,4},... | collective-permute-start | bytes 1179656 | tf_op jit(solution)/shard_map/ppermute | solution.py:18
  374.5 37.4 %collective-permute-start.33 = (bf16[8,32,2,384]{3,1,2,0:T(8,128)(2,1)S(1)}, bf16[8,32,2,384]{3,1,2,0:T(8,128)(2,1)S(1)}, u32[]{:S(2)}, u32[]{:S(2)}) collective-permute-start(bf16[8,32,2,384]{3,1,2,0:T(8,128)(2,1)S(1)} %broadcast_select_fusion.2), channel_id=1, source_target_pairs={{0,8},{8,0},{1,9},{9,1},{2,10},{10,2},{3,11},{11,3},{4,12},{12,4},... | collective-permute-start | bytes 1179656 | tf_op jit(solution)/shard_map/ppermute | solution.py:18
  417.3 36.6 %collective-permute-start.11 = (bf16[8,32,2,384]{3,1,2,0:T(8,128)(2,1)S(1)}, bf16[8,32,2,384]{3,1,2,0:T(8,128)(2,1)S(1)}, u32[]{:S(2)}, u32[]{:S(2)}) collective-permute-start(bf16[8,32,2,384]{3,1,2,0:T(8,128)(2,1)S(1)} %broadcast_select_fusion.28), channel_id=1, source_target_pairs={{0,32},{32,0},{1,33},{33,1},{2,34},{34,2},{3,35},{35,3},{4,36},{36... | collective-permute-start | bytes 1179656 | tf_op jit(solution)/shard_map/ppermute | solution.py:18
  418.0 44.3 %collective-permute-start.17 = (bf16[8,32,2,384]{3,1,2,0:T(8,128)(2,1)S(1)}, bf16[8,32,2,384]{3,1,2,0:T(8,128)(2,1)S(1)}, u32[]{:S(2)}, u32[]{:S(2)}) collective-permute-start(bf16[8,32,2,384]{3,1,2,0:T(8,128)(2,1)S(1)} %broadcast_select_fusion.22), channel_id=1, source_target_pairs={{0,32},{32,0},{1,33},{33,1},{2,34},{34,2},{3,35},{35,3},{4,36},{36... | collective-permute-start | bytes 1179656 | tf_op jit(solution)/shard_map/ppermute | solution.py:18
  426.4 44.3 %collective-permute-start.23 = (bf16[8,32,2,384]{3,1,2,0:T(8,128)(2,1)S(1)}, bf16[8,32,2,384]{3,1,2,0:T(8,128)(2,1)S(1)}, u32[]{:S(2)}, u32[]{:S(2)}) collective-permute-start(bf16[8,32,2,384]{3,1,2,0:T(8,128)(2,1)S(1)} %broadcast_select_fusion.16), channel_id=1, source_target_pairs={{0,32},{32,0},{1,33},{33,1},{2,34},{34,2},{3,35},{35,3},{4,36},{36... | collective-permute-start | bytes 1179656 | tf_op jit(solution)/shard_map/ppermute | solution.py:18
  434.8 44.3 %collective-permute-start.29 = (bf16[8,32,2,384]{3,1,2,0:T(8,128)(2,1)S(1)}, bf16[8,32,2,384]{3,1,2,0:T(8,128)(2,1)S(1)}, u32[]{:S(2)}, u32[]{:S(2)}) collective-permute-start(bf16[8,32,2,384]{3,1,2,0:T(8,128)(2,1)S(1)} %broadcast_select_fusion.10), channel_id=1, source_target_pairs={{0,32},{32,0},{1,33},{33,1},{2,34},{34,2},{3,35},{35,3},{4,36},{36... | collective-permute-start | bytes 1179656 | tf_op jit(solution)/shard_map/ppermute | solution.py:18
  445.5 40.6 %collective-permute-start.35 = (bf16[8,32,2,384]{3,1,2,0:T(8,128)(2,1)S(1)}, bf16[8,32,2,384]{3,1,2,0:T(8,128)(2,1)S(1)}, u32[]{:S(2)}, u32[]{:S(2)}) collective-permute-start(bf16[8,32,2,384]{3,1,2,0:T(8,128)(2,1)S(1)} %broadcast_select_fusion.4), channel_id=1, source_target_pairs={{0,32},{32,0},{1,33},{33,1},{2,34},{34,2},{3,35},{35,3},{4,36},{36... | collective-permute-start | bytes 1179656 | tf_op jit(solution)/shard_map/ppermute | solution.py:18
  462.3 37.1 %collective-permute-start.12 = (bf16[8,32,2,384]{3,1,2,0:T(8,128)(2,1)}, bf16[8,32,2,384]{3,1,2,0:T(8,128)(2,1)}, u32[]{:S(2)}, u32[]{:S(2)}) collective-permute-start(bf16[8,32,2,384]{3,1,2,0:T(8,128)(2,1)} %broadcast_select_fusion.29), channel_id=1, source_target_pairs={{0,64},{64,0},{1,65},{65,1},{2,66},{66,2},{3,67},{67,3},{4,68},{68... | collective-permute-start | bytes 1179656 | tf_op jit(solution)/shard_map/ppermute | solution.py:18
  470.7 39.2 %collective-permute-start.18 = (bf16[8,32,2,384]{3,1,2,0:T(8,128)(2,1)}, bf16[8,32,2,384]{3,1,2,0:T(8,128)(2,1)}, u32[]{:S(2)}, u32[]{:S(2)}) collective-permute-start(bf16[8,32,2,384]{3,1,2,0:T(8,128)(2,1)} %broadcast_select_fusion.23), channel_id=1, source_target_pairs={{0,64},{64,0},{1,65},{65,1},{2,66},{66,2},{3,67},{67,3},{4,68},{68... | collective-permute-start | bytes 1179656 | tf_op jit(solution)/shard_map/ppermute | solution.py:18
  479.2 41.2 %collective-permute-start.24 = (bf16[8,32,2,384]{3,1,2,0:T(8,128)(2,1)}, bf16[8,32,2,384]{3,1,2,0:T(8,128)(2,1)}, u32[]{:S(2)}, u32[]{:S(2)}) collective-permute-start(bf16[8,32,2,384]{3,1,2,0:T(8,128)(2,1)} %broadcast_select_fusion.17), channel_id=1, source_target_pairs={{0,64},{64,0},{1,65},{65,1},{2,66},{66,2},{3,67},{67,3},{4,68},{68... | collective-permute-start | bytes 1179656 | tf_op jit(solution)/shard_map/ppermute | solution.py:18
  486.0 86.9 %collective-permute-start.30 = (bf16[8,32,2,384]{3,1,2,0:T(8,128)(2,1)}, bf16[8,32,2,384]{3,1,2,0:T(8,128)(2,1)}, u32[]{:S(2)}, u32[]{:S(2)}) collective-permute-start(bf16[8,32,2,384]{3,1,2,0:T(8,128)(2,1)} %broadcast_select_fusion.11), channel_id=1, source_target_pairs={{0,64},{64,0},{1,65},{65,1},{2,66},{66,2},{3,67},{67,3},{4,68},{68... | collective-permute-start | bytes 1179656 | tf_op jit(solution)/shard_map/ppermute | solution.py:18
  489.3 107.4 %collective-permute-start.36 = (bf16[8,32,2,384]{3,1,2,0:T(8,128)(2,1)S(1)}, bf16[8,32,2,384]{3,1,2,0:T(8,128)(2,1)}, u32[]{:S(2)}, u32[]{:S(2)}) collective-permute-start(bf16[8,32,2,384]{3,1,2,0:T(8,128)(2,1)S(1)} %broadcast_select_fusion.5), channel_id=1, source_target_pairs={{0,64},{64,0},{1,65},{65,1},{2,66},{66,2},{3,67},{67,3},{4,68},{68... | collective-permute-start | bytes 1179656 | tf_op jit(solution)/shard_map/ppermute | solution.py:18
  (24 other events, 511.8 us)
where the time goes:
time: 633 us; the launch traced here: 624 us
  waiting for transfers between devices  285 us (45%)
  other arithmetic  104 us (16%)
  local copies, waits for them, and re-layouts  100 us (16%)
  starting transfers between devices  56.4 us (9%)
  matrix products  41.2 us (7%)
  between operations  27.7 us (4%)
  blocking collectives  9.25 us (1%)
    ppermute x37, waiting for transfers between devices, swapped(): return lax.ppermute(block, axis, route)  285 us
    another operation x7, other arithmetic  83.1 us
    another operation x7, local copies, waits for them, and re-layouts, shards(): return jnp.stack(results)[None]  63.5 us
    ppermute x37, starting transfers between devices, swapped(): return lax.ppermute(block, axis, route)  56.4 us
    dot_general x6, matrix products, shards(): jnp.einsum('asikf,sjkf->aijf', left, partner_of(spectra, masks[rnd], bits...  35.6 us
    select_n x37, other arithmetic, partner_of(): held = jnp.where(mask_value >> bit & 1 == 1, moved, held)  17.7 us
    select_n x6, local copies, waits for them, and re-layouts, partner_of(): held = jnp.where(mask_value >> bit & 1 == 1, moved, held)  16.9 us
  transfers between devices with their start and end apart: 37, of which 20 were waited for; matrix products, arithmetic and copies ran while one was open for 19% of the time, Pallas kernels for 0%

commit v1 on v0

v1 whole, which is shorter than its diff:
```python
import jax
import jax.numpy as jnp
import numpy as np
from jax import lax
from jax.experimental import pallas as pl
from jax.experimental.pallas import tpu as pltpu
from jax.sharding import Mesh
from jax.sharding import PartitionSpec as P

F = 768
L = 6144
K = 64
CAP = 32
SEG = 8
ROUNDS = 6
LOCAL = 4
HALF = F // 2
Q = L // 4
G = 256
CLASSES = (0, 2, 1, 3)
VMEM = 48 * 1024 * 1024


def angles(steps, freqs):
    return (np.outer(steps, freqs) % L) * (2.0 * np.pi / L)


def class_bins(residue):
    return 4 * np.arange(F // 4) + residue


def dft_tables():
    out = np.zeros((4, Q, 2 * G), np.float32)
    for at, residue in enumerate(CLASSES):
        angle = angles(np.arange(Q), class_bins(residue))
        out[at, :, : F // 4] = np.cos(angle)
        out[at, :, G : G + F // 4] = np.sin(angle)
    return out.astype(jnp.bfloat16)


def tap_tables():
    out = np.zeros((2, K, 4 * G), np.float32)
    for at, residue in enumerate(CLASSES):
        angle = angles(np.arange(K), class_bins(residue))
        out[0, :, at * G : at * G + F // 4] = np.cos(angle)
        out[1, :, at * G : at * G + F // 4] = np.sin(angle)
    return out


def spectra_kernel(counts, x, taps, tap_table, table, out, y, re, im):
    step = pl.program_id(0)
    rows = x.shape[0]

    @pl.when(step == 0)
    def _():
        def tile(t, carry):
            at = pl.ds(pl.multiple_of(t * 16, 16), 16)
            total = jnp.zeros((16, 128), jnp.float32)
            for c in range(L // 128):
                v = x[at, c * 128 : (c + 1) * 128].astype(jnp.float32)
                total = total + v * v
            mean = jnp.sum(total, axis=1, keepdims=True) * (1.0 / L)
            top = jnp.broadcast_to(2.5 * jnp.sqrt(mean + 1e-6), (16, 128))

            def clipped(start):
                v = x[at, start : start + 128].astype(jnp.float32)
                v = jnp.minimum(jnp.maximum(v, -top), top)
                return v.astype(jnp.bfloat16).astype(jnp.float32)

            for c in range(Q // 128):
                x0, x1, x2, x3 = [clipped(q * Q + c * 128) for q in range(4)]
                s02, d02, s13, d13 = x0 + x2, x0 - x2, x1 + x3, x1 - x3
                for n, v in enumerate((s02 + s13, s02 - s13, d02, -d13)):
                    hi = v.astype(jnp.bfloat16)
                    lo = (v - hi.astype(jnp.float32)).astype(jnp.bfloat16)
                    y[2 * n, at, c * 128 : (c + 1) * 128] = hi
                    y[2 * n + 1, at, c * 128 : (c + 1) * 128] = lo
            return carry

        lax.fori_loop(0, rows // 16, tile, 0)

    def product(n):
        a = jnp.dot(y[2 * n], table[0], preferred_element_type=jnp.float32)
        b = jnp.dot(y[2 * n + 1], table[0], preferred_element_type=jnp.float32)
        return a + b

    for at in range(2):

        @pl.when(step == at)
        def _(at=at):
            s = product(at)
            re[:, at * G : (at + 1) * G] = s[:, :G]
            im[:, at * G : (at + 1) * G] = -s[:, G:]

    for at in range(2, 4):

        @pl.when(step == at)
        def _(at=at):
            p, q = product(2), product(3)
            if at == 2:
                re[:, at * G : (at + 1) * G] = p[:, :G] + q[:, G:]
                im[:, at * G : (at + 1) * G] = q[:, :G] - p[:, G:]
            else:
                re[:, at * G : (at + 1) * G] = p[:, :G] - q[:, G:]
                im[:, at * G : (at + 1) * G] = -(p[:, G:] + q[:, :G])

    @pl.when(step == 3)
    def _():
        hr = jnp.sum(tap_table[0] * taps[...], axis=0, keepdims=True)
        hi = -jnp.sum(tap_table[1] * taps[...], axis=0, keepdims=True)
        fr = re[...] * hr - im[...] * hi
        fi = re[...] * hi + im[...] * hr
        power = jnp.sum(fr * fr + fi * fi, axis=1, keepdims=True) * (1.0 / F) + 1e-6
        slot = lax.broadcasted_iota(jnp.int32, (rows, 1), 0) % CAP
        live = jnp.where(slot < counts[0], 1.0, 0.0)
        scale = live / jnp.sqrt(power)
        white = jnp.concatenate([fr * scale, fi * scale], axis=0).astype(jnp.bfloat16)
        src = lax.broadcasted_iota(jnp.int32, (4 * G, F), 0)
        dst = lax.broadcasted_iota(jnp.int32, (4 * G, F), 1)
        residue = dst % 4
        place = jnp.where(residue == 1, 2, jnp.where(residue == 2, 1, residue))
        spread = jnp.where(src == place * G + dst // 4, 1.0, 0.0).astype(jnp.bfloat16)
        ordered = jnp.dot(white, spread, preferred_element_type=jnp.float32).astype(jnp.bfloat16)
        for half in range(2):
            for seg in range(LOCAL):
                for part in range(2):
                    start = part * rows + seg * CAP
                    out[half, seg * 2 + part] = ordered[start : start + CAP, half * HALF : (half + 1) * HALF]


def spectra_of(traces, counts, taps):
    segs, cap, length = traces.shape
    rows = segs * cap
    return pl.pallas_call(
        spectra_kernel,
        out_shape=jax.ShapeDtypeStruct((2, 2 * segs, cap, HALF), jnp.bfloat16),
        grid=(4,),
        in_specs=[
            pl.BlockSpec(memory_space=pltpu.SMEM),
            pl.BlockSpec((rows, length), lambda i: (0, 0)),
            pl.BlockSpec((K, 1), lambda i: (0, 0)),
            pl.BlockSpec((2, K, 4 * G), lambda i: (0, 0, 0)),
            pl.BlockSpec((1, Q, 2 * G), lambda i: (i, 0, 0)),
        ],
        out_specs=pl.BlockSpec((2, 2 * segs, cap, HALF), lambda i: (0, 0, 0, 0)),
        scratch_shapes=[
            pltpu.VMEM((8, rows, Q), jnp.bfloat16),
            pltpu.VMEM((rows, 4 * G), jnp.float32),
            pltpu.VMEM((rows, 4 * G), jnp.float32),
        ],
        compiler_params=pltpu.CompilerParams(vmem_limit_bytes=VMEM),
        name="spectra",
    )(counts, traces.reshape(rows, length), taps.reshape(K, 1), tap_tables(), dft_tables())


def pick_kernel(place, gathered, out, sems):
    copies = []
    for d in range(out.shape[0]):
        for r in range(out.shape[1]):
            copies.append(
                pltpu.make_async_copy(
                    gathered.at[place[0, r], :, jnp.bitwise_xor(place[1, r], d)],
                    out.at[d, r],
                    sems.at[d * out.shape[1] + r],
                )
            )
    for copy in copies:
        copy.start()
    for copy in copies:
        copy.wait()


def pick(gathered, place, rounds):
    return pl.pallas_call(
        pick_kernel,
        out_shape=jax.ShapeDtypeStruct((8, rounds, 2, CAP, HALF), jnp.bfloat16),
        in_specs=[pl.BlockSpec(memory_space=pltpu.SMEM), pl.BlockSpec(memory_space=pl.ANY)],
        out_specs=pl.BlockSpec(memory_space=pl.ANY),
        scratch_shapes=[pltpu.SemaphoreType.DMA((8 * rounds,))],
        name="pick",
    )(place, gathered)


def cross_kernel(info, mine, other, partner, kept, out, left):
    @pl.when(pl.program_id(0) == 0)
    def _():
        for where, block in ((info[0], mine), (1 - info[0], other)):
            for seg in range(LOCAL):
                a_re = block[0, 2 * seg].astype(jnp.float32) * (1.0 / SEG)
                a_im = block[0, 2 * seg + 1].astype(jnp.float32) * (1.0 / SEG)
                for n, v in enumerate((a_re + a_im, a_re, a_im)):
                    left[n * SEG + where * LOCAL + seg] = v

    def tile(at, carry):
        lanes = pl.ds(pl.multiple_of(at // 2 * 128, 128), 128)
        rows = pl.ds(pl.multiple_of(at % 2 * 16, 16), 16)
        b1, b2, b3 = [], [], []
        for sec in range(2):
            for seg in range(LOCAL):
                b_re = partner[2 * seg, 0, sec, rows, lanes].astype(jnp.float32)
                b_im = partner[2 * seg + 1, 0, sec, rows, lanes].astype(jnp.float32)
                b1.append(b_re)
                b2.append(b_re + b_im)
                b3.append(b_im - b_re)
        for i in range(CAP):
            k1 = k2 = k3 = None
            for s in range(SEG):
                t1 = left[s, i : i + 1, lanes] * b1[s]
                t2 = left[SEG + s, i : i + 1, lanes] * b2[s]
                t3 = left[2 * SEG + s, i : i + 1, lanes] * b3[s]
                k1 = t1 if k1 is None else k1 + t1
                k2 = t2 if k2 is None else k2 + t2
                k3 = t3 if k3 is None else k3 + t3
            out[0, 0, i, rows, lanes] = (k1 + k3).astype(jnp.bfloat16)
            out[0, 1, i, rows, lanes] = (k1 - k2).astype(jnp.bfloat16)
        return carry

    lax.fori_loop(0, HALF // 128 * (CAP // 16), tile, 0)


def cross_of(info, own, other, partner, kept):
    rounds = partner.shape[1]
    out = jax.ShapeDtypeStruct((ROUNDS, 2, CAP, CAP, HALF), jnp.bfloat16)
    block = (2 * LOCAL, CAP, HALF)
    fresh = kept is None
    in_specs = [
        pl.BlockSpec((1,) + block, lambda r, info: (info[0], 0, 0, 0)),
        pl.BlockSpec((1,) + block, lambda r, info: (0, 0, 0, 0)),
        pl.BlockSpec((2 * LOCAL, 1, 2, CAP, HALF), lambda r, info: (0, r, 0, 0, 0)),
    ]
    args = [own, other, partner]
    if not fresh:
        in_specs.append(pl.BlockSpec(memory_space=pl.ANY))
        args.append(kept)

    def kernel(info_ref, mine_ref, other_ref, partner_ref, *rest):
        cross_kernel(info_ref, mine_ref, other_ref, partner_ref, None, rest[-2], rest[-1])

    return pl.pallas_call(
        kernel,
        out_shape=out,
        grid_spec=pltpu.PrefetchScalarGridSpec(
            num_scalar_prefetch=1,
            grid=(rounds,),
            in_specs=in_specs,
            out_specs=pl.BlockSpec((1, 2, CAP, CAP, HALF), lambda r, info: (info[1 + r], 0, 0, 0, 0)),
            scratch_shapes=[pltpu.VMEM((3 * SEG, CAP, HALF), jnp.float32)],
        ),
        input_output_aliases={} if fresh else {4: 0},
        compiler_params=pltpu.CompilerParams(vmem_limit_bytes=VMEM),
        cost_estimate=pl.CostEstimate(flops=rounds * 8 * SEG * CAP * CAP * HALF, bytes_accessed=rounds * 2000000, transcendentals=0),
        name="cross",
    )(info, *args)


def shards(traces, counts, taps, masks):
    section = lax.axis_index("section")
    zcore = lax.axis_index("z") * 2 + lax.axis_index("core")
    near = jnp.argmax(masks == 1).astype(jnp.int32)
    far = jnp.arange(ROUNDS - 1, dtype=jnp.int32)
    far = far + (far >= near).astype(jnp.int32)
    far_masks = masks[far]

    white = spectra_of(traces, counts, taps)
    pieces = lax.all_to_all(white.reshape(16, CAP, HALF), ("section", "yh", "x"), 0, 0, tiled=True)
    gathered = lax.all_gather(pieces, ("z", "core"), axis=0, tiled=False)

    own = lax.dynamic_index_in_dim(white, section, 0, keepdims=True)
    away = lax.dynamic_index_in_dim(white, 1 - section, 0, keepdims=True)
    other = lax.ppermute(away, "section", [(0, 1), (1, 0)])
    both = jnp.where(section == 0, jnp.stack([own[0], other[0]], 1), jnp.stack([other[0], own[0]], 1))
    sibling = lax.ppermute(both, "core", [(0, 1), (1, 0)])
    first = cross_of(jnp.stack([section, near]), white, other, sibling[:, None], None)

    place = jnp.stack([jnp.bitwise_xor(zcore, far_masks & 15), far_masks >> 4])
    picked = pick(gathered.reshape(16, 2, 8, CAP, HALF), place, ROUNDS - 1)
    partners = lax.all_to_all(picked, ("yh", "x"), 0, 0, tiled=True)
    result = cross_of(jnp.concatenate([section[None], far]), white, other, partners, first)
    return result[None]


def solution(mesh):
    fine = Mesh(mesh.devices.reshape(2, 2, 4, 8, 2), ("section", "yh", "x", "z", "core"))
    blk = ("yh", "x", "z", "core")
    return jax.shard_map(
        shards,
        mesh=fine,
        in_specs=(P("section", blk, None), P(blk), P(), P()),
        out_specs=P(blk, None, None, None, None, "section"),
        check_vma=False,
    )
```

time: 633 us -> 211 us (0.33)
  the two profiles are of different devices: /device:TPU:224 before, /device:TPU:1 now
where the time goes in v1:
time: 211 us
  Pallas kernels  94.5 us (45%)
  waiting for transfers between devices  69.9 us (33%)
  blocking collectives  16.7 us (8%)
  between operations  14.1 us (7%)
  starting transfers between devices  7.99 us (4%)
  local copies, waits for them, and re-layouts  3.93 us (2%)
  other arithmetic  3.37 us (2%)
    pallas_call x1, Pallas kernels, pick(): pl.pallas_call(pick_kernel, out_shape=jax.ShapeDtypeStruct((8, rounds, 2,...  61.7 us
    all_gather x1, waiting for transfers between devices, shards(): gathered = lax.all_gather(pieces, ('z', 'core'), axis=0, tiled=False)  44 us
    ppermute x1, waiting for transfers between devices, shards(): other = lax.ppermute(away, 'section', [(0, 1), (1, 0)])  25.9 us
    pallas_call x2, Pallas kernels, cross_of(): pl.pallas_call(kernel, out_shape=out, grid_spec=pltpu.PrefetchScalarGridS...  24.3 us
    all_to_all x1, blocking collectives, shards(): lax.all_to_all(white.reshape(16, CAP, HALF), ('section', 'yh', 'x'), 0, 0...  16.7 us
    pallas_call x1, Pallas kernels, spectra_of(): pl.pallas_call(spectra_kernel, out_shape=jax.ShapeDtypeStruct((2, 2 * seg...  8.49 us
    all_to_all x1, starting transfers between devices, shards(): partners = lax.all_to_all(picked, ('yh', 'x'), 0, 0, tiled=True)  6.44 us
  transfers between devices with their start and end apart: 4, of which 2 were waited for; matrix products, arithmetic and copies ran while one was open for 2% of the time, Pallas kernels for 2%

profile of v1, /device:TPU:1, one launch (start us, length us, event | category | flops | bytes accessed | tf_op | source)
XLA Modules:
  0.0 210.5 jit_solution(10037182579118509559)
XLA Ops:
  7.2 0.7 copy.12.taps
  8.0 1.4 copy-done
  9.4 1.0 copy-done.1
  10.4 8.5 %spectra.1.mine_ref = bf16[2,8,32,384]{3,2,1,0:T(8,128)(2,1)S(1)} custom-call(s32[1]{0:T(128)S(6)} %copy.15.counts, bf16[128,6144]{1,0:T(8,128)(2,1)S(1)} %bitcast.19, f32[64,1]{1,0:T(8,128)S(1)} %copy.12.taps, f32[2,64,1024]{2,1,0:T(8,128)S(1)} %copy-done.1, bf16[4,1536,512]{2,1,0:T(8,128)(2,1)} %constant.43.clone.table), custom_call_target="tpu_custom_call" | custom-call | tf_op jit(solution)/shard_map/spectra/pallas_call | solution.py:134
  18.9 16.7 %all_to_all.10 = bf16[16,32,384]{2,1,0:T(8,128)(2,1)} all-to-all(bf16[16,32,384]{2,1,0:T(8,128)(2,1)S(1)} %bitcast.17), channel_id=1, replica_groups=mesh['section'=2,'yh'=2,'x'=4,'z'=8,'core'=2] {'section','yh','x'}, dimensions={0} | all-to-all | bytes 786432 | tf_op jit(solution)/shard_map/all_to_all | solution.py:265
  35.5 0.0 all-gather.3.cloned.1.call-update
  35.6 0.7 compare_reduce_fusion
  36.3 0.6 fusion.2
  36.9 0.6 gather_fusion
  37.6 0.6 pad_add_fusion.place
  38.2 44.0 %all-gather.3.cloned.1.call-done = bf16[256,32,384]{2,1,0:T(8,128)(2,1)} async-done(((bf16[16,32,384]{2,1,0:T(8,128)(2,1)}), bf16[256,32,384]{2,1,0:T(8,128)(2,1)}) %all-gather.3.cloned.1.call-update) | async-done | bytes 6291472 | tf_op jit(solution)/shard_map/all_gather | solution.py:266
  82.2 61.7 %pick.1 = bf16[8,5,2,32,384]{4,3,2,1,0:T(8,128)(2,1)} custom-call(s32[2,5]{1,0:T(2,128)} %pad_add_fusion.place, bf16[16,2,8,32,384]{4,3,2,1,0:T(8,128)(2,1)} %bitcast.20), custom_call_target="tpu_custom_call" | custom-call | tf_op jit(solution)/shard_map/pick/pallas_call | solution.py:174
  143.9 6.4 %all-to-all-start.1 = ((bf16[8,5,2,32,384]{4,3,2,1,0:T(8,128)(2,1)}), bf16[8,5,2,32,384]{4,3,2,1,0:T(8,128)(2,1)S(1)}, u32[]{:S(2)}, u32[]{:S(2)}) async-start(bf16[8,5,2,32,384]{4,3,2,1,0:T(8,128)(2,1)} %pick.1), calls=%async_computation.1 | async-start | bytes 3932160 | tf_op jit(solution)/shard_map/all_to_all | solution.py:277
  150.4 0.4 collective-permute-start
  150.7 25.9 %collective-permute-done.other_ref = bf16[1,8,32,384]{3,2,1,0:T(8,128)(2,1)S(1)} collective-permute-done((bf16[1,8,32,384]{3,2,1,0:T(8,128)(2,1)S(1)}, bf16[1,8,32,384]{3,2,1,0:T(8,128)(2,1)S(1)}, u32[]{:S(2)}, u32[]{:S(2)}) %collective-permute-start) | collective-permute-done | bytes 196640 | tf_op jit(solution)/shard_map/ppermute | solution.py:270
  176.7 0.1 maximum_select_fusion
  176.7 1.2 collective-permute-start.1
  177.9 0.6 fusion
  178.5 0.7 pad_add_fusion.2.info_ref
  179.2 0.1 pad_add_fusion.1.info_ref
  179.3 0.0 collective-permute-done.1
  179.4 5.2 %cross.2.rest_0_ = bf16[6,2,32,32,384]{4,3,2,1,0:T(8,128)(2,1)} custom-call(s32[2]{0:T(128)S(1)} %pad_add_fusion.2.info_ref, bf16[2,8,32,384]{3,2,1,0:T(8,128)(2,1)S(1)} %spectra.1.mine_ref, bf16[1,8,32,384]{3,2,1,0:T(8,128)(2,1)S(1)} %collective-permute-done.other_ref, bf16[8,1,2,32,384]{4,3,2,1,0:T(8,128)(2,1)S(1)} %copy.13.partner_ref), custom_call_target="tpu_custom_call" | custom-call | flops 25165824 | bytes 2000000 | tf_op jit(solution)/shard_map/cross/pallas_call | solution.py:239
  184.5 0.0 all-to-all-done.1.partner_ref
  184.5 19.2 %cross.3 = bf16[6,2,32,32,384]{4,3,2,1,0:T(8,128)(2,1)} custom-call(s32[6]{0:T(128)S(1)} %pad_add_fusion.1.info_ref, bf16[2,8,32,384]{3,2,1,0:T(8,128)(2,1)S(1)} %spectra.1.mine_ref, bf16[1,8,32,384]{3,2,1,0:T(8,128)(2,1)S(1)} %collective-permute-done.other_ref, ...), custom_call_target="tpu_custom_call", output_to_operand_aliasing={{}: (4, {})} | custom-call | flops 125829120 | bytes 10000000 | tf_op jit(solution)/shard_map/cross/pallas_call | solution.py:239
  (9 shorter events, 0.1 us)
Async XLA Ops:
  6.5 29.0 %copy-start.2 = (s32[6]{0:T(128)S(1)}, s32[6]{0:T(128)}, u32[]{:S(2)}) copy-start(s32[6]{0:T(128)} %param.9) | copy-start | bytes 76
  6.5 75.6 %all-gather.3.cloned.1.call-start = ((), (), s32[]{:S(2)}) async-start(), calls=%async_computation.2 | async-start | bytes 6684672 | tf_op jit(solution)/shard_map/all_gather | solution.py:266
  7.9 1.4 copy-start
  9.4 1.0 copy-start.1
  143.9 40.7 %all-to-all-start.1 = ((bf16[8,5,2,32,384]{4,3,2,1,0:T(8,128)(2,1)}), bf16[8,5,2,32,384]{4,3,2,1,0:T(8,128)(2,1)S(1)}, u32[]{:S(2)}, u32[]{:S(2)}) async-start(bf16[8,5,2,32,384]{4,3,2,1,0:T(8,128)(2,1)} %pick.1), calls=%async_computation.1 | async-start | bytes 3932160 | tf_op jit(solution)/shard_map/all_to_all | solution.py:277
  150.4 26.3 %collective-permute-start = (bf16[1,8,32,384]{3,2,1,0:T(8,128)(2,1)S(1)}, bf16[1,8,32,384]{3,2,1,0:T(8,128)(2,1)S(1)}, u32[]{:S(2)}, u32[]{:S(2)}) collective-permute-start(bf16[1,8,32,384]{3,2,1,0:T(8,128)(2,1)S(1)} %get-tuple-element.8), channel_id=1, source_target_pairs={{0,128},{128,0},{1,129},{129,1},{2,130},{130,2},{3,131},{131,3},{4... | collective-permute-start | bytes 589832 | tf_op jit(solution)/shard_map/ppermute | solution.py:270
  176.7 2.6 %collective-permute-start.1 = (bf16[8,2,32,384]{3,2,0,1:T(8,128)(2,1)S(1)}, bf16[8,2,32,384]{3,2,0,1:T(8,128)(2,1)S(1)}, u32[]{:S(2)}, u32[]{:S(2)}) collective-permute-start(bf16[8,2,32,384]{3,2,0,1:T(8,128)(2,1)S(1)} %maximum_select_fusion), channel_id=1, source_target_pairs={{0,1},{1,0},{2,3},{3,2},{4,5},{5,4},{6,7},{7,6},{8,9},{9,8},{10,11... | collective-permute-start | bytes 1179656 | tf_op jit(solution)/shard_map/ppermute | solution.py:272
Sparse Core Ops, SparseCore 0:
  35.7 46.4 all-gather.2

commit v2 on v1

--- a/solution.py
+++ b/solution.py
@@ -170,113 +170,138 @@
         copy.wait()
 
 
-def pick(gathered, place, rounds):
+def pick(gathered, place):
+    rounds = place.shape[1]
     return pl.pallas_call(
         pick_kernel,
         out_shape=jax.ShapeDtypeStruct((8, rounds, 2, CAP, HALF), jnp.bfloat16),
         in_specs=[pl.BlockSpec(memory_space=pltpu.SMEM), pl.BlockSpec(memory_space=pl.ANY)],
-        out_specs=pl.BlockSpec(memory_space=pl.ANY),
+        out_specs=pl.BlockSpec(memory_space=pltpu.VMEM),
         scratch_shapes=[pltpu.SemaphoreType.DMA((8 * rounds,))],
+        compiler_params=pltpu.CompilerParams(vmem_limit_bytes=VMEM),
         name="pick",
     )(place, gathered)
 
 
-def cross_kernel(info, mine, other, partner, kept, out, left):
+def products(left, right, n, lo, rows, lanes):
+    sums = [None] * 8
+    for s in range(n * SEG, (n + 1) * SEG):
+        b = right[s, rows, lanes]
+        for i in range(8):
+            t = left[s, lo + i : lo + i + 1, lanes] * b
+            sums[i] = t if sums[i] is None else sums[i] + t
+    return sums
+
+
+def cross_kernel(order, own, partner, out, left, right, by_piece):
     @pl.when(pl.program_id(0) == 0)
     def _():
-        for where, block in ((info[0], mine), (1 - info[0], other)):
-            for seg in range(LOCAL):
-                a_re = block[0, 2 * seg].astype(jnp.float32) * (1.0 / SEG)
-                a_im = block[0, 2 * seg + 1].astype(jnp.float32) * (1.0 / SEG)
-                for n, v in enumerate((a_re + a_im, a_re, a_im)):
-                    left[n * SEG + where * LOCAL + seg] = v
+        for s in range(SEG):
+            sec, seg = divmod(s, LOCAL)
+            a_re = own[sec, 2 * seg].astype(jnp.float32) * (1.0 / SEG)
+            a_im = own[sec, 2 * seg + 1].astype(jnp.float32) * (1.0 / SEG)
+            left[s] = a_re + a_im
+            left[SEG + s] = a_re
+            left[2 * SEG + s] = a_im
+
+    for s in range(SEG):
+        sec, seg = divmod(s, LOCAL)
+        if by_piece:
+            b_re, b_im = partner[2 * seg, 0, sec], partner[2 * seg + 1, 0, sec]
+        else:
+            b_re, b_im = partner[sec, 2 * seg], partner[sec, 2 * seg + 1]
+        b_re, b_im = b_re.astype(jnp.float32), b_im.astype(jnp.float32)
+        right[s] = b_re
+        right[SEG + s] = b_re + b_im
+        right[2 * SEG + s] = b_im - b_re
 
     def tile(at, carry):
         lanes = pl.ds(pl.multiple_of(at // 2 * 128, 128), 128)
         rows = pl.ds(pl.multiple_of(at % 2 * 16, 16), 16)
-        b1, b2, b3 = [], [], []
-        for sec in range(2):
-            for seg in range(LOCAL):
-                b_re = partner[2 * seg, 0, sec, rows, lanes].astype(jnp.float32)
-                b_im = partner[2 * seg + 1, 0, sec, rows, lanes].astype(jnp.float32)
-                b1.append(b_re)
-                b2.append(b_re + b_im)
-                b3.append(b_im - b_re)
-        for i in range(CAP):
-            k1 = k2 = k3 = None
-            for s in range(SEG):
-                t1 = left[s, i : i + 1, lanes] * b1[s]
-                t2 = left[SEG + s, i : i + 1, lanes] * b2[s]
-                t3 = left[2 * SEG + s, i : i + 1, lanes] * b3[s]
-                k1 = t1 if k1 is None else k1 + t1
-                k2 = t2 if k2 is None else k2 + t2
-                k3 = t3 if k3 is None else k3 + t3
-            out[0, 0, i, rows, lanes] = (k1 + k3).astype(jnp.bfloat16)
-            out[0, 1, i, rows, lanes] = (k1 - k2).astype(jnp.bfloat16)
+        for lo in range(0, CAP, 8):
+            k1 = products(left, right, 0, lo, rows, lanes)
+            k3 = products(left, right, 2, lo, rows, lanes)
+            for i in range(8):
+                out[0, 0, lo + i, rows, lanes] = (k1[i] + k3[i]).astype(jnp.bfloat16)
+            k2 = products(left, right, 1, lo, rows, lanes)
+            for i in range(8):
+                out[0, 1, lo + i, rows, lanes] = (k1[i] - k2[i]).astype(jnp.bfloat16)
         return carry
 
     lax.fori_loop(0, HALF // 128 * (CAP // 16), tile, 0)
 
 
-def cross_of(info, own, other, partner, kept):
-    rounds = partner.shape[1]
-    out = jax.ShapeDtypeStruct((ROUNDS, 2, CAP, CAP, HALF), jnp.bfloat16)
-    block = (2 * LOCAL, CAP, HALF)
-    fresh = kept is None
+def cross_of(order, own, partner, kept):
+    rounds = order.shape[0]
+    by_piece = partner.ndim == 5
+    half = (2, 2 * LOCAL, CAP, HALF)
     in_specs = [
-        pl.BlockSpec((1,) + block, lambda r, info: (info[0], 0, 0, 0)),
-        pl.BlockSpec((1,) + block, lambda r, info: (0, 0, 0, 0)),
-        pl.BlockSpec((2 * LOCAL, 1, 2, CAP, HALF), lambda r, info: (0, r, 0, 0, 0)),
+        pl.BlockSpec(half, lambda r, order: (0, 0, 0, 0)),
+        pl.BlockSpec((2 * LOCAL, 1, 2, CAP, HALF), lambda r, order: (0, r, 0, 0, 0))
+        if by_piece
+        else pl.BlockSpec(half, lambda r, order: (0, 0, 0, 0)),
     ]
-    args = [own, other, partner]
-    if not fresh:
+    args = [own, partner]
+    if kept is not None:
         in_specs.append(pl.BlockSpec(memory_space=pl.ANY))
         args.append(kept)
 
-    def kernel(info_ref, mine_ref, other_ref, partner_ref, *rest):
-        cross_kernel(info_ref, mine_ref, other_ref, partner_ref, None, rest[-2], rest[-1])
+    def kernel(order_ref, own_ref, partner_ref, *rest):
+        cross_kernel(order_ref, own_ref, partner_ref, *rest[-3:], by_piece)
 
     return pl.pallas_call(
         kernel,
-        out_shape=out,
+        out_shape=jax.ShapeDtypeStruct((ROUNDS, 2, CAP, CAP, HALF), jnp.bfloat16),
         grid_spec=pltpu.PrefetchScalarGridSpec(
             num_scalar_prefetch=1,
             grid=(rounds,),
             in_specs=in_specs,
-            out_specs=pl.BlockSpec((1, 2, CAP, CAP, HALF), lambda r, info: (info[1 + r], 0, 0, 0, 0)),
-            scratch_shapes=[pltpu.VMEM((3 * SEG, CAP, HALF), jnp.float32)],
+            out_specs=pl.BlockSpec((1, 2, CAP, CAP, HALF), lambda r, order: (order[r], 0, 0, 0, 0)),
+            scratch_shapes=[
+                pltpu.VMEM((3 * SEG, CAP, HALF), jnp.float32),
+                pltpu.VMEM((3 * SEG, CAP, HALF), jnp.float32),
+            ],
         ),
-        input_output_aliases={} if fresh else {4: 0},
+        input_output_aliases={} if kept is None else {3: 0},
         compiler_params=pltpu.CompilerParams(vmem_limit_bytes=VMEM),
-        cost_estimate=pl.CostEstimate(flops=rounds * 8 * SEG * CAP * CAP * HALF, bytes_accessed=rounds * 2000000, transcendentals=0),
+        cost_estimate=pl.CostEstimate(
+            flops=rounds * 8 * SEG * CAP * CAP * HALF, bytes_accessed=rounds * 2000000, transcendentals=0
+        ),
         name="cross",
-    )(info, *args)
+    )(order, *args)
+
+
+def flipped(block, axes, sizes, mask):
+    count = int(np.prod(sizes))
+    return lax.ppermute(block, axes, [(i, i ^ mask) for i in range(count)])
 
 
 def shards(traces, counts, taps, masks):
     section = lax.axis_index("section")
     zcore = lax.axis_index("z") * 2 + lax.axis_index("core")
+
+    white = spectra_of(traces, counts, taps)
+    pieces = lax.all_to_all(white.reshape(16, CAP, HALF), ("section", "yh", "x"), 0, 0, tiled=True)
+    gathered = lax.all_gather(pieces, ("z", "core"), axis=0, tiled=False)
+
+    white, _ = lax.optimization_barrier((white, pieces))
+    own = lax.dynamic_index_in_dim(white, section, 0, keepdims=True)
+    away = lax.dynamic_index_in_dim(white, 1 - section, 0, keepdims=True)
+    other = flipped(away, "section", (2,), 1)
+    both = jnp.where(section == 0, jnp.concatenate([own, other]), jnp.concatenate([other, own]))
+    sibling = flipped(both, "core", (2,), 1)
     near = jnp.argmax(masks == 1).astype(jnp.int32)
+    result = cross_of(near[None], both, sibling, None)
+
     far = jnp.arange(ROUNDS - 1, dtype=jnp.int32)
     far = far + (far >= near).astype(jnp.int32)
     far_masks = masks[far]
-
-    white = spectra_of(traces, counts, taps)
-    pieces = lax.all_to_all(white.reshape(16, CAP, HALF), ("section", "yh", "x"), 0, 0, tiled=True)
-    gathered = lax.all_gather(pieces, ("z", "core"), axis=0, tiled=False)
-
-    own = lax.dynamic_index_in_dim(white, section, 0, keepdims=True)
-    away = lax.dynamic_index_in_dim(white, 1 - section, 0, keepdims=True)
-    other = lax.ppermute(away, "section", [(0, 1), (1, 0)])
-    both = jnp.where(section == 0, jnp.stack([own[0], other[0]], 1), jnp.stack([other[0], own[0]], 1))
-    sibling = lax.ppermute(both, "core", [(0, 1), (1, 0)])
-    first = cross_of(jnp.stack([section, near]), white, other, sibling[:, None], None)
-
     place = jnp.stack([jnp.bitwise_xor(zcore, far_masks & 15), far_masks >> 4])
-    picked = pick(gathered.reshape(16, 2, 8, CAP, HALF), place, ROUNDS - 1)
+    gathered, result, place = lax.optimization_barrier((gathered, result, place))
+    picked = pick(gathered.reshape(16, 2, 8, CAP, HALF), place)
+    picked, far, both = lax.optimization_barrier((picked, far, both))
     partners = lax.all_to_all(picked, ("yh", "x"), 0, 0, tiled=True)
-    result = cross_of(jnp.concatenate([section[None], far]), white, other, partners, first)
-    return result[None]
+    return cross_of(far, both, partners, result)[None]
 
 
 def solution(mesh):

time: 211 us -> 142 us (0.67)
  Pallas kernels: 94.5 us -> 33.1 us
  waiting for transfers between devices: 69.9 us -> 35.5 us
  blocking collectives: 16.7 us -> 49.7 us
  starting transfers between devices: 7.99 us -> 3.2 us
    pallas_call x1, Pallas kernels: 61.7 us -> 2.42 us  [pick(): pl.pallas_call(pick_kernel, out_shape=jax.ShapeDtypeStruct((8, rounds, 2,...]
    all_to_all x0 -> x1, blocking collectives: none -> 33.1 us  [shards(): partners = lax.all_to_all(picked, ('yh', 'x'), 0, 0, tiled=True)]
    ppermute x2, waiting for transfers between devices: 25.9 us -> 3.77 us  [flipped(): return lax.ppermute(block, axes, [(i, i ^ mask) for i in range(count)])]
    all_gather x1, waiting for transfers between devices: 44 us -> 31.7 us  [shards(): gathered = lax.all_gather(pieces, ('z', 'core'), axis=0, tiled=False)]
    all_to_all x1 -> x0, starting transfers between devices: 6.44 us -> none  [shards(): partners = lax.all_to_all(picked, ('yh', 'x'), 0, 0, tiled=True)]
    pallas_call x2, Pallas kernels: 24.3 us -> 22.2 us  [cross_of(): pl.pallas_call(kernel, out_shape=jax.ShapeDtypeStruct((ROUNDS, 2, CAP, CA...]
  transfers between devices with their start and end apart: 4 -> 3, of which waited for: 2 -> 3; matrix products, arithmetic and copies ran while one was open for 2% -> 2% of each run, Pallas kernels for 2% -> 3%
where the time goes in v2:
time: 142 us
  blocking collectives  49.7 us (35%)
  waiting for transfers between devices  35.5 us (25%)
  Pallas kernels  33.1 us (23%)
  between operations  14.1 us (10%)
  local copies, waits for them, and re-layouts  3.88 us (3%)
  starting transfers between devices  3.2 us (2%)
  other arithmetic  2.2 us (2%)
    all_to_all x1, blocking collectives, shards(): partners = lax.all_to_all(picked, ('yh', 'x'), 0, 0, tiled=True)  33.1 us
    all_gather x1, waiting for transfers between devices, shards(): gathered = lax.all_gather(pieces, ('z', 'core'), axis=0, tiled=False)  31.7 us
    pallas_call x2, Pallas kernels, cross_of(): pl.pallas_call(kernel, out_shape=jax.ShapeDtypeStruct((ROUNDS, 2, CAP, CA...  22.2 us
    all_to_all x1, blocking collectives, shards(): lax.all_to_all(white.reshape(16, CAP, HALF), ('section', 'yh', 'x'), 0, 0...  16.7 us
    pallas_call x1, Pallas kernels, spectra_of(): pl.pallas_call(spectra_kernel, out_shape=jax.ShapeDtypeStruct((2, 2 * seg...  8.49 us
    ppermute x2, waiting for transfers between devices, flipped(): return lax.ppermute(block, axes, [(i, i ^ mask) for i in range(count)])  3.77 us
    ppermute x2, starting transfers between devices, flipped(): return lax.ppermute(block, axes, [(i, i ^ mask) for i in range(count)])  3.2 us
  transfers between devices with their start and end apart: 3, of which 3 were waited for; matrix products, arithmetic and copies ran while one was open for 2% of the time, Pallas kernels for 3%

profile of v2, /device:TPU:1, one launch (start us, length us, event | category | flops | bytes accessed | tf_op | source)
XLA Modules:
  0.0 141.7 jit_solution(12534596726935019467)
XLA Ops:
  6.5 0.0 copy-start.2
  6.5 0.0 all-gather.3.cloned.1.call-start
  7.2 0.7 copy.10.taps
  7.9 0.0 copy-start
  8.0 1.4 copy-done
  9.4 1.0 copy-done.1
  10.4 8.5 %spectra.1 = bf16[2,8,32,384]{3,2,1,0:T(8,128)(2,1)S(1)} custom-call(s32[1]{0:T(128)S(6)} %copy.12.counts, bf16[128,6144]{1,0:T(8,128)(2,1)S(1)} %bitcast.14, f32[64,1]{1,0:T(8,128)S(1)} %copy.10.taps, f32[2,64,1024]{2,1,0:T(8,128)S(1)} %copy-done.1, bf16[4,1536,512]{2,1,0:T(8,128)(2,1)} %constant.43.clone.table), custom_call_target="tpu_custom_call" | custom-call | tf_op jit(solution)/shard_map/spectra/pallas_call | solution.py:134
  18.9 16.7 %all_to_all.10 = bf16[16,32,384]{2,1,0:T(8,128)(2,1)} all-to-all(bf16[16,32,384]{2,1,0:T(8,128)(2,1)S(1)} %bitcast.13), channel_id=1, replica_groups=mesh['section'=2,'yh'=2,'x'=4,'z'=8,'core'=2] {'section','yh','x'}, dimensions={0} | all-to-all | bytes 786432 | tf_op jit(solution)/shard_map/all_to_all | solution.py:284
  35.5 0.0 all-gather.3.cloned.1.call-update
  35.6 0.0 copy-done.2
  35.6 0.7 compare_reduce_fusion
  36.4 0.1 collective-permute-start
  36.5 0.7 fusion.2
  37.2 0.6 gather_fusion
  37.8 3.1 %collective-permute-done = bf16[1,8,32,384]{3,2,1,0:T(8,128)(2,1)S(1)} collective-permute-done((bf16[1,8,32,384]{3,2,1,0:T(8,128)(2,1)S(1)}, bf16[1,8,32,384]{3,2,1,0:T(8,128)(2,1)S(1)}, u32[]{:S(2)}, u32[]{:S(2)}) %collective-permute-start) | collective-permute-done | bytes 196640 | tf_op jit(solution)/shard_map/ppermute | solution.py:276
  41.0 0.1 maximum_select_fusion.own_ref
  41.0 3.1 %collective-permute-start.1 = (bf16[2,8,32,384]{3,2,1,0:T(8,128)(2,1)S(1)}, bf16[2,8,32,384]{3,2,1,0:T(8,128)(2,1)S(1)}, u32[]{:S(2)}, u32[]{:S(2)}) collective-permute-start(bf16[2,8,32,384]{3,2,1,0:T(8,128)(2,1)S(1)} %maximum_select_fusion.own_ref), channel_id=1, source_target_pairs={{0,1},{1,0},{2,3},{3,2},{4,5},{5,4},{6,7},{7,6},{8,9},{9,8},{10,11... | collective-permute-start | bytes 1179656 | tf_op jit(solution)/shard_map/ppermute | solution.py:276
  44.2 0.7 fusion.1.order_ref
  44.9 0.6 collective-permute-done.1.partner_ref
  45.5 5.0 %cross.2.rest_0_ = bf16[6,2,32,32,384]{4,3,2,1,0:T(8,128)(2,1)} custom-call(s32[1]{0:T(128)} %bitcast.4.order_ref, bf16[2,8,32,384]{3,2,1,0:T(8,128)(2,1)S(1)} %maximum_select_fusion.own_ref, bf16[2,8,32,384]{3,2,1,0:T(8,128)(2,1)S(1)} %collective-permute-done.1.partner_ref), custom_call_target="tpu_custom_call" | custom-call | flops 25165824 | bytes 2000000 | tf_op jit(solution)/shard_map/cross/pallas_call | solution.py:252
  50.5 31.7 %all-gather.3.cloned.1.call-done = bf16[256,32,384]{2,1,0:T(8,128)(2,1)} async-done(((bf16[16,32,384]{2,1,0:T(8,128)(2,1)}), bf16[256,32,384]{2,1,0:T(8,128)(2,1)}) %all-gather.3.cloned.1.call-update) | async-done | bytes 6291472 | tf_op jit(solution)/shard_map/all_gather | solution.py:285
  82.2 2.4 %pick.1 = bf16[8,5,2,32,384]{4,3,2,1,0:T(8,128)(2,1)S(1)} custom-call(s32[2,5]{1,0:T(2,128)S(1)} %pad_add_fusion.place, bf16[16,2,8,32,384]{4,3,2,1,0:T(8,128)(2,1)} %bitcast.15), custom_call_target="tpu_custom_call" | custom-call | tf_op jit(solution)/shard_map/pick/pallas_call | solution.py:175
  84.6 33.1 %all_to_all.11.partner_ref = bf16[8,5,2,32,384]{4,3,2,1,0:T(8,128)(2,1)S(1)} all-to-all(bf16[8,5,2,32,384]{4,3,2,1,0:T(8,128)(2,1)S(1)} %pick.1), channel_id=1, replica_groups=mesh['section'=2,'yh'=2,'x'=4,'z'=8,'core'=2] {'yh','x'}, dimensions={0} | all-to-all | bytes 3932160 | tf_op jit(solution)/shard_map/all_to_all | solution.py:303
  117.7 17.2 %cross.3 = bf16[6,2,32,32,384]{4,3,2,1,0:T(8,128)(2,1)} custom-call(s32[5]{0:T(128)S(1)} %fusion.1.order_ref, bf16[2,8,32,384]{3,2,1,0:T(8,128)(2,1)S(1)} %maximum_select_fusion.own_ref, bf16[8,5,2,32,384]{4,3,2,1,0:T(8,128)(2,1)S(1)} %all_to_all.11.partner_ref, bf16[6,2,32,32,384]{4,3,2,1,0:T(8,128)(2,1)} %cross.2.rest_0_), custom_call_target="tpu_custom_call", output_to_operand_aliasing={{}: (3, {})} | custom-call | flops 125829120 | bytes 10000000 | tf_op jit(solution)/shard_map/cross/pallas_call | solution.py:252
  (5 shorter events, 0.1 us)
Async XLA Ops:
  6.5 29.1 %copy-start.2 = (s32[6]{0:T(128)S(1)}, s32[6]{0:T(128)}, u32[]{:S(2)}) copy-start(s32[6]{0:T(128)} %param.9) | copy-start | bytes 76
  6.5 75.6 %all-gather.3.cloned.1.call-start = ((), (), s32[]{:S(2)}) async-start(), calls=%async_computation.2 | async-start | bytes 6684672 | tf_op jit(solution)/shard_map/all_gather | solution.py:285
  7.9 1.4 copy-start
  9.4 1.0 copy-start.1
  36.4 4.6 %collective-permute-start = (bf16[1,8,32,384]{3,2,1,0:T(8,128)(2,1)S(1)}, bf16[1,8,32,384]{3,2,1,0:T(8,128)(2,1)S(1)}, u32[]{:S(2)}, u32[]{:S(2)}) collective-permute-start(bf16[1,8,32,384]{3,2,1,0:T(8,128)(2,1)S(1)} %get-tuple-element.22), channel_id=1, source_target_pairs={{0,128},{128,0},{1,129},{129,1},{2,130},{130,2},{3,131},{131,3},{4... | collective-permute-start | bytes 589832 | tf_op jit(solution)/shard_map/ppermute | solution.py:276
  41.0 4.5 %collective-permute-start.1 = (bf16[2,8,32,384]{3,2,1,0:T(8,128)(2,1)S(1)}, bf16[2,8,32,384]{3,2,1,0:T(8,128)(2,1)S(1)}, u32[]{:S(2)}, u32[]{:S(2)}) collective-permute-start(bf16[2,8,32,384]{3,2,1,0:T(8,128)(2,1)S(1)} %maximum_select_fusion.own_ref), channel_id=1, source_target_pairs={{0,1},{1,0},{2,3},{3,2},{4,5},{5,4},{6,7},{7,6},{8,9},{9,8},{10,11... | collective-permute-start | bytes 1179656 | tf_op jit(solution)/shard_map/ppermute | solution.py:276
Sparse Core Ops, SparseCore 0:
  35.7 46.4 all-gather.2

commit v3 on v0

v3 whole, which is shorter than its diff:
```python
import jax
import jax.numpy as jnp
import numpy as np
from jax import lax
from jax.experimental import pallas as pl
from jax.experimental.pallas import tpu as pltpu
from jax.sharding import Mesh
from jax.sharding import PartitionSpec as P

F = 768
L = 6144
K = 64
CAP = 32
SEG = 8
ROUNDS = 6
LOCAL = 4
HALF = F // 2
Q = L // 4
G = 256
CLASSES = (0, 2, 1, 3)
VMEM = 48 * 1024 * 1024


def angles(steps, freqs):
    return (np.outer(steps, freqs) % L) * (2.0 * np.pi / L)


def class_bins(residue):
    return 4 * np.arange(F // 4) + residue


def dft_tables():
    out = np.zeros((4, Q, 2 * G), np.float32)
    for at, residue in enumerate(CLASSES):
        angle = angles(np.arange(Q), class_bins(residue))
        out[at, :, : F // 4] = np.cos(angle)
        out[at, :, G : G + F // 4] = np.sin(angle)
    return out.astype(jnp.bfloat16)


def tap_tables():
    out = np.zeros((2, K, 4 * G), np.float32)
    for at, residue in enumerate(CLASSES):
        angle = angles(np.arange(K), class_bins(residue))
        out[0, :, at * G : at * G + F // 4] = np.cos(angle)
        out[1, :, at * G : at * G + F // 4] = np.sin(angle)
    return out


def spectra_kernel(counts, taps, traces, tap_source, table_source, out, x, tap_table, table, spread, y, re, im, sems):
    segs, rows = traces.shape[0], x.shape[0]
    loads = [pltpu.make_async_copy(traces.at[s], x.at[pl.ds(s * CAP, CAP)], sems.at[s]) for s in range(segs)]
    tables = [pltpu.make_async_copy(table_source.at[k], table.at[k], sems.at[segs + k]) for k in range(4)]
    tap_load = pltpu.make_async_copy(tap_source, tap_table, sems.at[segs + 4])
    for copy in loads + tables + [tap_load]:
        copy.start()

    src = lax.broadcasted_iota(jnp.int32, (4 * G, F), 0)
    dst = lax.broadcasted_iota(jnp.int32, (4 * G, F), 1)
    residue = dst & 3
    place = jnp.where(residue == 1, 2, jnp.where(residue == 2, 1, residue))
    spread[...] = jnp.where(src == place * G + (dst >> 2), 1.0, 0.0).astype(jnp.bfloat16)

    def tile(t, carry):
        at = pl.ds(pl.multiple_of(t * 16, 16), 16)
        total = jnp.zeros((16, 128), jnp.float32)
        for c in range(L // 128):
            v = x[at, c * 128 : (c + 1) * 128].astype(jnp.float32)
            total = total + v * v
        mean = jnp.sum(total, axis=1, keepdims=True) * (1.0 / L)
        top = jnp.broadcast_to(2.5 * jnp.sqrt(mean + 1e-6), (16, 128))

        def clipped(start):
            v = x[at, start : start + 128].astype(jnp.float32)
            v = jnp.minimum(jnp.maximum(v, -top), top)
            return v.astype(jnp.bfloat16).astype(jnp.float32)

        for c in range(Q // 128):
            x0, x1, x2, x3 = [clipped(q * Q + c * 128) for q in range(4)]
            s02, d02, s13, d13 = x0 + x2, x0 - x2, x1 + x3, x1 - x3
            for n, v in enumerate((s02 + s13, s02 - s13, d02, -d13)):
                hi = v.astype(jnp.bfloat16)
                lo = (v - hi.astype(jnp.float32)).astype(jnp.bfloat16)
                y[2 * n, at, c * 128 : (c + 1) * 128] = hi
                y[2 * n + 1, at, c * 128 : (c + 1) * 128] = lo
        return carry

    for s in range(segs):
        loads[s].wait()
        lax.fori_loop(s * CAP // 16, (s + 1) * CAP // 16, tile, 0)

    def product(n, k):
        a = jnp.dot(y[2 * n], table[k], preferred_element_type=jnp.float32)
        b = jnp.dot(y[2 * n + 1], table[k], preferred_element_type=jnp.float32)
        return a + b

    for k in range(4):
        tables[k].wait()
        at = slice(k * G, (k + 1) * G)
        if k < 2:
            p = product(k, k)
            re[:, at] = p[:, :G]
            im[:, at] = -p[:, G:]
        else:
            p, q = product(2, k), product(3, k)
            if k == 2:
                re[:, at] = p[:, :G] + q[:, G:]
                im[:, at] = q[:, :G] - p[:, G:]
            else:
                re[:, at] = p[:, :G] - q[:, G:]
                im[:, at] = -(p[:, G:] + q[:, :G])

    tap_load.wait()
    square = (K, K)
    same = lax.broadcasted_iota(jnp.int32, square, 0) == lax.broadcasted_iota(jnp.int32, square, 1)
    column = jnp.sum(jnp.where(same, jnp.broadcast_to(taps[...], square), 0.0), axis=1, keepdims=True)
    hr = jnp.sum(tap_table[0] * column, axis=0, keepdims=True)
    hi = -jnp.sum(tap_table[1] * column, axis=0, keepdims=True)
    fr = re[...] * hr - im[...] * hi
    fi = re[...] * hi + im[...] * hr
    power = jnp.sum(fr * fr + fi * fi, axis=1, keepdims=True) * (1.0 / F) + 1e-6
    slot = lax.broadcasted_iota(jnp.int32, (rows, 1), 0) % CAP
    live = jnp.where(slot < counts[0], 1.0, 0.0)
    scale = live / jnp.sqrt(power)
    white = jnp.concatenate([fr * scale, fi * scale], axis=0).astype(jnp.bfloat16)
    ordered = jnp.dot(white, spread[...], preferred_element_type=jnp.float32)
    for half in range(2):
        for seg in range(LOCAL):
            for part in range(2):
                start, piece = part * rows + seg * CAP, seg * 2 + part
                for fg in range(HALF // 128):
                    at = half * HALF + fg * 128
                    block = pltpu.roll(ordered[start : start + CAP, at : at + 128], 16 * piece, 1)
                    out[half, piece, :, fg * 128 : (fg + 1) * 128] = block.astype(jnp.bfloat16)


def spectra_of(traces, counts, taps):
    segs, cap, length = traces.shape
    rows = segs * cap
    far_away = pl.BlockSpec(memory_space=pl.ANY)
    return pl.pallas_call(
        spectra_kernel,
        out_shape=jax.ShapeDtypeStruct((2, 2 * segs, cap, HALF), jnp.bfloat16),
        in_specs=[
            pl.BlockSpec(memory_space=pltpu.SMEM),
            pl.BlockSpec(memory_space=pltpu.VMEM),
            far_away,
            far_away,
            far_away,
        ],
        out_specs=pl.BlockSpec(memory_space=pltpu.VMEM),
        scratch_shapes=[
            pltpu.VMEM((rows, length), jnp.bfloat16),
            pltpu.VMEM((2, K, 4 * G), jnp.float32),
            pltpu.VMEM((4, Q, 2 * G), jnp.bfloat16),
            pltpu.VMEM((4 * G, F), jnp.bfloat16),
            pltpu.VMEM((8, rows, Q), jnp.bfloat16),
            pltpu.VMEM((rows, 4 * G), jnp.float32),
            pltpu.VMEM((rows, 4 * G), jnp.float32),
            pltpu.SemaphoreType.DMA((segs + 5,)),
        ],
        compiler_params=pltpu.CompilerParams(vmem_limit_bytes=62 * 1024 * 1024),
        name="spectra",
    )(counts, taps.reshape(1, K), traces, tap_tables(), dft_tables())


def pick_kernel(place, *refs):
    slabs, out = (refs[:8], refs[8:16]), refs[16]
    for r in range(out.shape[1]):
        for k in range(8):

            @pl.when(place[0, r] == k)
            def _(r=r, k=k):
                for d in range(out.shape[0]):
                    src = jnp.bitwise_xor(place[1, r], d)
                    for h in range(2):
                        out[d, r, h] = slabs[h][k][src]


def pick(first, second, place):
    rounds = place.shape[1]
    inside = pl.BlockSpec(memory_space=pltpu.VMEM)
    return pl.pallas_call(
        pick_kernel,
        out_shape=jax.ShapeDtypeStruct((16, rounds, 2, CAP // 2, HALF), jnp.bfloat16),
        in_specs=[pl.BlockSpec(memory_space=pltpu.SMEM)] + [inside] * 16,
        out_specs=inside,
        compiler_params=pltpu.CompilerParams(vmem_limit_bytes=VMEM),
        name="pick",
    )(place, *first, *second)


def place_bits(shape, dtype):
    lane = lax.broadcasted_iota(dtype, shape, 1)
    return [(lane & (16 << b)) != 0 for b in range(3)]


def swirl(tiles, bits):
    held = [tiles[-n % 8] for n in range(8)]
    for b in range(3):
        held = [jnp.where(bits[b], held[(n - (1 << b)) % 8], held[n]) for n in range(8)]
    return held


def weights_kernel(own, out):
    bits = place_bits((8, 128), jnp.int32)
    row = lax.broadcasted_iota(jnp.int32, (16, 128), 0)
    diagonal = (lax.broadcasted_iota(jnp.int32, (16, 128), 1) & 15) == row
    for h in range(2):
        for piece in range(8):
            block = own[h, piece].astype(jnp.float32) * (1.0 / SEG)
            for tile in range(2):
                v = block[tile * 8 : (tile + 1) * 8]
                v = pltpu.roll(pltpu.roll(v, -16 * piece % 128, 1), 0, 1, stride=16, stride_axis=0)
                for b in range(3):
                    v = jnp.where(bits[b], pltpu.roll(v, 8 - (1 << b), 0), v)
                for g in range(8):
                    line = jnp.broadcast_to(v[-g % 8][None], (16, 128))
                    at = h * 128 + (g + piece) % 8 * 16
                    out[0, 0, g, at : at + 16, tile * 128 : (tile + 1) * 128] = jnp.where(
                        diagonal, line, 0.0
                    ).astype(jnp.bfloat16)


def weights_of(own):
    return pl.pallas_call(
        weights_kernel,
        out_shape=jax.ShapeDtypeStruct((HALF // 128, CAP // 16, 8, 256, 256), jnp.bfloat16),
        grid=(HALF // 128, CAP // 16),
        in_specs=[pl.BlockSpec((2, 8, 16, 128), lambda fg, it: (0, 0, it, fg))],
        out_specs=pl.BlockSpec((1, 1, 8, 256, 256), lambda fg, it: (fg, it, 0, 0, 0)),
        compiler_params=pltpu.CompilerParams(vmem_limit_bytes=VMEM),
        name="weights",
    )(own)


def cross_kernel(order, partner, sibling, weights, out, left, held, sums, done, load_sems, store_sems):
    bits = place_bits((16, 128), jnp.int16)
    groups, halves = HALF // 128, CAP // 16
    loads = [
        [pltpu.make_async_copy(weights.at[fg, it], held.at[fg, it], load_sems.at[fg * halves + it]) for it in range(halves)]
        for fg in range(groups)
    ]
    for it in range(halves):
        for fg in range(groups):
            loads[fg][it].start()

    def arrange(r, block):
        for fg in range(groups):
            for h in range(2):
                for jh in range(2):
                    x = [block(p, h, jh, slice(fg * 128, (fg + 1) * 128)) for p in range(8)]
                    turned = []
                    for p in range(8):
                        other = x[p ^ 1]
                        turned.append(pltpu.roll(other, 16, 1) if p % 2 else -pltpu.roll(other, 112, 1))
                    for a, tiles in enumerate((x, turned)):
                        at = pl.ds(pl.multiple_of((a * ROUNDS + r) * CAP + jh * 16, 16), 16)
                        for g, z in enumerate(swirl(tiles, bits)):
                            left[fg, g, at, h * 128 : (h + 1) * 128] = z

    def arrange_far(r, carry):
        arrange(r, lambda p, h, jh, lanes: partner[2 * p + jh, r, h, :, lanes])
        return carry

    lax.fori_loop(0, ROUNDS - 1, arrange_far, 0)
    arrange(ROUNDS - 1, lambda p, h, jh, lanes: sibling[h, p, jh * 16 : (jh + 1) * 16, lanes])

    def store(it, r):
        part = pl.ds(it * 16, 16)
        return pltpu.make_async_copy(done.at[r, :, part], out.at[order[r], :, part], store_sems.at[it * ROUNDS + r])

    for it in range(halves):
        for fg in range(groups):
            loads[fg][it].wait()
            for g in range(8):
                total = jnp.dot(left[fg, g], held[fg, it, g], preferred_element_type=jnp.float32)
                sums[fg, g] = total.astype(jnp.bfloat16)

        def finish(r, carry, it=it):
            for fg in range(groups):
                for a in range(2):
                    for jh in range(2):
                        rows = pl.ds(pl.multiple_of((a * ROUNDS + r) * CAP + jh * 16, 16), 16)
                        for tile in range(2):
                            cols = slice(tile * 128, (tile + 1) * 128)
                            turned = swirl([sums[fg, g, rows, cols] for g in range(8)], bits)
                            for i in range(8):
                                done[r, a, it * 16 + tile * 8 + i, jh * 16 : (jh + 1) * 16, fg * 128 : (fg + 1) * 128] = (
                                    pltpu.roll(turned[i], -16 * i % 128, 1)
                                )
            store(it, r).start()
            return carry

        lax.fori_loop(0, ROUNDS, finish, 0)

    for it in range(halves):
        for r in range(ROUNDS):
            store(it, r).wait()


def cross_of(order, partner, sibling, weights):
    rows = 2 * ROUNDS * CAP
    groups, halves = HALF // 128, CAP // 16
    shape = (ROUNDS, 2, CAP, CAP, HALF)
    return pl.pallas_call(
        cross_kernel,
        out_shape=jax.ShapeDtypeStruct(shape, jnp.bfloat16),
        in_specs=[
            pl.BlockSpec(memory_space=pltpu.SMEM),
            pl.BlockSpec(memory_space=pltpu.VMEM),
            pl.BlockSpec(memory_space=pltpu.VMEM),
            pl.BlockSpec(memory_space=pl.ANY),
        ],
        out_specs=pl.BlockSpec(memory_space=pl.ANY),
        scratch_shapes=[
            pltpu.VMEM((groups, 8, rows, 256), jnp.bfloat16),
            pltpu.VMEM((groups, halves, 8, 256, 256), jnp.bfloat16),
            pltpu.VMEM((groups, 8, rows, 256), jnp.bfloat16),
            pltpu.VMEM(shape, jnp.bfloat16),
            pltpu.SemaphoreType.DMA((groups * halves,)),
            pltpu.SemaphoreType.DMA((halves * ROUNDS,)),
        ],
        compiler_params=pltpu.CompilerParams(vmem_limit_bytes=VMEM),
        name="cross",
    )(order, partner, sibling, weights)


def flipped(block, axis):
    return lax.ppermute(block, axis, [(0, 1), (1, 0)])


def around(block, last):
    ring = lax.axis_size("z")

    def shift(held, way):
        return lax.ppermute(held, "z", [(i, (i + way) % ring) for i in range(ring)])

    slabs = [block] * ring
    for step in range(1, ring // 2):
        slabs[-step] = shift(slabs[1 - step], 1)
        slabs[step] = shift(slabs[step - 1], -1)
    slabs[ring // 2] = shift(slabs[(ring // 2 + last) % ring], last)
    return slabs


def shards(traces, counts, taps, masks):
    section = lax.axis_index("section")
    z = lax.axis_index("z")

    white = spectra_of(traces, counts, taps)
    pieces = lax.all_to_all(
        white.reshape(32, CAP // 2, HALF), ("section", "yh", "x", "core"), 0, 0, tiled=True
    )
    first, second = around(pieces[:16], 1), around(pieces[16:], -1)

    white, _ = lax.optimization_barrier((white, pieces))
    own = lax.dynamic_index_in_dim(white, section, 0, keepdims=True)
    away = lax.dynamic_index_in_dim(white, 1 - section, 0, keepdims=True)
    other = flipped(away, "section")
    both = jnp.where(section == 0, jnp.concatenate([own, other]), jnp.concatenate([other, own]))
    sibling = flipped(both, "core")
    weights = weights_of(both)
    near = jnp.argmax(masks == 1).astype(jnp.int32)
    far = jnp.arange(ROUNDS - 1, dtype=jnp.int32)
    far = far + (far >= near).astype(jnp.int32)
    far_masks = masks[far]
    order = jnp.concatenate([far, near[None]])
    apart = jnp.bitwise_xor(z, far_masks >> 1 & 7) - z & 7
    place = jnp.stack([apart, far_masks >> 4 << 1 | far_masks & 1])

    first, second, place, order, sibling, weights = lax.optimization_barrier(
        (first, second, place, order, sibling, weights)
    )
    picked = pick(first, second, place).reshape(16, -1, HALF)
    partners = lax.all_to_all(picked, ("yh", "x", "core"), 0, 0, tiled=True)
    partners = partners.reshape(16, ROUNDS - 1, 2, CAP // 2, HALF)
    return cross_of(order, partners, sibling, weights)[None]


def solution(mesh):
    fine = Mesh(mesh.devices.reshape(2, 2, 4, 8, 2), ("section", "yh", "x", "z", "core"))
    blk = ("yh", "x", "z", "core")
    return jax.shard_map(
        shards,
        mesh=fine,
        in_specs=(P("section", blk, None), P(blk), P(), P()),
        out_specs=P(blk, None, None, None, None, "section"),
        check_vma=False,
    )
```

time: 633 us -> 111 us (0.18)
  the two profiles are of different devices: /device:TPU:224 before, /device:TPU:1 now
where the time goes in v3:
time: 111 us
  blocking collectives  33.9 us (31%)
  starting transfers between devices  31 us (28%)
  Pallas kernels  24.7 us (22%)
  waiting for transfers between devices  15.6 us (14%)
  other arithmetic  2.78 us (3%)
  local copies, waits for them, and re-layouts  1.75 us (2%)
    all_to_all x1, blocking collectives, shards(): partners = lax.all_to_all(picked, ('yh', 'x', 'core'), 0, 0, tiled=True)  33.9 us
    ppermute x14, starting transfers between devices, shift(): return lax.ppermute(held, 'z', [(i, (i + way) % ring) for i in range(ring)])  20.1 us
    pallas_call x1, Pallas kernels, spectra_of(): pl.pallas_call(spectra_kernel, out_shape=jax.ShapeDtypeStruct((2, 2 * seg...  9.73 us
    pallas_call x1, Pallas kernels, cross_of(): pl.pallas_call(cross_kernel, out_shape=jax.ShapeDtypeStruct(shape, jnp.bf...  9.42 us
    all_to_all x1, waiting for transfers between devices, shards(): lax.all_to_all(white.reshape(32, CAP // 2, HALF), ('section', 'yh', 'x',...  9.05 us
    all_to_all x1, starting transfers between devices, shards(): lax.all_to_all(white.reshape(32, CAP // 2, HALF), ('section', 'yh', 'x',...  8.6 us
    ppermute x14, waiting for transfers between devices, shift(): return lax.ppermute(held, 'z', [(i, (i + way) % ring) for i in range(ring)])  6.54 us
    pallas_call x1, Pallas kernels, weights_of(): pl.pallas_call(weights_kernel, out_shape=jax.ShapeDtypeStruct((HALF // 12...  4.47 us
  transfers between devices with their start and end apart: 17, of which 5 were waited for; matrix products, arithmetic and copies ran while one was open for 4% of the time, Pallas kernels for 4%

profile of v3, /device:TPU:1, one launch (start us, length us, event | category | flops | bytes accessed | tf_op | source)
XLA Modules:
  0.0 110.7 jit_solution(2509298815370858141)
XLA Ops:
  0.7 9.7 %spectra.1 = bf16[2,8,32,384]{3,2,1,0:T(8,128)(2,1)} custom-call(s32[1]{0:T(128)S(6)} %copy.7.counts, f32[1,64]{1,0:T(1,128)} %bitcast.15, bf16[4,32,6144]{2,1,0:T(8,128)(2,1)} %traces.1, f32[2,64,1024]{2,1,0:T(8,128)} %constant.40.clone.tap_source, bf16[4,1536,512]{2,1,0:T(8,128)(2,1)} %constant.41.clone.table_source), custom_call_target="tpu_custom_call" | custom-call | tf_op jit(solution)/shard_map/spectra/pallas_call | solution.py:141
  10.4 8.6 %all-to-all-start = ((bf16[32,16,384]{2,1,0:T(8,128)(2,1)}), bf16[32,16,384]{2,1,0:T(8,128)(2,1)S(1)}, u32[]{:S(2)}, u32[]{:S(2)}) async-start(bf16[32,16,384]{2,1,0:T(8,128)(2,1)} %bitcast.14), calls=%async_computation | async-start | bytes 786432 | tf_op jit(solution)/shard_map/all_to_all | solution.py:352
  19.0 0.7 compare_reduce_fusion
  19.7 0.6 fusion.2
  20.4 9.1 %all-to-all-done = bf16[32,16,384]{2,1,0:T(8,128)(2,1)S(1)} async-done(((bf16[32,16,384]{2,1,0:T(8,128)(2,1)}), bf16[32,16,384]{2,1,0:T(8,128)(2,1)S(1)}, u32[]{:S(2)}, u32[]{:S(2)}) %all-to-all-start) | async-done | bytes 393248 | tf_op jit(solution)/shard_map/all_to_all | solution.py:352
  29.5 5.7 %collective-permute-start.7 = (bf16[16,16,384]{2,1,0:T(8,128)(2,1)S(1)}, bf16[16,16,384]{2,1,0:T(8,128)(2,1)S(1)}, u32[]{:S(2)}, u32[]{:S(2)}) collective-permute-start(bf16[16,16,384]{2,1,0:T(8,128)(2,1)S(1)} %get-tuple-element.39.refs_8_), channel_id=1, source_target_pairs={{0,14},{2,0},{4,2},{6,4},{8,6},{10,8},{12,10},{14,12},{1,15},{3,1}... | collective-permute-start | bytes 589832 | tf_op jit(solution)/shard_map/ppermute | solution.py:337
  35.1 1.1 constant_dynamic-slice_fusion.1
  36.6 0.6 gather_fusion
  37.4 2.7 %collective-permute-start = (bf16[16,16,384]{2,1,0:T(8,128)(2,1)S(1)}, bf16[16,16,384]{2,1,0:T(8,128)(2,1)S(1)}, u32[]{:S(2)}, u32[]{:S(2)}) collective-permute-start(bf16[16,16,384]{2,1,0:T(8,128)(2,1)S(1)} %get-tuple-element.31.refs_0_), channel_id=1, source_target_pairs={{0,14},{2,0},{4,2},{6,4},{8,6},{10,8},{12,10},{14,12},{1,15},{3,1}... | collective-permute-start | bytes 589832 | tf_op jit(solution)/shard_map/ppermute | solution.py:337
  40.1 2.6 %collective-permute-start.8 = (bf16[16,16,384]{2,1,0:T(8,128)(2,1)S(1)}, bf16[16,16,384]{2,1,0:T(8,128)(2,1)S(1)}, u32[]{:S(2)}, u32[]{:S(2)}) collective-permute-start(bf16[16,16,384]{2,1,0:T(8,128)(2,1)S(1)} %collective-permute-done.7.refs_9_), channel_id=1, source_target_pairs={{0,14},{2,0},{4,2},{6,4},{8,6},{10,8},{12,10},{14,12},{1,15},{3,1}... | collective-permute-start | bytes 589832 | tf_op jit(solution)/shard_map/ppermute | solution.py:337
  42.7 0.6 fusion.1
  43.5 1.9 %collective-permute-start.15 = (bf16[2,8,32,384]{3,2,1,0:T(8,128)(2,1)S(1)}, bf16[2,8,32,384]{3,2,1,0:T(8,128)(2,1)S(1)}, u32[]{:S(2)}, u32[]{:S(2)}) collective-permute-start(bf16[2,8,32,384]{3,2,1,0:T(8,128)(2,1)S(1)} %maximum_select_fusion.own), channel_id=1, source_target_pairs={{0,1},{1,0},{2,3},{3,2},{4,5},{5,4},{6,7},{7,6},{8,9},{9,8},{10,11... | collective-permute-start | bytes 1179656 | tf_op jit(solution)/shard_map/ppermute | solution.py:330
  45.4 1.3 %collective-permute-done.11.refs_15_ = bf16[16,16,384]{2,1,0:T(8,128)(2,1)S(1)} collective-permute-done((bf16[16,16,384]{2,1,0:T(8,128)(2,1)S(1)}, bf16[16,16,384]{2,1,0:T(8,128)(2,1)S(1)}, u32[]{:S(2)}, u32[]{:S(2)}) %collective-permute-start.11) | collective-permute-done | bytes 196640 | tf_op jit(solution)/shard_map/ppermute | solution.py:337
  46.6 2.7 %collective-permute-start.1 = (bf16[16,16,384]{2,1,0:T(8,128)(2,1)S(1)}, bf16[16,16,384]{2,1,0:T(8,128)(2,1)S(1)}, u32[]{:S(2)}, u32[]{:S(2)}) collective-permute-start(bf16[16,16,384]{2,1,0:T(8,128)(2,1)S(1)} %collective-permute-done.refs_1_), channel_id=1, source_target_pairs={{0,14},{2,0},{4,2},{6,4},{8,6},{10,8},{12,10},{14,12},{1,15},{3,1}... | collective-permute-start | bytes 589832 | tf_op jit(solution)/shard_map/ppermute | solution.py:337
  49.3 2.1 %collective-permute-start.9 = (bf16[16,16,384]{2,1,0:T(8,128)(2,1)S(1)}, bf16[16,16,384]{2,1,0:T(8,128)(2,1)S(1)}, u32[]{:S(2)}, u32[]{:S(2)}) collective-permute-start(bf16[16,16,384]{2,1,0:T(8,128)(2,1)S(1)} %collective-permute-done.8.refs_10_), channel_id=1, source_target_pairs={{0,14},{2,0},{4,2},{6,4},{8,6},{10,8},{12,10},{14,12},{1,15},{3,1}... | collective-permute-start | bytes 589832 | tf_op jit(solution)/shard_map/ppermute | solution.py:337
  51.4 3.1 %collective-permute-done.12.refs_14_ = bf16[16,16,384]{2,1,0:T(8,128)(2,1)S(1)} collective-permute-done((bf16[16,16,384]{2,1,0:T(8,128)(2,1)S(1)}, bf16[16,16,384]{2,1,0:T(8,128)(2,1)S(1)}, u32[]{:S(2)}, u32[]{:S(2)}) %collective-permute-start.12) | collective-permute-done | bytes 196640 | tf_op jit(solution)/shard_map/ppermute | solution.py:337
  54.5 2.7 %collective-permute-start.2 = (bf16[16,16,384]{2,1,0:T(8,128)(2,1)S(1)}, bf16[16,16,384]{2,1,0:T(8,128)(2,1)S(1)}, u32[]{:S(2)}, u32[]{:S(2)}) collective-permute-start(bf16[16,16,384]{2,1,0:T(8,128)(2,1)S(1)} %collective-permute-done.1.refs_2_), channel_id=1, source_target_pairs={{0,14},{2,0},{4,2},{6,4},{8,6},{10,8},{12,10},{14,12},{1,15},{3,1}... | collective-permute-start | bytes 589832 | tf_op jit(solution)/shard_map/ppermute | solution.py:337
  57.2 1.6 %collective-permute-start.10 = (bf16[16,16,384]{2,1,0:T(8,128)(2,1)S(1)}, bf16[16,16,384]{2,1,0:T(8,128)(2,1)S(1)}, u32[]{:S(2)}, u32[]{:S(2)}) collective-permute-start(bf16[16,16,384]{2,1,0:T(8,128)(2,1)S(1)} %collective-permute-done.9.refs_11_), channel_id=1, source_target_pairs={{0,14},{2,0},{4,2},{6,4},{8,6},{10,8},{12,10},{14,12},{1,15},{3,1}... | collective-permute-start | bytes 589832 | tf_op jit(solution)/shard_map/ppermute | solution.py:337
  58.8 0.7 pad_add_fusion.1.order
  59.5 4.5 %weights.1 = bf16[3,2,8,256,256]{4,3,2,1,0:T(8,128)(2,1)} custom-call(bf16[2,8,32,384]{3,2,1,0:T(8,128)(2,1)S(1)} %maximum_select_fusion.own), custom_call_target="tpu_custom_call" | custom-call | tf_op jit(solution)/shard_map/weights/pallas_call | solution.py:226
  64.6 1.5 %collective-permute-done.6.refs_4_ = bf16[16,16,384]{2,1,0:T(8,128)(2,1)S(1)} collective-permute-done((bf16[16,16,384]{2,1,0:T(8,128)(2,1)S(1)}, bf16[16,16,384]{2,1,0:T(8,128)(2,1)S(1)}, u32[]{:S(2)}, u32[]{:S(2)}) %collective-permute-start.6) | collective-permute-done | bytes 196640 | tf_op jit(solution)/shard_map/ppermute | solution.py:337
  66.1 1.1 pick.1
  67.2 33.9 %all_to_all.10 = bf16[16,160,384]{2,1,0:T(8,128)(2,1)S(1)} all-to-all(bf16[16,160,384]{2,1,0:T(8,128)(2,1)S(1)} %bitcast.12), channel_id=1, replica_groups=mesh['section'=2,'yh'=2,'x'=4,'z'=8,'core'=2] {'yh','x','core'}, dimensions={0} | all-to-all | bytes 3932160 | tf_op jit(solution)/shard_map/all_to_all | solution.py:376
  101.1 9.4 %cross.1 = bf16[6,2,32,32,384]{4,3,2,1,0:T(8,128)(2,1)} custom-call(s32[6]{0:T(128)S(1)} %pad_add_fusion.1.order, bf16[16,5,2,16,384]{4,3,2,1,0:T(8,128)(2,1)S(1)} %bitcast.13, bf16[2,8,32,384]{3,2,1,0:T(8,128)(2,1)S(1)} %collective-permute-done.15.sibling, bf16[3,2,8,256,256]{4,3,2,1,0:T(8,128)(2,1)} %weights.1), custom_call_target="tpu_custom_call" | custom-call | tf_op jit(solution)/shard_map/cross/pallas_call | solution.py:306
  (28 shorter events, 1.3 us)
Async XLA Ops:
  0.0 19.0 %copy-start = (s32[6]{0:T(128)S(1)}, s32[6]{0:T(128)}, u32[]{:S(2)}) copy-start(s32[6]{0:T(128)} %param.9) | copy-start | bytes 76
  10.4 19.0 %all-to-all-start = ((bf16[32,16,384]{2,1,0:T(8,128)(2,1)}), bf16[32,16,384]{2,1,0:T(8,128)(2,1)S(1)}, u32[]{:S(2)}, u32[]{:S(2)}) async-start(bf16[32,16,384]{2,1,0:T(8,128)(2,1)} %bitcast.14), calls=%async_computation | async-start | bytes 786432 | tf_op jit(solution)/shard_map/all_to_all | solution.py:352
  29.5 10.6 %collective-permute-start.7 = (bf16[16,16,384]{2,1,0:T(8,128)(2,1)S(1)}, bf16[16,16,384]{2,1,0:T(8,128)(2,1)S(1)}, u32[]{:S(2)}, u32[]{:S(2)}) collective-permute-start(bf16[16,16,384]{2,1,0:T(8,128)(2,1)S(1)} %get-tuple-element.39.refs_8_), channel_id=1, source_target_pairs={{0,14},{2,0},{4,2},{6,4},{8,6},{10,8},{12,10},{14,12},{1,15},{3,1}... | collective-permute-start | bytes 589832 | tf_op jit(solution)/shard_map/ppermute | solution.py:337
  35.1 7.6 %collective-permute-start.3 = (bf16[16,16,384]{2,1,0:T(8,128)(2,1)S(1)}, bf16[16,16,384]{2,1,0:T(8,128)(2,1)S(1)}, u32[]{:S(2)}, u32[]{:S(2)}) collective-permute-start(bf16[16,16,384]{2,1,0:T(8,128)(2,1)S(1)} %get-tuple-element.31.refs_0_), channel_id=1, source_target_pairs={{0,2},{2,4},{4,6},{6,8},{8,10},{10,12},{12,14},{14,0},{1,3},{3,5},... | collective-permute-start | bytes 589832 | tf_op jit(solution)/shard_map/ppermute | solution.py:337
  36.2 7.2 %collective-permute-start.14 = (bf16[1,8,32,384]{3,2,1,0:T(8,128)(2,1)S(1)}, bf16[1,8,32,384]{3,2,1,0:T(8,128)(2,1)S(1)}, u32[]{:S(2)}, u32[]{:S(2)}) collective-permute-start(bf16[1,8,32,384]{3,2,1,0:T(8,128)(2,1)S(1)} %get-tuple-element.50), channel_id=1, source_target_pairs={{0,128},{128,0},{1,129},{129,1},{2,130},{130,2},{3,131},{131,3},{4... | collective-permute-start | bytes 589832 | tf_op jit(solution)/shard_map/ppermute | solution.py:330
  37.3 9.3 %collective-permute-start.11 = (bf16[16,16,384]{2,1,0:T(8,128)(2,1)S(1)}, bf16[16,16,384]{2,1,0:T(8,128)(2,1)S(1)}, u32[]{:S(2)}, u32[]{:S(2)}) collective-permute-start(bf16[16,16,384]{2,1,0:T(8,128)(2,1)S(1)} %get-tuple-element.39.refs_8_), channel_id=1, source_target_pairs={{0,2},{2,4},{4,6},{6,8},{8,10},{10,12},{12,14},{14,0},{1,3},{3,5},... | collective-permute-start | bytes 589832 | tf_op jit(solution)/shard_map/ppermute | solution.py:337
  37.4 9.2 %collective-permute-start = (bf16[16,16,384]{2,1,0:T(8,128)(2,1)S(1)}, bf16[16,16,384]{2,1,0:T(8,128)(2,1)S(1)}, u32[]{:S(2)}, u32[]{:S(2)}) collective-permute-start(bf16[16,16,384]{2,1,0:T(8,128)(2,1)S(1)} %get-tuple-element.31.refs_0_), channel_id=1, source_target_pairs={{0,14},{2,0},{4,2},{6,4},{8,6},{10,8},{12,10},{14,12},{1,15},{3,1}... | collective-permute-start | bytes 589832 | tf_op jit(solution)/shard_map/ppermute | solution.py:337
  40.1 9.2 %collective-permute-start.8 = (bf16[16,16,384]{2,1,0:T(8,128)(2,1)S(1)}, bf16[16,16,384]{2,1,0:T(8,128)(2,1)S(1)}, u32[]{:S(2)}, u32[]{:S(2)}) collective-permute-start(bf16[16,16,384]{2,1,0:T(8,128)(2,1)S(1)} %collective-permute-done.7.refs_9_), channel_id=1, source_target_pairs={{0,14},{2,0},{4,2},{6,4},{8,6},{10,8},{12,10},{14,12},{1,15},{3,1}... | collective-permute-start | bytes 589832 | tf_op jit(solution)/shard_map/ppermute | solution.py:337
  42.7 8.7 %collective-permute-start.4 = (bf16[16,16,384]{2,1,0:T(8,128)(2,1)S(1)}, bf16[16,16,384]{2,1,0:T(8,128)(2,1)S(1)}, u32[]{:S(2)}, u32[]{:S(2)}) collective-permute-start(bf16[16,16,384]{2,1,0:T(8,128)(2,1)S(1)} %collective-permute-done.3.refs_7_), channel_id=1, source_target_pairs={{0,2},{2,4},{4,6},{6,8},{8,10},{10,12},{12,14},{14,0},{1,3},{3,5},... | collective-permute-start | bytes 589832 | tf_op jit(solution)/shard_map/ppermute | solution.py:337
  43.5 20.5 %collective-permute-start.15 = (bf16[2,8,32,384]{3,2,1,0:T(8,128)(2,1)S(1)}, bf16[2,8,32,384]{3,2,1,0:T(8,128)(2,1)S(1)}, u32[]{:S(2)}, u32[]{:S(2)}) collective-permute-start(bf16[2,8,32,384]{3,2,1,0:T(8,128)(2,1)S(1)} %maximum_select_fusion.own), channel_id=1, source_target_pairs={{0,1},{1,0},{2,3},{3,2},{4,5},{5,4},{6,7},{7,6},{8,9},{9,8},{10,11... | collective-permute-start | bytes 1179656 | tf_op jit(solution)/shard_map/ppermute | solution.py:330
  46.6 7.9 %collective-permute-start.12 = (bf16[16,16,384]{2,1,0:T(8,128)(2,1)S(1)}, bf16[16,16,384]{2,1,0:T(8,128)(2,1)S(1)}, u32[]{:S(2)}, u32[]{:S(2)}) collective-permute-start(bf16[16,16,384]{2,1,0:T(8,128)(2,1)S(1)} %collective-permute-done.11.refs_15_), channel_id=1, source_target_pairs={{0,2},{2,4},{4,6},{6,8},{8,10},{10,12},{12,14},{14,0},{1,3},{3,5},... | collective-permute-start | bytes 589832 | tf_op jit(solution)/shard_map/ppermute | solution.py:337
  46.6 7.9 %collective-permute-start.1 = (bf16[16,16,384]{2,1,0:T(8,128)(2,1)S(1)}, bf16[16,16,384]{2,1,0:T(8,128)(2,1)S(1)}, u32[]{:S(2)}, u32[]{:S(2)}) collective-permute-start(bf16[16,16,384]{2,1,0:T(8,128)(2,1)S(1)} %collective-permute-done.refs_1_), channel_id=1, source_target_pairs={{0,14},{2,0},{4,2},{6,4},{8,6},{10,8},{12,10},{14,12},{1,15},{3,1}... | collective-permute-start | bytes 589832 | tf_op jit(solution)/shard_map/ppermute | solution.py:337
  49.3 7.9 %collective-permute-start.9 = (bf16[16,16,384]{2,1,0:T(8,128)(2,1)S(1)}, bf16[16,16,384]{2,1,0:T(8,128)(2,1)S(1)}, u32[]{:S(2)}, u32[]{:S(2)}) collective-permute-start(bf16[16,16,384]{2,1,0:T(8,128)(2,1)S(1)} %collective-permute-done.8.refs_10_), channel_id=1, source_target_pairs={{0,14},{2,0},{4,2},{6,4},{8,6},{10,8},{12,10},{14,12},{1,15},{3,1}... | collective-permute-start | bytes 589832 | tf_op jit(solution)/shard_map/ppermute | solution.py:337
  51.4 7.4 %collective-permute-start.5 = (bf16[16,16,384]{2,1,0:T(8,128)(2,1)S(1)}, bf16[16,16,384]{2,1,0:T(8,128)(2,1)S(1)}, u32[]{:S(2)}, u32[]{:S(2)}) collective-permute-start(bf16[16,16,384]{2,1,0:T(8,128)(2,1)S(1)} %collective-permute-done.4.refs_6_), channel_id=1, source_target_pairs={{0,2},{2,4},{4,6},{6,8},{8,10},{10,12},{12,14},{14,0},{1,3},{3,5},... | collective-permute-start | bytes 589832 | tf_op jit(solution)/shard_map/ppermute | solution.py:337
  54.5 9.5 %collective-permute-start.13 = (bf16[16,16,384]{2,1,0:T(8,128)(2,1)S(1)}, bf16[16,16,384]{2,1,0:T(8,128)(2,1)S(1)}, u32[]{:S(2)}, u32[]{:S(2)}) collective-permute-start(bf16[16,16,384]{2,1,0:T(8,128)(2,1)S(1)} %collective-permute-done.12.refs_14_), channel_id=1, source_target_pairs={{0,2},{2,4},{4,6},{6,8},{8,10},{10,12},{12,14},{14,0},{1,3},{3,5},... | collective-permute-start | bytes 589832 | tf_op jit(solution)/shard_map/ppermute | solution.py:337
  54.5 9.5 %collective-permute-start.2 = (bf16[16,16,384]{2,1,0:T(8,128)(2,1)S(1)}, bf16[16,16,384]{2,1,0:T(8,128)(2,1)S(1)}, u32[]{:S(2)}, u32[]{:S(2)}) collective-permute-start(bf16[16,16,384]{2,1,0:T(8,128)(2,1)S(1)} %collective-permute-done.1.refs_2_), channel_id=1, source_target_pairs={{0,14},{2,0},{4,2},{6,4},{8,6},{10,8},{12,10},{14,12},{1,15},{3,1}... | collective-permute-start | bytes 589832 | tf_op jit(solution)/shard_map/ppermute | solution.py:337
  57.2 7.4 %collective-permute-start.10 = (bf16[16,16,384]{2,1,0:T(8,128)(2,1)S(1)}, bf16[16,16,384]{2,1,0:T(8,128)(2,1)S(1)}, u32[]{:S(2)}, u32[]{:S(2)}) collective-permute-start(bf16[16,16,384]{2,1,0:T(8,128)(2,1)S(1)} %collective-permute-done.9.refs_11_), channel_id=1, source_target_pairs={{0,14},{2,0},{4,2},{6,4},{8,6},{10,8},{12,10},{14,12},{1,15},{3,1}... | collective-permute-start | bytes 589832 | tf_op jit(solution)/shard_map/ppermute | solution.py:337
  58.8 7.4 %collective-permute-start.6 = (bf16[16,16,384]{2,1,0:T(8,128)(2,1)S(1)}, bf16[16,16,384]{2,1,0:T(8,128)(2,1)S(1)}, u32[]{:S(2)}, u32[]{:S(2)}) collective-permute-start(bf16[16,16,384]{2,1,0:T(8,128)(2,1)S(1)} %collective-permute-done.5.refs_5_), channel_id=1, source_target_pairs={{0,2},{2,4},{4,6},{6,8},{8,10},{10,12},{12,14},{14,0},{1,3},{3,5},... | collective-permute-start | bytes 589832 | tf_op jit(solution)/shard_map/ppermute | solution.py:337

commit v4 on v3

v4 whole, which is shorter than its diff:
```python
import jax
import jax.numpy as jnp
import numpy as np
from jax import lax
from jax.experimental import pallas as pl
from jax.experimental.pallas import tpu as pltpu
from jax.sharding import Mesh
from jax.sharding import PartitionSpec as P

F = 768
L = 6144
K = 64
CAP = 32
SEG = 8
ROUNDS = 6
LOCAL = 4
HALF = F // 2
Q = L // 4
E = F // 8
ODD = F // 2
EVEN = 128
CLASSES = (0, 4, 2, 6)
LANES = ODD + 4 * EVEN
VMEM = 48 * 1024 * 1024


def angles(steps, freqs):
    return (np.outer(steps, freqs) % L) * (2.0 * np.pi / L)


def odd_bins():
    return np.concatenate([np.arange(1, F, 4), np.arange(3, F, 4)])


def odd_table():
    angle = angles(np.arange(Q), odd_bins())
    sine = np.sin(angle) * np.where(odd_bins() % 4 == 1, 1.0, -1.0)
    return np.concatenate([np.cos(angle), sine], axis=1).astype(np.float32).astype(jnp.bfloat16)


def even_table():
    out = np.zeros((Q // 2, 8, EVEN), np.float32)
    for at, residue in enumerate(CLASSES):
        angle = angles(np.arange(Q // 2), np.arange(residue, F, 8))
        first, second = ((0, 1), (2, 3), (4, 6), (5, 7))[at]
        out[:, first, :E] = np.cos(angle)
        out[:, second, :E] = np.sin(angle) * (-1.0 if residue == 6 else 1.0)
    return out.reshape(Q // 2, 8 * EVEN).astype(jnp.bfloat16)


def tap_tables():
    out = np.zeros((2, K, LANES), np.float32)
    angle = angles(np.arange(K), odd_bins())
    out[:, :, :ODD] = np.cos(angle), np.sin(angle)
    for at, residue in enumerate(CLASSES):
        angle = angles(np.arange(K), np.arange(residue, F, 8))
        start = ODD + at * EVEN
        out[:, :, start : start + E] = np.cos(angle), np.sin(angle)
    return out


def spectra_kernel(
    counts, section, taps, traces, tap_source, odd_source, even_source, out, own, away, x, tap_table, odd, even, spread, y, w, re, im, sems
):
    segs, rows = traces.shape[0], x.shape[0]
    loads = [pltpu.make_async_copy(traces.at[s], x.at[pl.ds(s * CAP, CAP)], sems.at[s]) for s in range(segs)]
    even_load = pltpu.make_async_copy(even_source, even, sems.at[segs])
    odd_load = pltpu.make_async_copy(odd_source, odd, sems.at[segs + 1])
    tap_load = pltpu.make_async_copy(tap_source, tap_table, sems.at[segs + 2])
    for copy in loads:
        copy.start()

    src = lax.broadcasted_iota(jnp.int32, (LANES, F), 0)
    dst = lax.broadcasted_iota(jnp.int32, (LANES, F), 1)
    residue = dst & 7
    place = jnp.where((dst & 3) == 1, dst >> 2, (dst >> 2) + ODD // 2)
    for at, cls in enumerate(CLASSES):
        place = jnp.where(residue == cls, (dst >> 3) + (ODD + at * EVEN), place)
    spread[...] = jnp.where(src == place, 1.0, 0.0).astype(jnp.bfloat16)
    for copy in (even_load, odd_load, tap_load):
        copy.start()

    def tile(t, carry):
        at = pl.ds(pl.multiple_of(t * 16, 16), 16)
        total = jnp.zeros((16, 128), jnp.float32)
        for c in range(L // 128):
            v = x[at, c * 128 : (c + 1) * 128].astype(jnp.float32)
            total = total + v * v
        mean = jnp.sum(total, axis=1, keepdims=True) * (1.0 / L)
        top = jnp.broadcast_to(2.5 * jnp.sqrt(mean + 1e-6), (16, 128))

        def clipped(start):
            v = x[at, start : start + 128].astype(jnp.float32)
            v = jnp.minimum(jnp.maximum(v, -top), top)
            return v.astype(jnp.bfloat16).astype(jnp.float32)

        def keep(ref, n, c, v):
            hi = v.astype(jnp.bfloat16)
            lo = (v - hi.astype(jnp.float32)).astype(jnp.bfloat16)
            ref[2 * n, at, c * 128 : (c + 1) * 128] = hi
            ref[2 * n + 1, at, c * 128 : (c + 1) * 128] = lo

        half = Q // 256
        for c in range(half):
            even_sums = []
            for c_at in (c, c + half):
                x0, x1, x2, x3 = [clipped(q * Q + c_at * 128) for q in range(4)]
                keep(y, 0, c_at, x0 - x2)
                keep(y, 1, c_at, x3 - x1)
                s02, s13 = x0 + x2, x1 + x3
                even_sums.append((s02 + s13, s02 - s13))
            (a0, a2), (b0, b2) = even_sums
            for n, v in enumerate((a0 + b0, a0 - b0, a2, -b2)):
                keep(w, n, c, v)
        return carry

    for s in range(segs):
        loads[s].wait()
        lax.fori_loop(s * CAP // 16, (s + 1) * CAP // 16, tile, 0)

    def product(ref, n, table, lanes):
        a = jnp.dot(ref[2 * n], table[:, lanes], preferred_element_type=jnp.float32)
        b = jnp.dot(ref[2 * n + 1], table[:, lanes], preferred_element_type=jnp.float32)
        return a + b

    even_load.wait()
    for n in range(2):
        p = product(w, n, even, slice(2 * n * EVEN, (2 * n + 2) * EVEN))
        at = slice(ODD + n * EVEN, ODD + (n + 1) * EVEN)
        re[:, at] = p[:, :EVEN]
        im[:, at] = -p[:, EVEN:]

    def paired(p, q, at, width):
        sign = jnp.where(lax.broadcasted_iota(jnp.int32, (1, width), 1) < width // 2, 1.0, -1.0)
        re[:, at] = p[:, :width] + q[:, width:]
        im[:, at] = (q[:, :width] - p[:, width:]) * sign

    lanes = slice(4 * EVEN, 8 * EVEN)
    paired(product(w, 2, even, lanes), product(w, 3, even, lanes), slice(ODD + 2 * EVEN, LANES), 2 * EVEN)
    odd_load.wait()
    lanes = slice(0, 2 * ODD)
    paired(product(y, 0, odd, lanes), product(y, 1, odd, lanes), slice(0, ODD), ODD)

    tap_load.wait()
    square = (K, K)
    same = lax.broadcasted_iota(jnp.int32, square, 0) == lax.broadcasted_iota(jnp.int32, square, 1)
    column = jnp.sum(jnp.where(same, jnp.broadcast_to(taps[...], square), 0.0), axis=1, keepdims=True)
    hr = jnp.sum(tap_table[0] * column, axis=0, keepdims=True)
    hi = -jnp.sum(tap_table[1] * column, axis=0, keepdims=True)
    fr = re[...] * hr - im[...] * hi
    fi = re[...] * hi + im[...] * hr
    power = jnp.sum(fr * fr + fi * fi, axis=1, keepdims=True) * (1.0 / F) + 1e-6
    slot = lax.broadcasted_iota(jnp.int32, (rows, 1), 0) % CAP
    live = jnp.where(slot < counts[0], 1.0, 0.0)
    scale = live / jnp.sqrt(power)
    white = jnp.concatenate([fr * scale, fi * scale], axis=0).astype(jnp.bfloat16)
    ordered = jnp.dot(white, spread[...], preferred_element_type=jnp.float32)
    for half in range(2):
        for seg in range(LOCAL):
            for part in range(2):
                start, piece = part * rows + seg * CAP, seg * 2 + part
                for fg in range(HALF // 128):
                    at = half * HALF + fg * 128
                    block = pltpu.roll(ordered[start : start + CAP, at : at + 128], 16 * piece, 1)
                    out[half, piece, :, fg * 128 : (fg + 1) * 128] = block.astype(jnp.bfloat16)
    for half in range(2):

        @pl.when(section[0] == half)
        def _(half=half):
            own[0] = out[half]
            away[0] = out[1 - half]


def spectra_of(traces, counts, taps, section):
    segs, cap, length = traces.shape
    rows = segs * cap
    far_away = pl.BlockSpec(memory_space=pl.ANY)
    return pl.pallas_call(
        spectra_kernel,
        out_shape=[jax.ShapeDtypeStruct((n, 2 * segs, cap, HALF), jnp.bfloat16) for n in (2, 1, 1)],
        in_specs=[
            pl.BlockSpec(memory_space=pltpu.SMEM),
            pl.BlockSpec(memory_space=pltpu.SMEM),
            pl.BlockSpec(memory_space=pltpu.VMEM),
            far_away,
            far_away,
            far_away,
            far_away,
        ],
        out_specs=[pl.BlockSpec(memory_space=pltpu.VMEM)] * 3,
        scratch_shapes=[
            pltpu.VMEM((rows, length), jnp.bfloat16),
            pltpu.VMEM((2, K, LANES), jnp.float32),
            pltpu.VMEM((Q, 2 * ODD), jnp.bfloat16),
            pltpu.VMEM((Q // 2, 8 * EVEN), jnp.bfloat16),
            pltpu.VMEM((LANES, F), jnp.bfloat16),
            pltpu.VMEM((4, rows, Q), jnp.bfloat16),
            pltpu.VMEM((8, rows, Q // 2), jnp.bfloat16),
            pltpu.VMEM((rows, LANES), jnp.float32),
            pltpu.VMEM((rows, LANES), jnp.float32),
            pltpu.SemaphoreType.DMA((segs + 3,)),
        ],
        compiler_params=pltpu.CompilerParams(vmem_limit_bytes=62 * 1024 * 1024),
        name="spectra",
    )(counts, section, taps.reshape(1, K), traces, tap_tables(), odd_table(), even_table())


def near_round(masks):
    return sum(jnp.where(masks[r] == 1, r, 0) for r in range(ROUNDS))


def far_round(masks, n):
    return n + (n >= near_round(masks)).astype(jnp.int32)


def pick_kernel(masks, z, *refs):
    slabs, (out, held, sems) = (refs[:8], refs[8:16]), refs[16:]
    copies = []
    for n in range(out.shape[1]):
        mask = masks[far_round(masks, n)]
        apart = (jnp.bitwise_xor(z[0], (mask >> 1) & 7) - z[0]) & 7
        across = ((mask >> 4) << 1) | (mask & 1)
        for k in range(8):

            @pl.when(apart == k)
            def _(n=n, k=k, across=across):
                for d in range(out.shape[0]):
                    src = jnp.bitwise_xor(across, d)
                    for h in range(2):
                        held[n, d, h] = slabs[h][k][src]

        copies.append(pltpu.make_async_copy(held.at[n], out.at[:, n], sems.at[n]))
        copies[-1].start()
    for copy in copies:
        copy.wait()


def pick(first, second, masks, z):
    inside = pl.BlockSpec(memory_space=pltpu.VMEM)
    half = (2, CAP // 2, HALF)
    return pl.pallas_call(
        pick_kernel,
        out_shape=jax.ShapeDtypeStruct((16, ROUNDS - 1) + half, jnp.bfloat16),
        in_specs=[pl.BlockSpec(memory_space=pltpu.SMEM)] * 2 + [inside] * 16,
        out_specs=pl.BlockSpec(memory_space=pl.ANY),
        scratch_shapes=[
            pltpu.VMEM((ROUNDS - 1, 16) + half, jnp.bfloat16),
            pltpu.SemaphoreType.DMA((ROUNDS - 1,)),
        ],
        compiler_params=pltpu.CompilerParams(vmem_limit_bytes=8 * 1024 * 1024),
        name="pick",
    )(masks, z, *first, *second)


def place_bits(shape, dtype):
    lane = lax.broadcasted_iota(dtype, shape, 1)
    return [(lane & (16 << b)) != 0 for b in range(3)]


def swirl(tiles, bits):
    held = [tiles[-n % 8] for n in range(8)]
    for b in range(3):
        held = [jnp.where(bits[b], held[(n - (1 << b)) % 8], held[n]) for n in range(8)]
    return held


def fill_weights(own, out, it, fg):
    bits = place_bits((8, 128), jnp.int32)
    row = lax.broadcasted_iota(jnp.int32, (16, 128), 0)
    diagonal = (lax.broadcasted_iota(jnp.int32, (16, 128), 1) & 15) == row
    lanes = pl.ds(pl.multiple_of(fg * 128, 128), 128)
    for h in range(2):
        for piece in range(8):
            block = own[h, piece, it * 16 : (it + 1) * 16, lanes].astype(jnp.float32) * (1.0 / SEG)
            for tile in range(2):
                v = block[tile * 8 : (tile + 1) * 8]
                v = pltpu.roll(pltpu.roll(v, -16 * piece % 128, 1), 0, 1, stride=16, stride_axis=0)
                for b in range(3):
                    v = jnp.where(bits[b], pltpu.roll(v, 8 - (1 << b), 0), v)
                for g in range(8):
                    line = jnp.broadcast_to(v[-g % 8][None], (16, 128))
                    at = h * 128 + (g + piece) % 8 * 16
                    out[fg, g, at : at + 16, tile * 128 : (tile + 1) * 128] = jnp.where(diagonal, line, 0.0).astype(
                        jnp.bfloat16
                    )


GROUPS, HALVES = HALF // 128, CAP // 16


def arrange(left, rounds, r, block):
    bits = place_bits((16, 128), jnp.int16)
    for fg in range(GROUPS):
        for h in range(2):
            for jh in range(2):
                x = [block(p, h, jh, slice(fg * 128, (fg + 1) * 128)) for p in range(8)]
                turned = []
                for p in range(8):
                    other = x[p ^ 1]
                    turned.append(pltpu.roll(other, 16, 1) if p % 2 else -pltpu.roll(other, 112, 1))
                for a, tiles in enumerate((x, turned)):
                    at = pl.ds(pl.multiple_of((a * rounds + r) * CAP + jh * 16, 16), 16)
                    for g, z in enumerate(swirl(tiles, bits)):
                        left[fg, g, at, h * 128 : (h + 1) * 128] = z


def multiply(left, weights, sums, fg):
    for g in range(8):
        sums[fg, g] = jnp.dot(left[fg, g], weights[fg, g], preferred_element_type=jnp.float32).astype(jnp.bfloat16)


def finish(sums, done, rounds, it, fg):
    bits = place_bits((16, 128), jnp.int16)
    for r in range(rounds):
        for a in range(2):
            for jh in range(2):
                row = (a * rounds + r) * CAP + jh * 16
                for tile in range(2):
                    cols = slice(tile * 128, (tile + 1) * 128)
                    turned = swirl([sums[fg, g, row : row + 16, cols] for g in range(8)], bits)
                    for i in range(8):
                        done[r, a, it * 16 + tile * 8 + i, jh * 16 : (jh + 1) * 16, fg * 128 : (fg + 1) * 128] = (
                            pltpu.roll(turned[i], -16 * i % 128, 1)
                        )


def near_kernel(masks, own, sibling, out, weights, left, held, sums, done, sems):
    arrange(left, 1, 0, lambda p, h, jh, lanes: sibling[h, p, jh * 16 : (jh + 1) * 16, lanes])
    copies = []
    for it in range(HALVES):

        def fill(fg, carry, it=it):
            fill_weights(own, held.at[it], it, fg)
            return carry

        lax.fori_loop(0, GROUPS, fill, 0)
        copies.append(pltpu.make_async_copy(held.at[it], weights.at[it], sems.at[it]))
        copies[-1].start()
        for fg in range(GROUPS):
            multiply(left, held.at[it], sums, fg)
            finish(sums, done, 1, it, fg)
    copies.append(pltpu.make_async_copy(done.at[0], out.at[near_round(masks)], sems.at[HALVES]))
    copies[-1].start()
    for copy in copies:
        copy.wait()


def near_of(masks, own, sibling):
    inside = pl.BlockSpec(memory_space=pltpu.VMEM)
    return pl.pallas_call(
        near_kernel,
        out_shape=[
            jax.ShapeDtypeStruct((ROUNDS, 2, CAP, CAP, HALF), jnp.bfloat16),
            jax.ShapeDtypeStruct((HALVES, GROUPS, 8, 256, 256), jnp.bfloat16),
        ],
        in_specs=[pl.BlockSpec(memory_space=pltpu.SMEM), inside, inside],
        out_specs=[pl.BlockSpec(memory_space=pltpu.HBM)] * 2,
        scratch_shapes=[
            pltpu.VMEM((GROUPS, 8, 2 * CAP, 256), jnp.bfloat16),
            pltpu.VMEM((HALVES, GROUPS, 8, 256, 256), jnp.bfloat16),
            pltpu.VMEM((GROUPS, 8, 2 * CAP, 256), jnp.bfloat16),
            pltpu.VMEM((1, 2, CAP, CAP, HALF), jnp.bfloat16),
            pltpu.SemaphoreType.DMA((HALVES + 1,)),
        ],
        compiler_params=pltpu.CompilerParams(vmem_limit_bytes=24 * 1024 * 1024),
        cost_estimate=pl.CostEstimate(flops=400000000, bytes_accessed=9000000, transcendentals=0),
        name="near",
    )(masks, own, sibling)


def far_kernel(masks, partner, weights, kept, out, left, held, sums, done, load_sems, store_sems):
    rounds = ROUNDS - 1
    loads = [
        [
            pltpu.make_async_copy(weights.at[it, fg], held.at[it, fg], load_sems.at[it * GROUPS + fg])
            for fg in range(GROUPS)
        ]
        for it in range(HALVES)
    ]
    for it in range(HALVES):
        for fg in range(GROUPS):
            loads[it][fg].start()

    def arrange_one(r, carry):
        arrange(left, rounds, r, lambda p, h, jh, lanes: partner[2 * p + jh, r, h, :, lanes])
        return carry

    lax.fori_loop(0, rounds, arrange_one, 0)

    def store(it, r):
        part = pl.ds(it * 16, 16)
        return pltpu.make_async_copy(
            done.at[r, :, part], out.at[far_round(masks, r), :, part], store_sems.at[it * rounds + r]
        )

    steps = [(it, fg) for it in range(HALVES) for fg in range(GROUPS)]
    for n, (it, fg) in enumerate(steps + [(HALVES, 0)]):
        if n < len(steps):
            loads[it][fg].wait()
            multiply(left, held.at[it], sums, fg)
        if n > 0:
            last_it, last_fg = steps[n - 1]
            finish(sums, done, rounds, last_it, last_fg)
            if last_fg == GROUPS - 1:
                for r in range(rounds):
                    store(last_it, r).start()

    for it in range(HALVES):
        for r in range(rounds):
            store(it, r).wait()


def far_of(masks, partner, weights, kept):
    rounds = ROUNDS - 1
    rows = 2 * rounds * CAP
    return pl.pallas_call(
        far_kernel,
        out_shape=jax.ShapeDtypeStruct(kept.shape, kept.dtype),
        in_specs=[
            pl.BlockSpec(memory_space=pltpu.SMEM),
            pl.BlockSpec(memory_space=pltpu.VMEM),
            pl.BlockSpec(memory_space=pl.ANY),
            pl.BlockSpec(memory_space=pl.ANY),
        ],
        out_specs=pl.BlockSpec(memory_space=pl.ANY),
        scratch_shapes=[
            pltpu.VMEM((GROUPS, 8, rows, 256), jnp.bfloat16),
            pltpu.VMEM((HALVES, GROUPS, 8, 256, 256), jnp.bfloat16),
            pltpu.VMEM((GROUPS, 8, rows, 256), jnp.bfloat16),
            pltpu.VMEM((rounds,) + kept.shape[1:], jnp.bfloat16),
            pltpu.SemaphoreType.DMA((HALVES * GROUPS,)),
            pltpu.SemaphoreType.DMA((HALVES * rounds,)),
        ],
        input_output_aliases={3: 0},
        compiler_params=pltpu.CompilerParams(vmem_limit_bytes=VMEM),
        name="far",
    )(masks, partner, weights, kept)


def flipped(block, axis):
    return lax.ppermute(block, axis, [(0, 1), (1, 0)])


def around(block, last):
    ring = lax.axis_size("z")

    def shift(held, way):
        return lax.ppermute(held, "z", [(i, (i + way) % ring) for i in range(ring)])

    slabs = [block] * ring
    for step in range(1, ring // 2):
        slabs[-step] = shift(slabs[1 - step], 1)
        slabs[step] = shift(slabs[step - 1], -1)
    slabs[ring // 2] = shift(slabs[(ring // 2 + last) % ring], last)
    return slabs


def shards(traces, counts, taps, masks):
    section = lax.axis_index("section")
    z = lax.axis_index("z")

    white, own, away = spectra_of(traces, counts, taps, section[None])
    pieces = lax.all_to_all(
        white.reshape(32, CAP // 2, HALF), ("section", "yh", "x", "core"), 0, 0, tiled=True
    )
    first, second = around(pieces[:16], 1), around(pieces[16:], -1)

    own, away, _ = lax.optimization_barrier((own, away, pieces))
    other = flipped(away, "section")
    both = jnp.where(section == 0, jnp.concatenate([own, other]), jnp.concatenate([other, own]))
    sibling = flipped(both, "core")

    first, second, both, sibling = lax.optimization_barrier((first, second, both, sibling))
    picked = pick(first, second, masks, z[None])
    picked, both, sibling = lax.optimization_barrier((picked, both, sibling))
    partners = lax.all_to_all(picked.reshape(16, -1, HALF), ("yh", "x", "core"), 0, 0, tiled=True)
    result, weights = near_of(masks, both, sibling)
    return far_of(masks, partners.reshape(picked.shape), weights, result)[None]


def solution(mesh):
    fine = Mesh(mesh.devices.reshape(2, 2, 4, 8, 2), ("section", "yh", "x", "z", "core"))
    blk = ("yh", "x", "z", "core")
    return jax.shard_map(
        shards,
        mesh=fine,
        in_specs=(P("section", blk, None), P(blk), P(), P()),
        out_specs=P(blk, None, None, None, None, "section"),
        check_vma=False,
    )
```

time: 111 us -> 109 us (0.982)
  waiting for transfers between devices: 15.6 us -> 31.2 us
  blocking collectives: 33.9 us -> 19 us
  other arithmetic: 2.78 us -> 1.09 us
  starting transfers between devices: 31 us -> 29.8 us
    all_to_all x1, blocking collectives: 33.9 us -> 19 us  [shards(): lax.all_to_all(white.reshape(32, CAP // 2, HALF), ('section', 'yh', 'x',...]
    all_to_all x1, waiting for transfers between devices: 9.05 us -> 18 us  [shards(): lax.all_to_all(picked.reshape(16, -1, HALF), ('yh', 'x', 'core'), 0, 0, t...]
    ppermute x14, waiting for transfers between devices: 6.54 us -> 13.1 us  [shift(): return lax.ppermute(held, 'z', [(i, (i + way) % ring) for i in range(ring)])]
    unnamed x2 -> x4, local copies, waits for them, and re-layouts: 0.01 us -> 2.66 us
    all_to_all x1, starting transfers between devices: 8.6 us -> 7.43 us  [shards(): lax.all_to_all(picked.reshape(16, -1, HALF), ('yh', 'x', 'core'), 0, 0, t...]
  transfers between devices with their start and end apart: 17 -> 17, of which waited for: 5 -> 7; matrix products, arithmetic and copies ran while one was open for 4% -> 1% of each run, Pallas kernels for 4% -> 6%
where the time goes in v4:
time: 109 us
  waiting for transfers between devices  31.2 us (29%)
  starting transfers between devices  29.8 us (27%)
  Pallas kernels  24.2 us (22%)
  blocking collectives  19 us (17%)
  local copies, waits for them, and re-layouts  2.7 us (2%)
  other arithmetic  1.09 us (1%)
    ppermute x14, starting transfers between devices, shift(): return lax.ppermute(held, 'z', [(i, (i + way) % ring) for i in range(ring)])  20.2 us
    all_to_all x1, blocking collectives, shards(): lax.all_to_all(white.reshape(32, CAP // 2, HALF), ('section', 'yh', 'x',...  19 us
    all_to_all x1, waiting for transfers between devices, shards(): lax.all_to_all(picked.reshape(16, -1, HALF), ('yh', 'x', 'core'), 0, 0, t...  18 us
    ppermute x14, waiting for transfers between devices, shift(): return lax.ppermute(held, 'z', [(i, (i + way) % ring) for i in range(ring)])  13.1 us
    pallas_call x1, Pallas kernels, spectra_of(): pl.pallas_call(spectra_kernel, out_shape=[jax.ShapeDtypeStruct((n, 2 * se...  8.47 us
    all_to_all x1, starting transfers between devices, shards(): lax.all_to_all(picked.reshape(16, -1, HALF), ('yh', 'x', 'core'), 0, 0, t...  7.43 us
    pallas_call x1, Pallas kernels, far_of(): pl.pallas_call(far_kernel, out_shape=jax.ShapeDtypeStruct(kept.shape, kep...  7.23 us
    pallas_call x1, Pallas kernels, near_of(): pl.pallas_call(near_kernel, out_shape=[jax.ShapeDtypeStruct((ROUNDS, 2, C...  6.49 us
  transfers between devices with their start and end apart: 17, of which 7 were waited for; matrix products, arithmetic and copies ran while one was open for 1% of the time, Pallas kernels for 6%

profile of v4, /device:TPU:1, one launch (start us, length us, event | category | flops | bytes accessed | tf_op | source)
XLA Modules:
  0.0 108.9 jit_solution(4948433971094451806)
XLA Ops:
  0.7 8.5 %spectra.1 = (bf16[2,8,32,384]{3,2,1,0:T(8,128)(2,1)}, bf16[1,8,32,384]{3,2,1,0:T(8,128)(2,1)}, bf16[1,8,32,384]{3,2,1,0:T(8,128)(2,1)}) custom-call(s32[1]{0:T(128)S(6)} %copy.10.counts, s32[1]{0:T(128)} %bitcast.1.section, f32[1,64]{1,0:T(1,128)} %bitcast.9, bf16[4,32,6144]{2,1,0:T(8,128)(2,1)} %traces.1, f32[2,64,896]{2,1,0:T(8,128)} %constant.17.clone.tap_source, ...), custom_call_target="tpu_custom_call" | custom-call | tf_op jit(solution)/shard_map/spectra/pallas_call | solution.py:178
  9.1 19.0 %all_to_all.10 = bf16[32,16,384]{2,1,0:T(8,128)(2,1)S(1)} all-to-all(bf16[32,16,384]{2,1,0:T(8,128)(2,1)} %bitcast.8), channel_id=1, replica_groups=mesh['section'=2,'yh'=2,'x'=4,'z'=8,'core'=2] {'section','yh','x','core'}, dimensions={0} | all-to-all | bytes 786432 | tf_op jit(solution)/shard_map/all_to_all | solution.py:463
  28.2 5.7 %collective-permute-start.7 = (bf16[16,16,384]{2,1,0:T(8,128)(2,1)S(1)}, bf16[16,16,384]{2,1,0:T(8,128)(2,1)S(1)}, u32[]{:S(2)}, u32[]{:S(2)}) collective-permute-start(bf16[16,16,384]{2,1,0:T(8,128)(2,1)S(1)} %get-tuple-element.46.refs_8_), channel_id=1, source_target_pairs={{0,14},{2,0},{4,2},{6,4},{8,6},{10,8},{12,10},{14,12},{1,15},{3,1}... | collective-permute-start | bytes 589832 | tf_op jit(solution)/shard_map/ppermute | solution.py:448
  33.9 0.4 collective-permute-start.14
  34.2 2.7 %collective-permute-start = (bf16[16,16,384]{2,1,0:T(8,128)(2,1)S(1)}, bf16[16,16,384]{2,1,0:T(8,128)(2,1)S(1)}, u32[]{:S(2)}, u32[]{:S(2)}) collective-permute-start(bf16[16,16,384]{2,1,0:T(8,128)(2,1)S(1)} %get-tuple-element.38.refs_0_), channel_id=1, source_target_pairs={{0,14},{2,0},{4,2},{6,4},{8,6},{10,8},{12,10},{14,12},{1,15},{3,1}... | collective-permute-start | bytes 589832 | tf_op jit(solution)/shard_map/ppermute | solution.py:448
  36.9 1.1 %collective-permute-done.7.refs_9_ = bf16[16,16,384]{2,1,0:T(8,128)(2,1)S(1)} collective-permute-done((bf16[16,16,384]{2,1,0:T(8,128)(2,1)S(1)}, bf16[16,16,384]{2,1,0:T(8,128)(2,1)S(1)}, u32[]{:S(2)}, u32[]{:S(2)}) %collective-permute-start.7) | collective-permute-done | bytes 196640 | tf_op jit(solution)/shard_map/ppermute | solution.py:448
  38.0 3.4 %collective-permute-start.8 = (bf16[16,16,384]{2,1,0:T(8,128)(2,1)S(1)}, bf16[16,16,384]{2,1,0:T(8,128)(2,1)S(1)}, u32[]{:S(2)}, u32[]{:S(2)}) collective-permute-start(bf16[16,16,384]{2,1,0:T(8,128)(2,1)S(1)} %collective-permute-done.7.refs_9_), channel_id=1, source_target_pairs={{0,14},{2,0},{4,2},{6,4},{8,6},{10,8},{12,10},{14,12},{1,15},{3,1}... | collective-permute-start | bytes 589832 | tf_op jit(solution)/shard_map/ppermute | solution.py:448
  41.5 1.1 %maximum_select_fusion.own = bf16[2,8,32,384]{3,2,1,0:T(8,128)(2,1)S(1)} fusion(bf16[1,8,32,384]{3,2,1,0:T(8,128)(2,1)S(1)} %collective-permute-done.14, bf16[1,8,32,384]{3,2,1,0:T(8,128)(2,1)} %get-tuple-element.36, pred[]{:T(512)S(6)} %eq.3), kind=kLoop, calls=%fused_computation | loop fusion | flops 589824 | bytes 786433 | tf_op jit(solution)/shard_map/jit(_where)/select_n | solution.py:470
  42.5 1.9 %collective-permute-start.15 = (bf16[2,8,32,384]{3,2,1,0:T(8,128)(2,1)S(1)}, bf16[2,8,32,384]{3,2,1,0:T(8,128)(2,1)}, u32[]{:S(2)}, u32[]{:S(2)}) collective-permute-start(bf16[2,8,32,384]{3,2,1,0:T(8,128)(2,1)S(1)} %maximum_select_fusion.own), channel_id=1, source_target_pairs={{0,1},{1,0},{2,3},{3,2},{4,5},{5,4},{6,7},{7,6},{8,9},{9,8},{10,11... | collective-permute-start | bytes 1179656 | tf_op jit(solution)/shard_map/ppermute | solution.py:441
  44.4 0.9 collective-permute-done.11.refs_15_
  45.3 2.7 %collective-permute-start.1 = (bf16[16,16,384]{2,1,0:T(8,128)(2,1)S(1)}, bf16[16,16,384]{2,1,0:T(8,128)(2,1)S(1)}, u32[]{:S(2)}, u32[]{:S(2)}) collective-permute-start(bf16[16,16,384]{2,1,0:T(8,128)(2,1)S(1)} %collective-permute-done.refs_1_), channel_id=1, source_target_pairs={{0,14},{2,0},{4,2},{6,4},{8,6},{10,8},{12,10},{14,12},{1,15},{3,1}... | collective-permute-start | bytes 589832 | tf_op jit(solution)/shard_map/ppermute | solution.py:448
  48.0 1.2 %collective-permute-start.9 = (bf16[16,16,384]{2,1,0:T(8,128)(2,1)S(1)}, bf16[16,16,384]{2,1,0:T(8,128)(2,1)S(1)}, u32[]{:S(2)}, u32[]{:S(2)}) collective-permute-start(bf16[16,16,384]{2,1,0:T(8,128)(2,1)S(1)} %collective-permute-done.8.refs_10_), channel_id=1, source_target_pairs={{0,14},{2,0},{4,2},{6,4},{8,6},{10,8},{12,10},{14,12},{1,15},{3,1}... | collective-permute-start | bytes 589832 | tf_op jit(solution)/shard_map/ppermute | solution.py:448
  49.5 3.7 %collective-permute-done.12.refs_14_ = bf16[16,16,384]{2,1,0:T(8,128)(2,1)S(1)} collective-permute-done((bf16[16,16,384]{2,1,0:T(8,128)(2,1)S(1)}, bf16[16,16,384]{2,1,0:T(8,128)(2,1)S(1)}, u32[]{:S(2)}, u32[]{:S(2)}) %collective-permute-start.12) | collective-permute-done | bytes 196640 | tf_op jit(solution)/shard_map/ppermute | solution.py:448
  53.2 2.7 %collective-permute-start.2 = (bf16[16,16,384]{2,1,0:T(8,128)(2,1)S(1)}, bf16[16,16,384]{2,1,0:T(8,128)(2,1)S(1)}, u32[]{:S(2)}, u32[]{:S(2)}) collective-permute-start(bf16[16,16,384]{2,1,0:T(8,128)(2,1)S(1)} %collective-permute-done.1.refs_2_), channel_id=1, source_target_pairs={{0,14},{2,0},{4,2},{6,4},{8,6},{10,8},{12,10},{14,12},{1,15},{3,1}... | collective-permute-start | bytes 589832 | tf_op jit(solution)/shard_map/ppermute | solution.py:448
  55.9 1.6 %collective-permute-start.10 = (bf16[16,16,384]{2,1,0:T(8,128)(2,1)S(1)}, bf16[16,16,384]{2,1,0:T(8,128)(2,1)S(1)}, u32[]{:S(2)}, u32[]{:S(2)}) collective-permute-start(bf16[16,16,384]{2,1,0:T(8,128)(2,1)S(1)} %collective-permute-done.9.refs_11_), channel_id=1, source_target_pairs={{0,14},{2,0},{4,2},{6,4},{8,6},{10,8},{12,10},{14,12},{1,15},{3,1}... | collective-permute-start | bytes 589832 | tf_op jit(solution)/shard_map/ppermute | solution.py:448
  57.5 3.5 %collective-permute-done.13.refs_13_ = bf16[16,16,384]{2,1,0:T(8,128)(2,1)S(1)} collective-permute-done((bf16[16,16,384]{2,1,0:T(8,128)(2,1)S(1)}, bf16[16,16,384]{2,1,0:T(8,128)(2,1)S(1)}, u32[]{:S(2)}, u32[]{:S(2)}) %collective-permute-start.13) | collective-permute-done | bytes 196640 | tf_op jit(solution)/shard_map/ppermute | solution.py:448
  61.0 1.5 %collective-permute-done.10.refs_12_ = bf16[16,16,384]{2,1,0:T(8,128)(2,1)S(1)} collective-permute-done((bf16[16,16,384]{2,1,0:T(8,128)(2,1)S(1)}, bf16[16,16,384]{2,1,0:T(8,128)(2,1)S(1)}, u32[]{:S(2)}, u32[]{:S(2)}) %collective-permute-start.10) | collective-permute-done | bytes 196640 | tf_op jit(solution)/shard_map/ppermute | solution.py:448
  62.5 2.4 %collective-permute-done.6.refs_4_ = bf16[16,16,384]{2,1,0:T(8,128)(2,1)S(1)} collective-permute-done((bf16[16,16,384]{2,1,0:T(8,128)(2,1)S(1)}, bf16[16,16,384]{2,1,0:T(8,128)(2,1)S(1)}, u32[]{:S(2)}, u32[]{:S(2)}) %collective-permute-start.6) | collective-permute-done | bytes 196640 | tf_op jit(solution)/shard_map/ppermute | solution.py:448
  64.9 2.0 %pick.1 = bf16[16,5,2,16,384]{4,3,2,1,0:T(8,128)(2,1)} custom-call(s32[6]{0:T(128)S(1)} %copy-done.1, s32[1]{0:T(128)} %bitcast.z, bf16[16,16,384]{2,1,0:T(8,128)(2,1)S(1)} %get-tuple-element.38.refs_0_, bf16[16,16,384]{2,1,0:T(8,128)(2,1)S(1)} %collective-permute-done.refs_1_, bf16[16,16,384]{2,1,0:T(8,128)(2,1)S(1)} %collective-permute-done.1.refs_2_, ...), custom_call_target="tpu_custom_call" | custom-call | tf_op jit(solution)/shard_map/pick/pallas_call | solution.py:241
  66.9 7.4 %all-to-all-start.1 = ((bf16[16,160,384]{2,1,0:T(8,128)(2,1)}), bf16[16,160,384]{2,1,0:T(8,128)(2,1)S(1)}, u32[]{:S(2)}, u32[]{:S(2)}) async-start(bf16[16,160,384]{2,1,0:T(8,128)(2,1)} %bitcast.4), calls=%async_computation.1 | async-start | bytes 3932160 | tf_op jit(solution)/shard_map/all_to_all | solution.py:476
  74.3 6.5 %near.1 = (bf16[6,2,32,32,384]{4,3,2,1,0:T(8,128)(2,1)}, bf16[2,3,8,256,256]{4,3,2,1,0:T(8,128)(2,1)S(1)}) custom-call(s32[6]{0:T(128)S(1)} %copy-done.1, bf16[2,8,32,384]{3,2,1,0:T(8,128)(2,1)S(1)} %maximum_select_fusion.own, bf16[2,8,32,384]{3,2,1,0:T(8,128)(2,1)} %collective-permute-done.15.sibling), custom_call_target="tpu_custom_call" | custom-call | flops 400000000 | bytes 9000000 | tf_op jit(solution)/shard_map/near/pallas_call | solution.py:350
  80.9 2.6 %copy-done = bf16[2,3,8,256,256]{4,3,2,1,0:T(8,128)(2,1)} copy-done((bf16[2,3,8,256,256]{4,3,2,1,0:T(8,128)(2,1)}, bf16[2,3,8,256,256]{4,3,2,1,0:T(8,128)(2,1)S(1)}, u32[]{:S(2)}) %copy-start) | copy-done | bytes 6291480
  83.5 18.0 %all-to-all-done.1 = bf16[16,160,384]{2,1,0:T(8,128)(2,1)S(1)} async-done(((bf16[16,160,384]{2,1,0:T(8,128)(2,1)}), bf16[16,160,384]{2,1,0:T(8,128)(2,1)S(1)}, u32[]{:S(2)}, u32[]{:S(2)}) %all-to-all-start.1) | async-done | bytes 1966112 | tf_op jit(solution)/shard_map/all_to_all | solution.py:476
  101.5 7.2 %far.1 = bf16[6,2,32,32,384]{4,3,2,1,0:T(8,128)(2,1)} custom-call(s32[6]{0:T(128)S(1)} %copy-done.1, bf16[16,5,2,16,384]{4,3,2,1,0:T(8,128)(2,1)S(1)} %bitcast.7, bf16[2,3,8,256,256]{4,3,2,1,0:T(8,128)(2,1)} %copy-done, bf16[6,2,32,32,384]{4,3,2,1,0:T(8,128)(2,1)} %get-tuple-element.60.kept), custom_call_target="tpu_custom_call", output_to_operand_aliasing={{}: (3, {})} | custom-call | tf_op jit(solution)/shard_map/far/pallas_call | solution.py:416
  (21 shorter events, 0.3 us)
Async XLA Ops:
  9.1 55.7 %copy-start.1 = (s32[6]{0:T(128)S(1)}, s32[6]{0:T(128)}, u32[]{:S(2)}) copy-start(s32[6]{0:T(128)} %masks.5) | copy-start | bytes 76
  28.2 9.8 %collective-permute-start.7 = (bf16[16,16,384]{2,1,0:T(8,128)(2,1)S(1)}, bf16[16,16,384]{2,1,0:T(8,128)(2,1)S(1)}, u32[]{:S(2)}, u32[]{:S(2)}) collective-permute-start(bf16[16,16,384]{2,1,0:T(8,128)(2,1)S(1)} %get-tuple-element.46.refs_8_), channel_id=1, source_target_pairs={{0,14},{2,0},{4,2},{6,4},{8,6},{10,8},{12,10},{14,12},{1,15},{3,1}... | collective-permute-start | bytes 589832 | tf_op jit(solution)/shard_map/ppermute | solution.py:448
  33.9 7.6 %collective-permute-start.3 = (bf16[16,16,384]{2,1,0:T(8,128)(2,1)S(1)}, bf16[16,16,384]{2,1,0:T(8,128)(2,1)S(1)}, u32[]{:S(2)}, u32[]{:S(2)}) collective-permute-start(bf16[16,16,384]{2,1,0:T(8,128)(2,1)S(1)} %get-tuple-element.38.refs_0_), channel_id=1, source_target_pairs={{0,2},{2,4},{4,6},{6,8},{8,10},{10,12},{12,14},{14,0},{1,3},{3,5},... | collective-permute-start | bytes 589832 | tf_op jit(solution)/shard_map/ppermute | solution.py:448
  33.9 7.6 %collective-permute-start.14 = (bf16[1,8,32,384]{3,2,1,0:T(8,128)(2,1)}, bf16[1,8,32,384]{3,2,1,0:T(8,128)(2,1)S(1)}, u32[]{:S(2)}, u32[]{:S(2)}) collective-permute-start(bf16[1,8,32,384]{3,2,1,0:T(8,128)(2,1)} %get-tuple-element.37), channel_id=1, source_target_pairs={{0,128},{128,0},{1,129},{129,1},{2,130},{130,2},{3,131},{131,3},{4... | collective-permute-start | bytes 589832 | tf_op jit(solution)/shard_map/ppermute | solution.py:441
  34.2 11.1 %collective-permute-start.11 = (bf16[16,16,384]{2,1,0:T(8,128)(2,1)S(1)}, bf16[16,16,384]{2,1,0:T(8,128)(2,1)S(1)}, u32[]{:S(2)}, u32[]{:S(2)}) collective-permute-start(bf16[16,16,384]{2,1,0:T(8,128)(2,1)S(1)} %get-tuple-element.46.refs_8_), channel_id=1, source_target_pairs={{0,2},{2,4},{4,6},{6,8},{8,10},{10,12},{12,14},{14,0},{1,3},{3,5},... | collective-permute-start | bytes 589832 | tf_op jit(solution)/shard_map/ppermute | solution.py:448
  34.2 11.1 %collective-permute-start = (bf16[16,16,384]{2,1,0:T(8,128)(2,1)S(1)}, bf16[16,16,384]{2,1,0:T(8,128)(2,1)S(1)}, u32[]{:S(2)}, u32[]{:S(2)}) collective-permute-start(bf16[16,16,384]{2,1,0:T(8,128)(2,1)S(1)} %get-tuple-element.38.refs_0_), channel_id=1, source_target_pairs={{0,14},{2,0},{4,2},{6,4},{8,6},{10,8},{12,10},{14,12},{1,15},{3,1}... | collective-permute-start | bytes 589832 | tf_op jit(solution)/shard_map/ppermute | solution.py:448
  38.0 10.0 %collective-permute-start.8 = (bf16[16,16,384]{2,1,0:T(8,128)(2,1)S(1)}, bf16[16,16,384]{2,1,0:T(8,128)(2,1)S(1)}, u32[]{:S(2)}, u32[]{:S(2)}) collective-permute-start(bf16[16,16,384]{2,1,0:T(8,128)(2,1)S(1)} %collective-permute-done.7.refs_9_), channel_id=1, source_target_pairs={{0,14},{2,0},{4,2},{6,4},{8,6},{10,8},{12,10},{14,12},{1,15},{3,1}... | collective-permute-start | bytes 589832 | tf_op jit(solution)/shard_map/ppermute | solution.py:448
  41.4 7.8 %collective-permute-start.4 = (bf16[16,16,384]{2,1,0:T(8,128)(2,1)S(1)}, bf16[16,16,384]{2,1,0:T(8,128)(2,1)S(1)}, u32[]{:S(2)}, u32[]{:S(2)}) collective-permute-start(bf16[16,16,384]{2,1,0:T(8,128)(2,1)S(1)} %collective-permute-done.3.refs_7_), channel_id=1, source_target_pairs={{0,2},{2,4},{4,6},{6,8},{8,10},{10,12},{12,14},{14,0},{1,3},{3,5},... | collective-permute-start | bytes 589832 | tf_op jit(solution)/shard_map/ppermute | solution.py:448
  42.5 18.5 %collective-permute-start.15 = (bf16[2,8,32,384]{3,2,1,0:T(8,128)(2,1)S(1)}, bf16[2,8,32,384]{3,2,1,0:T(8,128)(2,1)}, u32[]{:S(2)}, u32[]{:S(2)}) collective-permute-start(bf16[2,8,32,384]{3,2,1,0:T(8,128)(2,1)S(1)} %maximum_select_fusion.own), channel_id=1, source_target_pairs={{0,1},{1,0},{2,3},{3,2},{4,5},{5,4},{6,7},{7,6},{8,9},{9,8},{10,11... | collective-permute-start | bytes 1179656 | tf_op jit(solution)/shard_map/ppermute | solution.py:441
  45.3 7.9 %collective-permute-start.12 = (bf16[16,16,384]{2,1,0:T(8,128)(2,1)S(1)}, bf16[16,16,384]{2,1,0:T(8,128)(2,1)S(1)}, u32[]{:S(2)}, u32[]{:S(2)}) collective-permute-start(bf16[16,16,384]{2,1,0:T(8,128)(2,1)S(1)} %collective-permute-done.11.refs_15_), channel_id=1, source_target_pairs={{0,2},{2,4},{4,6},{6,8},{8,10},{10,12},{12,14},{14,0},{1,3},{3,5},... | collective-permute-start | bytes 589832 | tf_op jit(solution)/shard_map/ppermute | solution.py:448
  45.3 7.9 %collective-permute-start.1 = (bf16[16,16,384]{2,1,0:T(8,128)(2,1)S(1)}, bf16[16,16,384]{2,1,0:T(8,128)(2,1)S(1)}, u32[]{:S(2)}, u32[]{:S(2)}) collective-permute-start(bf16[16,16,384]{2,1,0:T(8,128)(2,1)S(1)} %collective-permute-done.refs_1_), channel_id=1, source_target_pairs={{0,14},{2,0},{4,2},{6,4},{8,6},{10,8},{12,10},{14,12},{1,15},{3,1}... | collective-permute-start | bytes 589832 | tf_op jit(solution)/shard_map/ppermute | solution.py:448
  48.0 7.9 %collective-permute-start.9 = (bf16[16,16,384]{2,1,0:T(8,128)(2,1)S(1)}, bf16[16,16,384]{2,1,0:T(8,128)(2,1)S(1)}, u32[]{:S(2)}, u32[]{:S(2)}) collective-permute-start(bf16[16,16,384]{2,1,0:T(8,128)(2,1)S(1)} %collective-permute-done.8.refs_10_), channel_id=1, source_target_pairs={{0,14},{2,0},{4,2},{6,4},{8,6},{10,8},{12,10},{14,12},{1,15},{3,1}... | collective-permute-start | bytes 589832 | tf_op jit(solution)/shard_map/ppermute | solution.py:448
  49.2 8.3 %collective-permute-start.5 = (bf16[16,16,384]{2,1,0:T(8,128)(2,1)S(1)}, bf16[16,16,384]{2,1,0:T(8,128)(2,1)S(1)}, u32[]{:S(2)}, u32[]{:S(2)}) collective-permute-start(bf16[16,16,384]{2,1,0:T(8,128)(2,1)S(1)} %collective-permute-done.4.refs_6_), channel_id=1, source_target_pairs={{0,2},{2,4},{4,6},{6,8},{8,10},{10,12},{12,14},{14,0},{1,3},{3,5},... | collective-permute-start | bytes 589832 | tf_op jit(solution)/shard_map/ppermute | solution.py:448
  53.2 7.8 %collective-permute-start.13 = (bf16[16,16,384]{2,1,0:T(8,128)(2,1)S(1)}, bf16[16,16,384]{2,1,0:T(8,128)(2,1)S(1)}, u32[]{:S(2)}, u32[]{:S(2)}) collective-permute-start(bf16[16,16,384]{2,1,0:T(8,128)(2,1)S(1)} %collective-permute-done.12.refs_14_), channel_id=1, source_target_pairs={{0,2},{2,4},{4,6},{6,8},{8,10},{10,12},{12,14},{14,0},{1,3},{3,5},... | collective-permute-start | bytes 589832 | tf_op jit(solution)/shard_map/ppermute | solution.py:448
  53.2 7.8 %collective-permute-start.2 = (bf16[16,16,384]{2,1,0:T(8,128)(2,1)S(1)}, bf16[16,16,384]{2,1,0:T(8,128)(2,1)S(1)}, u32[]{:S(2)}, u32[]{:S(2)}) collective-permute-start(bf16[16,16,384]{2,1,0:T(8,128)(2,1)S(1)} %collective-permute-done.1.refs_2_), channel_id=1, source_target_pairs={{0,14},{2,0},{4,2},{6,4},{8,6},{10,8},{12,10},{14,12},{1,15},{3,1}... | collective-permute-start | bytes 589832 | tf_op jit(solution)/shard_map/ppermute | solution.py:448
  55.9 6.6 %collective-permute-start.10 = (bf16[16,16,384]{2,1,0:T(8,128)(2,1)S(1)}, bf16[16,16,384]{2,1,0:T(8,128)(2,1)S(1)}, u32[]{:S(2)}, u32[]{:S(2)}) collective-permute-start(bf16[16,16,384]{2,1,0:T(8,128)(2,1)S(1)} %collective-permute-done.9.refs_11_), channel_id=1, source_target_pairs={{0,14},{2,0},{4,2},{6,4},{8,6},{10,8},{12,10},{14,12},{1,15},{3,1}... | collective-permute-start | bytes 589832 | tf_op jit(solution)/shard_map/ppermute | solution.py:448
  57.5 7.4 %collective-permute-start.6 = (bf16[16,16,384]{2,1,0:T(8,128)(2,1)S(1)}, bf16[16,16,384]{2,1,0:T(8,128)(2,1)S(1)}, u32[]{:S(2)}, u32[]{:S(2)}) collective-permute-start(bf16[16,16,384]{2,1,0:T(8,128)(2,1)S(1)} %collective-permute-done.5.refs_5_), channel_id=1, source_target_pairs={{0,2},{2,4},{4,6},{6,8},{8,10},{10,12},{12,14},{14,0},{1,3},{3,5},... | collective-permute-start | bytes 589832 | tf_op jit(solution)/shard_map/ppermute | solution.py:448
  66.9 34.6 %all-to-all-start.1 = ((bf16[16,160,384]{2,1,0:T(8,128)(2,1)}), bf16[16,160,384]{2,1,0:T(8,128)(2,1)S(1)}, u32[]{:S(2)}, u32[]{:S(2)}) async-start(bf16[16,160,384]{2,1,0:T(8,128)(2,1)} %bitcast.4), calls=%async_computation.1 | async-start | bytes 3932160 | tf_op jit(solution)/shard_map/all_to_all | solution.py:476
  80.8 2.7 %copy-start = (bf16[2,3,8,256,256]{4,3,2,1,0:T(8,128)(2,1)}, bf16[2,3,8,256,256]{4,3,2,1,0:T(8,128)(2,1)S(1)}, u32[]{:S(2)}) copy-start(bf16[2,3,8,256,256]{4,3,2,1,0:T(8,128)(2,1)S(1)} %get-tuple-element.59.weights) | copy-start | bytes 18874372

commit v5 on v4

--- a/solution.py
+++ b/solution.py
@@ -1,3 +1,5 @@
+import math
+
 import jax
 import jax.numpy as jnp
 import numpy as np
@@ -205,12 +207,17 @@
     )(counts, section, taps.reshape(1, K), traces, tap_tables(), odd_table(), even_table())
 
 
-def near_round(masks):
-    return sum(jnp.where(masks[r] == 1, r, 0) for r in range(ROUNDS))
+FAR = ROUNDS - 2
+
+
+def round_of(masks, value):
+    return sum(jnp.where(masks[r] == value, r, 0) for r in range(ROUNDS))
 
 
 def far_round(masks, n):
-    return n + (n >= near_round(masks)).astype(jnp.int32)
+    near, across = round_of(masks, 1), round_of(masks, 127)
+    n = n + (n >= jnp.minimum(near, across)).astype(jnp.int32)
+    return n + (n >= jnp.maximum(near, across)).astype(jnp.int32)
 
 
 def pick_kernel(masks, z, *refs):
@@ -240,12 +247,12 @@
     half = (2, CAP // 2, HALF)
     return pl.pallas_call(
         pick_kernel,
-        out_shape=jax.ShapeDtypeStruct((16, ROUNDS - 1) + half, jnp.bfloat16),
+        out_shape=jax.ShapeDtypeStruct((16, FAR) + half, jnp.bfloat16),
         in_specs=[pl.BlockSpec(memory_space=pltpu.SMEM)] * 2 + [inside] * 16,
         out_specs=pl.BlockSpec(memory_space=pl.ANY),
         scratch_shapes=[
-            pltpu.VMEM((ROUNDS - 1, 16) + half, jnp.bfloat16),
-            pltpu.SemaphoreType.DMA((ROUNDS - 1,)),
+            pltpu.VMEM((FAR, 16) + half, jnp.bfloat16),
+            pltpu.SemaphoreType.DMA((FAR,)),
         ],
         compiler_params=pltpu.CompilerParams(vmem_limit_bytes=8 * 1024 * 1024),
         name="pick",
@@ -339,7 +346,7 @@
         for fg in range(GROUPS):
             multiply(left, held.at[it], sums, fg)
             finish(sums, done, 1, it, fg)
-    copies.append(pltpu.make_async_copy(done.at[0], out.at[near_round(masks)], sems.at[HALVES]))
+    copies.append(pltpu.make_async_copy(done.at[0], out.at[round_of(masks, 1)], sems.at[HALVES]))
     copies[-1].start()
     for copy in copies:
         copy.wait()
@@ -368,8 +375,8 @@
     )(masks, own, sibling)
 
 
-def far_kernel(masks, partner, weights, kept, out, left, held, sums, done, load_sems, store_sems):
-    rounds = ROUNDS - 1
+def far_kernel(masks, partner, across, weights, kept, out, left, held, sums, done, load_sems, store_sems):
+    rounds = FAR + 1
     loads = [
         [
             pltpu.make_async_copy(weights.at[it, fg], held.at[it, fg], load_sems.at[it * GROUPS + fg])
@@ -385,13 +392,13 @@
         arrange(left, rounds, r, lambda p, h, jh, lanes: partner[2 * p + jh, r, h, :, lanes])
         return carry
 
-    lax.fori_loop(0, rounds, arrange_one, 0)
+    arrange(left, rounds, FAR, lambda p, h, jh, lanes: across[h, p, jh * 16 : (jh + 1) * 16, lanes])
+    lax.fori_loop(0, FAR, arrange_one, 0)
 
     def store(it, r):
         part = pl.ds(it * 16, 16)
-        return pltpu.make_async_copy(
-            done.at[r, :, part], out.at[far_round(masks, r), :, part], store_sems.at[it * rounds + r]
-        )
+        at = far_round(masks, r) if r < FAR else round_of(masks, 127)
+        return pltpu.make_async_copy(done.at[r, :, part], out.at[at, :, part], store_sems.at[it * rounds + r])
 
     steps = [(it, fg) for it in range(HALVES) for fg in range(GROUPS)]
     for n, (it, fg) in enumerate(steps + [(HALVES, 0)]):
@@ -410,14 +417,15 @@
             store(it, r).wait()
 
 
-def far_of(masks, partner, weights, kept):
-    rounds = ROUNDS - 1
+def far_of(masks, partner, across, weights, kept):
+    rounds = FAR + 1
     rows = 2 * rounds * CAP
     return pl.pallas_call(
         far_kernel,
         out_shape=jax.ShapeDtypeStruct(kept.shape, kept.dtype),
         in_specs=[
             pl.BlockSpec(memory_space=pltpu.SMEM),
+            pl.BlockSpec(memory_space=pltpu.VMEM),
             pl.BlockSpec(memory_space=pltpu.VMEM),
             pl.BlockSpec(memory_space=pl.ANY),
             pl.BlockSpec(memory_space=pl.ANY),
@@ -431,14 +439,15 @@
             pltpu.SemaphoreType.DMA((HALVES * GROUPS,)),
             pltpu.SemaphoreType.DMA((HALVES * rounds,)),
         ],
-        input_output_aliases={3: 0},
+        input_output_aliases={4: 0},
         compiler_params=pltpu.CompilerParams(vmem_limit_bytes=VMEM),
         name="far",
-    )(masks, partner, weights, kept)
-
-
-def flipped(block, axis):
-    return lax.ppermute(block, axis, [(0, 1), (1, 0)])
+    )(masks, partner, across, weights, kept)
+
+
+def turned(block, axes, mask):
+    count = math.prod(lax.axis_size(axis) for axis in axes)
+    return lax.ppermute(block, axes, [(i, i ^ mask) for i in range(count)])
 
 
 def around(block, last):
@@ -466,16 +475,18 @@
     first, second = around(pieces[:16], 1), around(pieces[16:], -1)
 
     own, away, _ = lax.optimization_barrier((own, away, pieces))
-    other = flipped(away, "section")
+    other = turned(away, ("section",), 1)
     both = jnp.where(section == 0, jnp.concatenate([own, other]), jnp.concatenate([other, own]))
-    sibling = flipped(both, "core")
-
-    first, second, both, sibling = lax.optimization_barrier((first, second, both, sibling))
+    sibling = turned(both, ("core",), 1)
+    mirror = turned(both, ("yh", "x", "core"), 15)
+
+    first, second, both, sibling, mirror = lax.optimization_barrier((first, second, both, sibling, mirror))
     picked = pick(first, second, masks, z[None])
-    picked, both, sibling = lax.optimization_barrier((picked, both, sibling))
+    picked, both, sibling, mirror = lax.optimization_barrier((picked, both, sibling, mirror))
     partners = lax.all_to_all(picked.reshape(16, -1, HALF), ("yh", "x", "core"), 0, 0, tiled=True)
+    across = turned(mirror, ("z",), 7)
     result, weights = near_of(masks, both, sibling)
-    return far_of(masks, partners.reshape(picked.shape), weights, result)[None]
+    return far_of(masks, partners.reshape(picked.shape), across, weights, result)[None]
 
 
 def solution(mesh):

time: 109 us -> 108 us (level)
  starting transfers between devices: 29.8 us -> 28.7 us
    all_to_all x1, waiting for transfers between devices: 18 us -> 2.66 us  [shards(): lax.all_to_all(picked.reshape(16, -1, HALF), ('yh', 'x', 'core'), 0, 0, t...]
    ppermute x2 -> x4, waiting for transfers between devices: 0.01 us -> 10.9 us  [turned(): return lax.ppermute(block, axes, [(i, i ^ mask) for i in range(count)])]
    ppermute x14, waiting for transfers between devices: 13.1 us -> 17.5 us  [shift(): return lax.ppermute(held, 'z', [(i, (i + way) % ring) for i in range(ring)])]
    ppermute x14, starting transfers between devices: 20.2 us -> 17.8 us  [shift(): return lax.ppermute(held, 'z', [(i, (i + way) % ring) for i in range(ring)])]
    ppermute x2 -> x4, starting transfers between devices: 2.25 us -> 3.29 us  [turned(): return lax.ppermute(block, axes, [(i, i ^ mask) for i in range(count)])]
  transfers between devices with their start and end apart: 17 -> 19, of which waited for: 7 -> 10; matrix products, arithmetic and copies ran while one was open for 1% -> 1% of each run, Pallas kernels for 6% -> 6%
where the time goes in v5:
time: 108 us
  waiting for transfers between devices  31.1 us (29%)
  starting transfers between devices  28.7 us (27%)
  Pallas kernels  24.1 us (22%)
  blocking collectives  19 us (18%)
  local copies, waits for them, and re-layouts  2.7 us (2%)
  other arithmetic  1.09 us (1%)
    all_to_all x1, blocking collectives, shards(): lax.all_to_all(white.reshape(32, CAP // 2, HALF), ('section', 'yh', 'x',...  19 us
    ppermute x14, starting transfers between devices, shift(): return lax.ppermute(held, 'z', [(i, (i + way) % ring) for i in range(ring)])  17.8 us
    ppermute x14, waiting for transfers between devices, shift(): return lax.ppermute(held, 'z', [(i, (i + way) % ring) for i in range(ring)])  17.5 us
    ppermute x4, waiting for transfers between devices, turned(): return lax.ppermute(block, axes, [(i, i ^ mask) for i in range(count)])  10.9 us
    pallas_call x1, Pallas kernels, spectra_of(): pl.pallas_call(spectra_kernel, out_shape=[jax.ShapeDtypeStruct((n, 2 * se...  8.47 us
    all_to_all x1, starting transfers between devices, shards(): lax.all_to_all(picked.reshape(16, -1, HALF), ('yh', 'x', 'core'), 0, 0, t...  7.68 us
    pallas_call x1, Pallas kernels, far_of(): pl.pallas_call(far_kernel, out_shape=jax.ShapeDtypeStruct(kept.shape, kep...  7.3 us
    pallas_call x1, Pallas kernels, near_of(): pl.pallas_call(near_kernel, out_shape=[jax.ShapeDtypeStruct((ROUNDS, 2, C...  6.5 us
  transfers between devices with their start and end apart: 19, of which 10 were waited for; matrix products, arithmetic and copies ran while one was open for 1% of the time, Pallas kernels for 6%

profile of v5, /device:TPU:1, one launch (start us, length us, event | category | flops | bytes accessed | tf_op | source)
XLA Modules:
  0.0 107.7 jit_solution(11013950531389192713)
XLA Ops:
  0.7 8.5 %spectra.1 = (bf16[2,8,32,384]{3,2,1,0:T(8,128)(2,1)}, bf16[1,8,32,384]{3,2,1,0:T(8,128)(2,1)}, bf16[1,8,32,384]{3,2,1,0:T(8,128)(2,1)}) custom-call(s32[1]{0:T(128)S(6)} %copy.10.counts, s32[1]{0:T(128)} %bitcast.1.section, f32[1,64]{1,0:T(1,128)} %bitcast.9, bf16[4,32,6144]{2,1,0:T(8,128)(2,1)} %traces.1, f32[2,64,896]{2,1,0:T(8,128)} %constant.17.clone.tap_source, ...), custom_call_target="tpu_custom_call" | custom-call | tf_op jit(solution)/shard_map/spectra/pallas_call | solution.py:180
  9.1 19.0 %all_to_all.10 = bf16[32,16,384]{2,1,0:T(8,128)(2,1)S(1)} all-to-all(bf16[32,16,384]{2,1,0:T(8,128)(2,1)} %bitcast.8), channel_id=1, replica_groups=mesh['section'=2,'yh'=2,'x'=4,'z'=8,'core'=2] {'section','yh','x','core'}, dimensions={0} | all-to-all | bytes 786432 | tf_op jit(solution)/shard_map/all_to_all | solution.py:472
  28.2 1.7 %collective-permute-start.11 = (bf16[16,16,384]{2,1,0:T(8,128)(2,1)S(1)}, bf16[16,16,384]{2,1,0:T(8,128)(2,1)S(1)}, u32[]{:S(2)}, u32[]{:S(2)}) collective-permute-start(bf16[16,16,384]{2,1,0:T(8,128)(2,1)S(1)} %get-tuple-element.48.refs_8_), channel_id=1, source_target_pairs={{0,2},{2,4},{4,6},{6,8},{8,10},{10,12},{12,14},{14,0},{1,3},{3,5},... | collective-permute-start | bytes 589832 | tf_op jit(solution)/shard_map/ppermute | solution.py:457
  29.9 4.0 %collective-permute-start.7 = (bf16[16,16,384]{2,1,0:T(8,128)(2,1)S(1)}, bf16[16,16,384]{2,1,0:T(8,128)(2,1)S(1)}, u32[]{:S(2)}, u32[]{:S(2)}) collective-permute-start(bf16[16,16,384]{2,1,0:T(8,128)(2,1)S(1)} %get-tuple-element.48.refs_8_), channel_id=1, source_target_pairs={{0,14},{2,0},{4,2},{6,4},{8,6},{10,8},{12,10},{14,12},{1,15},{3,1}... | collective-permute-start | bytes 589832 | tf_op jit(solution)/shard_map/ppermute | solution.py:457
  33.9 2.7 %collective-permute-start = (bf16[16,16,384]{2,1,0:T(8,128)(2,1)S(1)}, bf16[16,16,384]{2,1,0:T(8,128)(2,1)S(1)}, u32[]{:S(2)}, u32[]{:S(2)}) collective-permute-start(bf16[16,16,384]{2,1,0:T(8,128)(2,1)S(1)} %get-tuple-element.40.refs_0_), channel_id=1, source_target_pairs={{0,14},{2,0},{4,2},{6,4},{8,6},{10,8},{12,10},{14,12},{1,15},{3,1}... | collective-permute-start | bytes 589832 | tf_op jit(solution)/shard_map/ppermute | solution.py:457
  37.0 2.0 %collective-permute-done.11.refs_15_ = bf16[16,16,384]{2,1,0:T(8,128)(2,1)S(1)} collective-permute-done((bf16[16,16,384]{2,1,0:T(8,128)(2,1)S(1)}, bf16[16,16,384]{2,1,0:T(8,128)(2,1)S(1)}, u32[]{:S(2)}, u32[]{:S(2)}) %collective-permute-start.11) | collective-permute-done | bytes 196640 | tf_op jit(solution)/shard_map/ppermute | solution.py:457
  39.0 2.7 %collective-permute-start.8 = (bf16[16,16,384]{2,1,0:T(8,128)(2,1)S(1)}, bf16[16,16,384]{2,1,0:T(8,128)(2,1)S(1)}, u32[]{:S(2)}, u32[]{:S(2)}) collective-permute-start(bf16[16,16,384]{2,1,0:T(8,128)(2,1)S(1)} %collective-permute-done.7.refs_9_), channel_id=1, source_target_pairs={{0,14},{2,0},{4,2},{6,4},{8,6},{10,8},{12,10},{14,12},{1,15},{3,1}... | collective-permute-start | bytes 589832 | tf_op jit(solution)/shard_map/ppermute | solution.py:457
  41.7 1.5 %collective-permute-done.3.refs_7_ = bf16[16,16,384]{2,1,0:T(8,128)(2,1)S(1)} collective-permute-done((bf16[16,16,384]{2,1,0:T(8,128)(2,1)S(1)}, bf16[16,16,384]{2,1,0:T(8,128)(2,1)S(1)}, u32[]{:S(2)}, u32[]{:S(2)}) %collective-permute-start.3) | collective-permute-done | bytes 196640 | tf_op jit(solution)/shard_map/ppermute | solution.py:457
  43.2 2.7 %collective-permute-start.1 = (bf16[16,16,384]{2,1,0:T(8,128)(2,1)S(1)}, bf16[16,16,384]{2,1,0:T(8,128)(2,1)S(1)}, u32[]{:S(2)}, u32[]{:S(2)}) collective-permute-start(bf16[16,16,384]{2,1,0:T(8,128)(2,1)S(1)} %collective-permute-done.refs_1_), channel_id=1, source_target_pairs={{0,14},{2,0},{4,2},{6,4},{8,6},{10,8},{12,10},{14,12},{1,15},{3,1}... | collective-permute-start | bytes 589832 | tf_op jit(solution)/shard_map/ppermute | solution.py:457
  47.0 2.7 %collective-permute-start.16 = (bf16[2,8,32,384]{3,2,1,0:T(8,128)(2,1)S(1)}, bf16[2,8,32,384]{3,2,1,0:T(8,128)(2,1)}, u32[]{:S(2)}, u32[]{:S(2)}) collective-permute-start(bf16[2,8,32,384]{3,2,1,0:T(8,128)(2,1)S(1)} %maximum_select_fusion.own), channel_id=1, source_target_pairs={{0,113},{1,112},{16,97},{17,96},{32,81},{33,80},{48,65},{49,64},{6... | collective-permute-start | bytes 1179656 | tf_op jit(solution)/shard_map/ppermute | solution.py:450
  49.8 1.2 %collective-permute-done.4.refs_6_ = bf16[16,16,384]{2,1,0:T(8,128)(2,1)S(1)} collective-permute-done((bf16[16,16,384]{2,1,0:T(8,128)(2,1)S(1)}, bf16[16,16,384]{2,1,0:T(8,128)(2,1)S(1)}, u32[]{:S(2)}, u32[]{:S(2)}) %collective-permute-start.4) | collective-permute-done | bytes 196640 | tf_op jit(solution)/shard_map/ppermute | solution.py:457
  51.0 1.8 %collective-permute-start.9 = (bf16[16,16,384]{2,1,0:T(8,128)(2,1)S(1)}, bf16[16,16,384]{2,1,0:T(8,128)(2,1)S(1)}, u32[]{:S(2)}, u32[]{:S(2)}) collective-permute-start(bf16[16,16,384]{2,1,0:T(8,128)(2,1)S(1)} %collective-permute-done.8.refs_10_), channel_id=1, source_target_pairs={{0,14},{2,0},{4,2},{6,4},{8,6},{10,8},{12,10},{14,12},{1,15},{3,1}... | collective-permute-start | bytes 589832 | tf_op jit(solution)/shard_map/ppermute | solution.py:457
  52.9 4.3 %collective-permute-done.13.refs_13_ = bf16[16,16,384]{2,1,0:T(8,128)(2,1)S(1)} collective-permute-done((bf16[16,16,384]{2,1,0:T(8,128)(2,1)S(1)}, bf16[16,16,384]{2,1,0:T(8,128)(2,1)S(1)}, u32[]{:S(2)}, u32[]{:S(2)}) %collective-permute-start.13) | collective-permute-done | bytes 196640 | tf_op jit(solution)/shard_map/ppermute | solution.py:457
  57.2 2.1 %collective-permute-start.10 = (bf16[16,16,384]{2,1,0:T(8,128)(2,1)S(1)}, bf16[16,16,384]{2,1,0:T(8,128)(2,1)S(1)}, u32[]{:S(2)}, u32[]{:S(2)}) collective-permute-start(bf16[16,16,384]{2,1,0:T(8,128)(2,1)S(1)} %collective-permute-done.9.refs_11_), channel_id=1, source_target_pairs={{0,14},{2,0},{4,2},{6,4},{8,6},{10,8},{12,10},{14,12},{1,15},{3,1}... | collective-permute-start | bytes 589832 | tf_op jit(solution)/shard_map/ppermute | solution.py:457
  59.3 2.0 %collective-permute-done.5.refs_5_ = bf16[16,16,384]{2,1,0:T(8,128)(2,1)S(1)} collective-permute-done((bf16[16,16,384]{2,1,0:T(8,128)(2,1)S(1)}, bf16[16,16,384]{2,1,0:T(8,128)(2,1)S(1)}, u32[]{:S(2)}, u32[]{:S(2)}) %collective-permute-start.5) | collective-permute-done | bytes 196640 | tf_op jit(solution)/shard_map/ppermute | solution.py:457
  62.1 3.7 %collective-permute-done.10.refs_12_ = bf16[16,16,384]{2,1,0:T(8,128)(2,1)S(1)} collective-permute-done((bf16[16,16,384]{2,1,0:T(8,128)(2,1)S(1)}, bf16[16,16,384]{2,1,0:T(8,128)(2,1)S(1)}, u32[]{:S(2)}, u32[]{:S(2)}) %collective-permute-start.10) | collective-permute-done | bytes 196640 | tf_op jit(solution)/shard_map/ppermute | solution.py:457
  65.8 1.9 %collective-permute-done.6.refs_4_ = bf16[16,16,384]{2,1,0:T(8,128)(2,1)S(1)} collective-permute-done((bf16[16,16,384]{2,1,0:T(8,128)(2,1)S(1)}, bf16[16,16,384]{2,1,0:T(8,128)(2,1)S(1)}, u32[]{:S(2)}, u32[]{:S(2)}) %collective-permute-start.6) | collective-permute-done | bytes 196640 | tf_op jit(solution)/shard_map/ppermute | solution.py:457
  67.7 1.9 %pick.1 = bf16[16,4,2,16,384]{4,3,2,1,0:T(8,128)(2,1)} custom-call(s32[6]{0:T(128)S(1)} %copy-done.1, s32[1]{0:T(128)} %bitcast.z, bf16[16,16,384]{2,1,0:T(8,128)(2,1)S(1)} %get-tuple-element.40.refs_0_, bf16[16,16,384]{2,1,0:T(8,128)(2,1)S(1)} %collective-permute-done.refs_1_, bf16[16,16,384]{2,1,0:T(8,128)(2,1)S(1)} %collective-permute-done.1.refs_2_, ...), custom_call_target="tpu_custom_call" | custom-call | tf_op jit(solution)/shard_map/pick/pallas_call | solution.py:248
  69.5 7.7 %all-to-all-start.1 = ((bf16[16,128,384]{2,1,0:T(8,128)(2,1)}), bf16[16,128,384]{2,1,0:T(8,128)(2,1)S(1)}, u32[]{:S(2)}, u32[]{:S(2)}) async-start(bf16[16,128,384]{2,1,0:T(8,128)(2,1)} %bitcast.4), calls=%async_computation.1 | async-start | bytes 3145728 | tf_op jit(solution)/shard_map/all_to_all | solution.py:486
  77.4 6.5 %near.1 = (bf16[6,2,32,32,384]{4,3,2,1,0:T(8,128)(2,1)}, bf16[2,3,8,256,256]{4,3,2,1,0:T(8,128)(2,1)S(1)}) custom-call(s32[6]{0:T(128)S(1)} %copy-done.1, bf16[2,8,32,384]{3,2,1,0:T(8,128)(2,1)S(1)} %maximum_select_fusion.own, bf16[2,8,32,384]{3,2,1,0:T(8,128)(2,1)} %collective-permute-done.15.sibling), custom_call_target="tpu_custom_call" | custom-call | flops 400000000 | bytes 9000000 | tf_op jit(solution)/shard_map/near/pallas_call | solution.py:357
  83.9 2.7 %copy-done = bf16[2,3,8,256,256]{4,3,2,1,0:T(8,128)(2,1)} copy-done((bf16[2,3,8,256,256]{4,3,2,1,0:T(8,128)(2,1)}, bf16[2,3,8,256,256]{4,3,2,1,0:T(8,128)(2,1)S(1)}, u32[]{:S(2)}) %copy-start) | copy-done | bytes 6291480
  86.6 10.9 %collective-permute-done.17.across = bf16[2,8,32,384]{3,2,1,0:T(8,128)(2,1)S(1)} collective-permute-done((bf16[2,8,32,384]{3,2,1,0:T(8,128)(2,1)}, bf16[2,8,32,384]{3,2,1,0:T(8,128)(2,1)S(1)}, u32[]{:S(2)}, u32[]{:S(2)}) %collective-permute-start.17) | collective-permute-done | bytes 393248 | tf_op jit(solution)/shard_map/ppermute | solution.py:450
  97.5 2.7 %all-to-all-done.1 = bf16[16,128,384]{2,1,0:T(8,128)(2,1)S(1)} async-done(((bf16[16,128,384]{2,1,0:T(8,128)(2,1)}), bf16[16,128,384]{2,1,0:T(8,128)(2,1)S(1)}, u32[]{:S(2)}, u32[]{:S(2)}) %all-to-all-start.1) | async-done | bytes 1572896 | tf_op jit(solution)/shard_map/all_to_all | solution.py:486
  100.2 7.3 %far.1 = bf16[6,2,32,32,384]{4,3,2,1,0:T(8,128)(2,1)} custom-call(s32[6]{0:T(128)S(1)} %copy-done.1, bf16[16,4,2,16,384]{4,3,2,1,0:T(8,128)(2,1)S(1)} %bitcast.7, bf16[2,8,32,384]{3,2,1,0:T(8,128)(2,1)S(1)} %collective-permute-done.17.across, bf16[2,3,8,256,256]{4,3,2,1,0:T(8,128)(2,1)} %copy-done, ...), custom_call_target="tpu_custom_call", output_to_operand_aliasing={{}: (4, {})} | custom-call | tf_op jit(solution)/shard_map/far/pallas_call | solution.py:423
  (25 shorter events, 2.6 us)
Async XLA Ops:
  9.1 58.5 %copy-start.1 = (s32[6]{0:T(128)S(1)}, s32[6]{0:T(128)}, u32[]{:S(2)}) copy-start(s32[6]{0:T(128)} %masks.5) | copy-start | bytes 76
  28.2 10.8 %collective-permute-start.11 = (bf16[16,16,384]{2,1,0:T(8,128)(2,1)S(1)}, bf16[16,16,384]{2,1,0:T(8,128)(2,1)S(1)}, u32[]{:S(2)}, u32[]{:S(2)}) collective-permute-start(bf16[16,16,384]{2,1,0:T(8,128)(2,1)S(1)} %get-tuple-element.48.refs_8_), channel_id=1, source_target_pairs={{0,2},{2,4},{4,6},{6,8},{8,10},{10,12},{12,14},{14,0},{1,3},{3,5},... | collective-permute-start | bytes 589832 | tf_op jit(solution)/shard_map/ppermute | solution.py:457
  29.9 9.1 %collective-permute-start.7 = (bf16[16,16,384]{2,1,0:T(8,128)(2,1)S(1)}, bf16[16,16,384]{2,1,0:T(8,128)(2,1)S(1)}, u32[]{:S(2)}, u32[]{:S(2)}) collective-permute-start(bf16[16,16,384]{2,1,0:T(8,128)(2,1)S(1)} %get-tuple-element.48.refs_8_), channel_id=1, source_target_pairs={{0,14},{2,0},{4,2},{6,4},{8,6},{10,8},{12,10},{14,12},{1,15},{3,1}... | collective-permute-start | bytes 589832 | tf_op jit(solution)/shard_map/ppermute | solution.py:457
  33.9 9.3 %collective-permute-start.3 = (bf16[16,16,384]{2,1,0:T(8,128)(2,1)S(1)}, bf16[16,16,384]{2,1,0:T(8,128)(2,1)S(1)}, u32[]{:S(2)}, u32[]{:S(2)}) collective-permute-start(bf16[16,16,384]{2,1,0:T(8,128)(2,1)S(1)} %get-tuple-element.40.refs_0_), channel_id=1, source_target_pairs={{0,2},{2,4},{4,6},{6,8},{8,10},{10,12},{12,14},{14,0},{1,3},{3,5},... | collective-permute-start | bytes 589832 | tf_op jit(solution)/shard_map/ppermute | solution.py:457
  33.9 9.3 %collective-permute-start = (bf16[16,16,384]{2,1,0:T(8,128)(2,1)S(1)}, bf16[16,16,384]{2,1,0:T(8,128)(2,1)S(1)}, u32[]{:S(2)}, u32[]{:S(2)}) collective-permute-start(bf16[16,16,384]{2,1,0:T(8,128)(2,1)S(1)} %get-tuple-element.40.refs_0_), channel_id=1, source_target_pairs={{0,14},{2,0},{4,2},{6,4},{8,6},{10,8},{12,10},{14,12},{1,15},{3,1}... | collective-permute-start | bytes 589832 | tf_op jit(solution)/shard_map/ppermute | solution.py:457
  36.6 9.3 %collective-permute-start.14 = (bf16[1,8,32,384]{3,2,1,0:T(8,128)(2,1)}, bf16[1,8,32,384]{3,2,1,0:T(8,128)(2,1)S(1)}, u32[]{:S(2)}, u32[]{:S(2)}) collective-permute-start(bf16[1,8,32,384]{3,2,1,0:T(8,128)(2,1)} %get-tuple-element.39), channel_id=1, source_target_pairs={{0,128},{128,0},{1,129},{129,1},{2,130},{130,2},{3,131},{131,3},{4... | collective-permute-start | bytes 589832 | tf_op jit(solution)/shard_map/ppermute | solution.py:450
  39.0 10.7 %collective-permute-start.12 = (bf16[16,16,384]{2,1,0:T(8,128)(2,1)S(1)}, bf16[16,16,384]{2,1,0:T(8,128)(2,1)S(1)}, u32[]{:S(2)}, u32[]{:S(2)}) collective-permute-start(bf16[16,16,384]{2,1,0:T(8,128)(2,1)S(1)} %collective-permute-done.11.refs_15_), channel_id=1, source_target_pairs={{0,2},{2,4},{4,6},{6,8},{8,10},{10,12},{12,14},{14,0},{1,3},{3,5},... | collective-permute-start | bytes 589832 | tf_op jit(solution)/shard_map/ppermute | solution.py:457
  39.0 10.7 %collective-permute-start.8 = (bf16[16,16,384]{2,1,0:T(8,128)(2,1)S(1)}, bf16[16,16,384]{2,1,0:T(8,128)(2,1)S(1)}, u32[]{:S(2)}, u32[]{:S(2)}) collective-permute-start(bf16[16,16,384]{2,1,0:T(8,128)(2,1)S(1)} %collective-permute-done.7.refs_9_), channel_id=1, source_target_pairs={{0,14},{2,0},{4,2},{6,4},{8,6},{10,8},{12,10},{14,12},{1,15},{3,1}... | collective-permute-start | bytes 589832 | tf_op jit(solution)/shard_map/ppermute | solution.py:457
  43.2 7.8 %collective-permute-start.4 = (bf16[16,16,384]{2,1,0:T(8,128)(2,1)S(1)}, bf16[16,16,384]{2,1,0:T(8,128)(2,1)S(1)}, u32[]{:S(2)}, u32[]{:S(2)}) collective-permute-start(bf16[16,16,384]{2,1,0:T(8,128)(2,1)S(1)} %collective-permute-done.3.refs_7_), channel_id=1, source_target_pairs={{0,2},{2,4},{4,6},{6,8},{8,10},{10,12},{12,14},{14,0},{1,3},{3,5},... | collective-permute-start | bytes 589832 | tf_op jit(solution)/shard_map/ppermute | solution.py:457
  43.2 9.6 %collective-permute-start.1 = (bf16[16,16,384]{2,1,0:T(8,128)(2,1)S(1)}, bf16[16,16,384]{2,1,0:T(8,128)(2,1)S(1)}, u32[]{:S(2)}, u32[]{:S(2)}) collective-permute-start(bf16[16,16,384]{2,1,0:T(8,128)(2,1)S(1)} %collective-permute-done.refs_1_), channel_id=1, source_target_pairs={{0,14},{2,0},{4,2},{6,4},{8,6},{10,8},{12,10},{14,12},{1,15},{3,1}... | collective-permute-start | bytes 589832 | tf_op jit(solution)/shard_map/ppermute | solution.py:457
  47.0 15.1 %collective-permute-start.16 = (bf16[2,8,32,384]{3,2,1,0:T(8,128)(2,1)S(1)}, bf16[2,8,32,384]{3,2,1,0:T(8,128)(2,1)}, u32[]{:S(2)}, u32[]{:S(2)}) collective-permute-start(bf16[2,8,32,384]{3,2,1,0:T(8,128)(2,1)S(1)} %maximum_select_fusion.own), channel_id=1, source_target_pairs={{0,113},{1,112},{16,97},{17,96},{32,81},{33,80},{48,65},{49,64},{6... | collective-permute-start | bytes 1179656 | tf_op jit(solution)/shard_map/ppermute | solution.py:450
  49.7 12.4 %collective-permute-start.15 = (bf16[2,8,32,384]{3,2,1,0:T(8,128)(2,1)S(1)}, bf16[2,8,32,384]{3,2,1,0:T(8,128)(2,1)}, u32[]{:S(2)}, u32[]{:S(2)}) collective-permute-start(bf16[2,8,32,384]{3,2,1,0:T(8,128)(2,1)S(1)} %maximum_select_fusion.own), channel_id=1, source_target_pairs={{0,1},{1,0},{2,3},{3,2},{4,5},{5,4},{6,7},{7,6},{8,9},{9,8},{10,11... | collective-permute-start | bytes 1179656 | tf_op jit(solution)/shard_map/ppermute | solution.py:450
  49.7 7.4 %collective-permute-start.13 = (bf16[16,16,384]{2,1,0:T(8,128)(2,1)S(1)}, bf16[16,16,384]{2,1,0:T(8,128)(2,1)S(1)}, u32[]{:S(2)}, u32[]{:S(2)}) collective-permute-start(bf16[16,16,384]{2,1,0:T(8,128)(2,1)S(1)} %collective-permute-done.12.refs_14_), channel_id=1, source_target_pairs={{0,2},{2,4},{4,6},{6,8},{8,10},{10,12},{12,14},{14,0},{1,3},{3,5},... | collective-permute-start | bytes 589832 | tf_op jit(solution)/shard_map/ppermute | solution.py:457
  51.0 6.2 %collective-permute-start.9 = (bf16[16,16,384]{2,1,0:T(8,128)(2,1)S(1)}, bf16[16,16,384]{2,1,0:T(8,128)(2,1)S(1)}, u32[]{:S(2)}, u32[]{:S(2)}) collective-permute-start(bf16[16,16,384]{2,1,0:T(8,128)(2,1)S(1)} %collective-permute-done.8.refs_10_), channel_id=1, source_target_pairs={{0,14},{2,0},{4,2},{6,4},{8,6},{10,8},{12,10},{14,12},{1,15},{3,1}... | collective-permute-start | bytes 589832 | tf_op jit(solution)/shard_map/ppermute | solution.py:457
  52.9 8.4 %collective-permute-start.5 = (bf16[16,16,384]{2,1,0:T(8,128)(2,1)S(1)}, bf16[16,16,384]{2,1,0:T(8,128)(2,1)S(1)}, u32[]{:S(2)}, u32[]{:S(2)}) collective-permute-start(bf16[16,16,384]{2,1,0:T(8,128)(2,1)S(1)} %collective-permute-done.4.refs_6_), channel_id=1, source_target_pairs={{0,2},{2,4},{4,6},{6,8},{8,10},{10,12},{12,14},{14,0},{1,3},{3,5},... | collective-permute-start | bytes 589832 | tf_op jit(solution)/shard_map/ppermute | solution.py:457
  57.2 4.9 %collective-permute-start.2 = (bf16[16,16,384]{2,1,0:T(8,128)(2,1)S(1)}, bf16[16,16,384]{2,1,0:T(8,128)(2,1)S(1)}, u32[]{:S(2)}, u32[]{:S(2)}) collective-permute-start(bf16[16,16,384]{2,1,0:T(8,128)(2,1)S(1)} %collective-permute-done.1.refs_2_), channel_id=1, source_target_pairs={{0,14},{2,0},{4,2},{6,4},{8,6},{10,8},{12,10},{14,12},{1,15},{3,1}... | collective-permute-start | bytes 589832 | tf_op jit(solution)/shard_map/ppermute | solution.py:457
  57.2 8.6 %collective-permute-start.10 = (bf16[16,16,384]{2,1,0:T(8,128)(2,1)S(1)}, bf16[16,16,384]{2,1,0:T(8,128)(2,1)S(1)}, u32[]{:S(2)}, u32[]{:S(2)}) collective-permute-start(bf16[16,16,384]{2,1,0:T(8,128)(2,1)S(1)} %collective-permute-done.9.refs_11_), channel_id=1, source_target_pairs={{0,14},{2,0},{4,2},{6,4},{8,6},{10,8},{12,10},{14,12},{1,15},{3,1}... | collective-permute-start | bytes 589832 | tf_op jit(solution)/shard_map/ppermute | solution.py:457
  61.3 6.3 %collective-permute-start.6 = (bf16[16,16,384]{2,1,0:T(8,128)(2,1)S(1)}, bf16[16,16,384]{2,1,0:T(8,128)(2,1)S(1)}, u32[]{:S(2)}, u32[]{:S(2)}) collective-permute-start(bf16[16,16,384]{2,1,0:T(8,128)(2,1)S(1)} %collective-permute-done.5.refs_5_), channel_id=1, source_target_pairs={{0,2},{2,4},{4,6},{6,8},{8,10},{10,12},{12,14},{14,0},{1,3},{3,5},... | collective-permute-start | bytes 589832 | tf_op jit(solution)/shard_map/ppermute | solution.py:457
  69.5 30.7 %all-to-all-start.1 = ((bf16[16,128,384]{2,1,0:T(8,128)(2,1)}), bf16[16,128,384]{2,1,0:T(8,128)(2,1)S(1)}, u32[]{:S(2)}, u32[]{:S(2)}) async-start(bf16[16,128,384]{2,1,0:T(8,128)(2,1)} %bitcast.4), calls=%async_computation.1 | async-start | bytes 3145728 | tf_op jit(solution)/shard_map/all_to_all | solution.py:486
  77.2 20.3 %collective-permute-start.17 = (bf16[2,8,32,384]{3,2,1,0:T(8,128)(2,1)}, bf16[2,8,32,384]{3,2,1,0:T(8,128)(2,1)S(1)}, u32[]{:S(2)}, u32[]{:S(2)}) collective-permute-start(bf16[2,8,32,384]{3,2,1,0:T(8,128)(2,1)} %collective-permute-done.16), channel_id=1, source_target_pairs={{0,14},{2,12},{4,10},{6,8},{8,6},{10,4},{12,2},{14,0},{1,15},{3,13... | collective-permute-start | bytes 1179656 | tf_op jit(solution)/shard_map/ppermute | solution.py:450
  83.9 2.7 %copy-start = (bf16[2,3,8,256,256]{4,3,2,1,0:T(8,128)(2,1)}, bf16[2,3,8,256,256]{4,3,2,1,0:T(8,128)(2,1)S(1)}, u32[]{:S(2)}) copy-start(bf16[2,3,8,256,256]{4,3,2,1,0:T(8,128)(2,1)S(1)} %get-tuple-element.63.weights) | copy-start | bytes 18874372

commit v6 on v5

--- a/solution.py
+++ b/solution.py
@@ -316,7 +316,7 @@
         sums[fg, g] = jnp.dot(left[fg, g], weights[fg, g], preferred_element_type=jnp.float32).astype(jnp.bfloat16)
 
 
-def finish(sums, done, rounds, it, fg):
+def finish(sums, done, rounds, it, fg, after=None):
     bits = place_bits((16, 128), jnp.int16)
     for r in range(rounds):
         for a in range(2):
@@ -329,6 +329,8 @@
                         done[r, a, it * 16 + tile * 8 + i, jh * 16 : (jh + 1) * 16, fg * 128 : (fg + 1) * 128] = (
                             pltpu.roll(turned[i], -16 * i % 128, 1)
                         )
+        if after is not None:
+            after(r)
 
 
 def near_kernel(masks, own, sibling, out, weights, left, held, sums, done, sems):
@@ -407,10 +409,8 @@
             multiply(left, held.at[it], sums, fg)
         if n > 0:
             last_it, last_fg = steps[n - 1]
-            finish(sums, done, rounds, last_it, last_fg)
-            if last_fg == GROUPS - 1:
-                for r in range(rounds):
-                    store(last_it, r).start()
+            leave = (lambda r, it=last_it: store(it, r).start()) if last_fg == GROUPS - 1 else None
+            finish(sums, done, rounds, last_it, last_fg, leave)
 
     for it in range(HALVES):
         for r in range(rounds):
@@ -450,17 +450,20 @@
     return lax.ppermute(block, axes, [(i, i ^ mask) for i in range(count)])
 
 
-def around(block, last):
+def around(chunks):
     ring = lax.axis_size("z")
 
     def shift(held, way):
         return lax.ppermute(held, "z", [(i, (i + way) % ring) for i in range(ring)])
 
-    slabs = [block] * ring
+    slabs = [[chunk] * ring for chunk in chunks]
     for step in range(1, ring // 2):
-        slabs[-step] = shift(slabs[1 - step], 1)
-        slabs[step] = shift(slabs[step - 1], -1)
-    slabs[ring // 2] = shift(slabs[(ring // 2 + last) % ring], last)
+        for held in slabs:
+            held[-step] = shift(held[1 - step], 1)
+            held[step] = shift(held[step - 1], -1)
+    for n, held in enumerate(slabs):
+        way = 1 - 2 * (n % 2)
+        held[ring // 2] = shift(held[(ring // 2 + way) % ring], way)
     return slabs
 
 
@@ -472,7 +475,7 @@
     pieces = lax.all_to_all(
         white.reshape(32, CAP // 2, HALF), ("section", "yh", "x", "core"), 0, 0, tiled=True
     )
-    first, second = around(pieces[:16], 1), around(pieces[16:], -1)
+    first, second = around((pieces[:16], pieces[16:]))
 
     own, away, _ = lax.optimization_barrier((own, away, pieces))
     other = turned(away, ("section",), 1)

time: 108 us -> 108 us (level)
  no operation moved by 1% of the time
where the time goes in v6:
time: 108 us; the launch traced here: 107 us
  waiting for transfers between devices  31.1 us (29%)
  starting transfers between devices  28.7 us (27%)
  Pallas kernels  23.9 us (22%)
  blocking collectives  19 us (18%)
  local copies, waits for them, and re-layouts  2.7 us (2%)
  other arithmetic  1.09 us (1%)
    all_to_all x1, blocking collectives, shards(): lax.all_to_all(white.reshape(32, CAP // 2, HALF), ('section', 'yh', 'x',...  19 us
    ppermute x14, starting transfers between devices, shift(): return lax.ppermute(held, 'z', [(i, (i + way) % ring) for i in range(ring)])  17.8 us
    ppermute x14, waiting for transfers between devices, shift(): return lax.ppermute(held, 'z', [(i, (i + way) % ring) for i in range(ring)])  17.5 us
    ppermute x4, waiting for transfers between devices, turned(): return lax.ppermute(block, axes, [(i, i ^ mask) for i in range(count)])  10.9 us
    pallas_call x1, Pallas kernels, spectra_of(): pl.pallas_call(spectra_kernel, out_shape=[jax.ShapeDtypeStruct((n, 2 * se...  8.47 us
    all_to_all x1, starting transfers between devices, shards(): lax.all_to_all(picked.reshape(16, -1, HALF), ('yh', 'x', 'core'), 0, 0, t...  7.68 us
    pallas_call x1, Pallas kernels, far_of(): pl.pallas_call(far_kernel, out_shape=jax.ShapeDtypeStruct(kept.shape, kep...  7.12 us
    pallas_call x1, Pallas kernels, near_of(): pl.pallas_call(near_kernel, out_shape=[jax.ShapeDtypeStruct((ROUNDS, 2, C...  6.5 us
  transfers between devices with their start and end apart: 19, of which 10 were waited for; matrix products, arithmetic and copies ran while one was open for 1% of the time, Pallas kernels for 6%

profile of v6, /device:TPU:1, one launch (start us, length us, event | category | flops | bytes accessed | tf_op | source)
XLA Modules:
  0.0 107.5 jit_solution(1361033574633837498)
XLA Ops:
  0.7 8.5 %spectra.1 = (bf16[2,8,32,384]{3,2,1,0:T(8,128)(2,1)}, bf16[1,8,32,384]{3,2,1,0:T(8,128)(2,1)}, bf16[1,8,32,384]{3,2,1,0:T(8,128)(2,1)}) custom-call(s32[1]{0:T(128)S(6)} %copy.10.counts, s32[1]{0:T(128)} %bitcast.1.section, f32[1,64]{1,0:T(1,128)} %bitcast.9, bf16[4,32,6144]{2,1,0:T(8,128)(2,1)} %traces.1, f32[2,64,896]{2,1,0:T(8,128)} %constant.17.clone.tap_source, ...), custom_call_target="tpu_custom_call" | custom-call | tf_op jit(solution)/shard_map/spectra/pallas_call | solution.py:180
  9.1 19.0 %all_to_all.10 = bf16[32,16,384]{2,1,0:T(8,128)(2,1)S(1)} all-to-all(bf16[32,16,384]{2,1,0:T(8,128)(2,1)} %bitcast.8), channel_id=1, replica_groups=mesh['section'=2,'yh'=2,'x'=4,'z'=8,'core'=2] {'section','yh','x','core'}, dimensions={0} | all-to-all | bytes 786432 | tf_op jit(solution)/shard_map/all_to_all | solution.py:475
  28.2 1.7 %collective-permute-start.11 = (bf16[16,16,384]{2,1,0:T(8,128)(2,1)S(1)}, bf16[16,16,384]{2,1,0:T(8,128)(2,1)S(1)}, u32[]{:S(2)}, u32[]{:S(2)}) collective-permute-start(bf16[16,16,384]{2,1,0:T(8,128)(2,1)S(1)} %get-tuple-element.48.refs_8_), channel_id=1, source_target_pairs={{0,2},{2,4},{4,6},{6,8},{8,10},{10,12},{12,14},{14,0},{1,3},{3,5},... | collective-permute-start | bytes 589832 | tf_op jit(solution)/shard_map/ppermute | solution.py:457
  29.9 4.0 %collective-permute-start.7 = (bf16[16,16,384]{2,1,0:T(8,128)(2,1)S(1)}, bf16[16,16,384]{2,1,0:T(8,128)(2,1)S(1)}, u32[]{:S(2)}, u32[]{:S(2)}) collective-permute-start(bf16[16,16,384]{2,1,0:T(8,128)(2,1)S(1)} %get-tuple-element.48.refs_8_), channel_id=1, source_target_pairs={{0,14},{2,0},{4,2},{6,4},{8,6},{10,8},{12,10},{14,12},{1,15},{3,1}... | collective-permute-start | bytes 589832 | tf_op jit(solution)/shard_map/ppermute | solution.py:457
  33.9 2.7 %collective-permute-start = (bf16[16,16,384]{2,1,0:T(8,128)(2,1)S(1)}, bf16[16,16,384]{2,1,0:T(8,128)(2,1)S(1)}, u32[]{:S(2)}, u32[]{:S(2)}) collective-permute-start(bf16[16,16,384]{2,1,0:T(8,128)(2,1)S(1)} %get-tuple-element.40.refs_0_), channel_id=1, source_target_pairs={{0,14},{2,0},{4,2},{6,4},{8,6},{10,8},{12,10},{14,12},{1,15},{3,1}... | collective-permute-start | bytes 589832 | tf_op jit(solution)/shard_map/ppermute | solution.py:457
  37.0 2.0 %collective-permute-done.11.refs_15_ = bf16[16,16,384]{2,1,0:T(8,128)(2,1)S(1)} collective-permute-done((bf16[16,16,384]{2,1,0:T(8,128)(2,1)S(1)}, bf16[16,16,384]{2,1,0:T(8,128)(2,1)S(1)}, u32[]{:S(2)}, u32[]{:S(2)}) %collective-permute-start.11) | collective-permute-done | bytes 196640 | tf_op jit(solution)/shard_map/ppermute | solution.py:457
  39.0 2.7 %collective-permute-start.8 = (bf16[16,16,384]{2,1,0:T(8,128)(2,1)S(1)}, bf16[16,16,384]{2,1,0:T(8,128)(2,1)S(1)}, u32[]{:S(2)}, u32[]{:S(2)}) collective-permute-start(bf16[16,16,384]{2,1,0:T(8,128)(2,1)S(1)} %collective-permute-done.7.refs_9_), channel_id=1, source_target_pairs={{0,14},{2,0},{4,2},{6,4},{8,6},{10,8},{12,10},{14,12},{1,15},{3,1}... | collective-permute-start | bytes 589832 | tf_op jit(solution)/shard_map/ppermute | solution.py:457
  41.7 1.5 %collective-permute-done.3.refs_7_ = bf16[16,16,384]{2,1,0:T(8,128)(2,1)S(1)} collective-permute-done((bf16[16,16,384]{2,1,0:T(8,128)(2,1)S(1)}, bf16[16,16,384]{2,1,0:T(8,128)(2,1)S(1)}, u32[]{:S(2)}, u32[]{:S(2)}) %collective-permute-start.3) | collective-permute-done | bytes 196640 | tf_op jit(solution)/shard_map/ppermute | solution.py:457
  43.2 2.7 %collective-permute-start.1 = (bf16[16,16,384]{2,1,0:T(8,128)(2,1)S(1)}, bf16[16,16,384]{2,1,0:T(8,128)(2,1)S(1)}, u32[]{:S(2)}, u32[]{:S(2)}) collective-permute-start(bf16[16,16,384]{2,1,0:T(8,128)(2,1)S(1)} %collective-permute-done.refs_1_), channel_id=1, source_target_pairs={{0,14},{2,0},{4,2},{6,4},{8,6},{10,8},{12,10},{14,12},{1,15},{3,1}... | collective-permute-start | bytes 589832 | tf_op jit(solution)/shard_map/ppermute | solution.py:457
  47.0 2.7 %collective-permute-start.16 = (bf16[2,8,32,384]{3,2,1,0:T(8,128)(2,1)S(1)}, bf16[2,8,32,384]{3,2,1,0:T(8,128)(2,1)}, u32[]{:S(2)}, u32[]{:S(2)}) collective-permute-start(bf16[2,8,32,384]{3,2,1,0:T(8,128)(2,1)S(1)} %maximum_select_fusion.own), channel_id=1, source_target_pairs={{0,113},{1,112},{16,97},{17,96},{32,81},{33,80},{48,65},{49,64},{6... | collective-permute-start | bytes 1179656 | tf_op jit(solution)/shard_map/ppermute | solution.py:450
  49.8 1.2 %collective-permute-done.4.refs_6_ = bf16[16,16,384]{2,1,0:T(8,128)(2,1)S(1)} collective-permute-done((bf16[16,16,384]{2,1,0:T(8,128)(2,1)S(1)}, bf16[16,16,384]{2,1,0:T(8,128)(2,1)S(1)}, u32[]{:S(2)}, u32[]{:S(2)}) %collective-permute-start.4) | collective-permute-done | bytes 196640 | tf_op jit(solution)/shard_map/ppermute | solution.py:457
  51.0 1.8 %collective-permute-start.9 = (bf16[16,16,384]{2,1,0:T(8,128)(2,1)S(1)}, bf16[16,16,384]{2,1,0:T(8,128)(2,1)S(1)}, u32[]{:S(2)}, u32[]{:S(2)}) collective-permute-start(bf16[16,16,384]{2,1,0:T(8,128)(2,1)S(1)} %collective-permute-done.8.refs_10_), channel_id=1, source_target_pairs={{0,14},{2,0},{4,2},{6,4},{8,6},{10,8},{12,10},{14,12},{1,15},{3,1}... | collective-permute-start | bytes 589832 | tf_op jit(solution)/shard_map/ppermute | solution.py:457
  52.9 4.3 %collective-permute-done.13.refs_13_ = bf16[16,16,384]{2,1,0:T(8,128)(2,1)S(1)} collective-permute-done((bf16[16,16,384]{2,1,0:T(8,128)(2,1)S(1)}, bf16[16,16,384]{2,1,0:T(8,128)(2,1)S(1)}, u32[]{:S(2)}, u32[]{:S(2)}) %collective-permute-start.13) | collective-permute-done | bytes 196640 | tf_op jit(solution)/shard_map/ppermute | solution.py:457
  57.2 2.1 %collective-permute-start.10 = (bf16[16,16,384]{2,1,0:T(8,128)(2,1)S(1)}, bf16[16,16,384]{2,1,0:T(8,128)(2,1)S(1)}, u32[]{:S(2)}, u32[]{:S(2)}) collective-permute-start(bf16[16,16,384]{2,1,0:T(8,128)(2,1)S(1)} %collective-permute-done.9.refs_11_), channel_id=1, source_target_pairs={{0,14},{2,0},{4,2},{6,4},{8,6},{10,8},{12,10},{14,12},{1,15},{3,1}... | collective-permute-start | bytes 589832 | tf_op jit(solution)/shard_map/ppermute | solution.py:457
  59.3 2.0 %collective-permute-done.5.refs_5_ = bf16[16,16,384]{2,1,0:T(8,128)(2,1)S(1)} collective-permute-done((bf16[16,16,384]{2,1,0:T(8,128)(2,1)S(1)}, bf16[16,16,384]{2,1,0:T(8,128)(2,1)S(1)}, u32[]{:S(2)}, u32[]{:S(2)}) %collective-permute-start.5) | collective-permute-done | bytes 196640 | tf_op jit(solution)/shard_map/ppermute | solution.py:457
  62.1 3.7 %collective-permute-done.10.refs_12_ = bf16[16,16,384]{2,1,0:T(8,128)(2,1)S(1)} collective-permute-done((bf16[16,16,384]{2,1,0:T(8,128)(2,1)S(1)}, bf16[16,16,384]{2,1,0:T(8,128)(2,1)S(1)}, u32[]{:S(2)}, u32[]{:S(2)}) %collective-permute-start.10) | collective-permute-done | bytes 196640 | tf_op jit(solution)/shard_map/ppermute | solution.py:457
  65.8 1.9 %collective-permute-done.6.refs_4_ = bf16[16,16,384]{2,1,0:T(8,128)(2,1)S(1)} collective-permute-done((bf16[16,16,384]{2,1,0:T(8,128)(2,1)S(1)}, bf16[16,16,384]{2,1,0:T(8,128)(2,1)S(1)}, u32[]{:S(2)}, u32[]{:S(2)}) %collective-permute-start.6) | collective-permute-done | bytes 196640 | tf_op jit(solution)/shard_map/ppermute | solution.py:457
  67.7 1.9 %pick.1 = bf16[16,4,2,16,384]{4,3,2,1,0:T(8,128)(2,1)} custom-call(s32[6]{0:T(128)S(1)} %copy-done.1, s32[1]{0:T(128)} %bitcast.z, bf16[16,16,384]{2,1,0:T(8,128)(2,1)S(1)} %get-tuple-element.40.refs_0_, bf16[16,16,384]{2,1,0:T(8,128)(2,1)S(1)} %collective-permute-done.refs_1_, bf16[16,16,384]{2,1,0:T(8,128)(2,1)S(1)} %collective-permute-done.1.refs_2_, ...), custom_call_target="tpu_custom_call" | custom-call | tf_op jit(solution)/shard_map/pick/pallas_call | solution.py:248
  69.5 7.7 %all-to-all-start.1 = ((bf16[16,128,384]{2,1,0:T(8,128)(2,1)}), bf16[16,128,384]{2,1,0:T(8,128)(2,1)S(1)}, u32[]{:S(2)}, u32[]{:S(2)}) async-start(bf16[16,128,384]{2,1,0:T(8,128)(2,1)} %bitcast.4), calls=%async_computation.1 | async-start | bytes 3145728 | tf_op jit(solution)/shard_map/all_to_all | solution.py:489
  77.4 6.5 %near.1 = (bf16[6,2,32,32,384]{4,3,2,1,0:T(8,128)(2,1)}, bf16[2,3,8,256,256]{4,3,2,1,0:T(8,128)(2,1)S(1)}) custom-call(s32[6]{0:T(128)S(1)} %copy-done.1, bf16[2,8,32,384]{3,2,1,0:T(8,128)(2,1)S(1)} %maximum_select_fusion.own, bf16[2,8,32,384]{3,2,1,0:T(8,128)(2,1)} %collective-permute-done.15.sibling), custom_call_target="tpu_custom_call" | custom-call | flops 400000000 | bytes 9000000 | tf_op jit(solution)/shard_map/near/pallas_call | solution.py:359
  83.9 2.7 %copy-done = bf16[2,3,8,256,256]{4,3,2,1,0:T(8,128)(2,1)} copy-done((bf16[2,3,8,256,256]{4,3,2,1,0:T(8,128)(2,1)}, bf16[2,3,8,256,256]{4,3,2,1,0:T(8,128)(2,1)S(1)}, u32[]{:S(2)}) %copy-start) | copy-done | bytes 6291480
  86.6 10.9 %collective-permute-done.17.across = bf16[2,8,32,384]{3,2,1,0:T(8,128)(2,1)S(1)} collective-permute-done((bf16[2,8,32,384]{3,2,1,0:T(8,128)(2,1)}, bf16[2,8,32,384]{3,2,1,0:T(8,128)(2,1)S(1)}, u32[]{:S(2)}, u32[]{:S(2)}) %collective-permute-start.17) | collective-permute-done | bytes 393248 | tf_op jit(solution)/shard_map/ppermute | solution.py:450
  97.5 2.7 %all-to-all-done.1 = bf16[16,128,384]{2,1,0:T(8,128)(2,1)S(1)} async-done(((bf16[16,128,384]{2,1,0:T(8,128)(2,1)}), bf16[16,128,384]{2,1,0:T(8,128)(2,1)S(1)}, u32[]{:S(2)}, u32[]{:S(2)}) %all-to-all-start.1) | async-done | bytes 1572896 | tf_op jit(solution)/shard_map/all_to_all | solution.py:489
  100.2 7.1 %far.1 = bf16[6,2,32,32,384]{4,3,2,1,0:T(8,128)(2,1)} custom-call(s32[6]{0:T(128)S(1)} %copy-done.1, bf16[16,4,2,16,384]{4,3,2,1,0:T(8,128)(2,1)S(1)} %bitcast.7, bf16[2,8,32,384]{3,2,1,0:T(8,128)(2,1)S(1)} %collective-permute-done.17.across, bf16[2,3,8,256,256]{4,3,2,1,0:T(8,128)(2,1)} %copy-done, ...), custom_call_target="tpu_custom_call", output_to_operand_aliasing={{}: (4, {})} | custom-call | tf_op jit(solution)/shard_map/far/pallas_call | solution.py:423
  (25 shorter events, 2.6 us)
Async XLA Ops:
  9.1 58.5 %copy-start.1 = (s32[6]{0:T(128)S(1)}, s32[6]{0:T(128)}, u32[]{:S(2)}) copy-start(s32[6]{0:T(128)} %masks.5) | copy-start | bytes 76
  28.2 10.8 %collective-permute-start.11 = (bf16[16,16,384]{2,1,0:T(8,128)(2,1)S(1)}, bf16[16,16,384]{2,1,0:T(8,128)(2,1)S(1)}, u32[]{:S(2)}, u32[]{:S(2)}) collective-permute-start(bf16[16,16,384]{2,1,0:T(8,128)(2,1)S(1)} %get-tuple-element.48.refs_8_), channel_id=1, source_target_pairs={{0,2},{2,4},{4,6},{6,8},{8,10},{10,12},{12,14},{14,0},{1,3},{3,5},... | collective-permute-start | bytes 589832 | tf_op jit(solution)/shard_map/ppermute | solution.py:457
  29.9 9.1 %collective-permute-start.7 = (bf16[16,16,384]{2,1,0:T(8,128)(2,1)S(1)}, bf16[16,16,384]{2,1,0:T(8,128)(2,1)S(1)}, u32[]{:S(2)}, u32[]{:S(2)}) collective-permute-start(bf16[16,16,384]{2,1,0:T(8,128)(2,1)S(1)} %get-tuple-element.48.refs_8_), channel_id=1, source_target_pairs={{0,14},{2,0},{4,2},{6,4},{8,6},{10,8},{12,10},{14,12},{1,15},{3,1}... | collective-permute-start | bytes 589832 | tf_op jit(solution)/shard_map/ppermute | solution.py:457
  33.9 9.3 %collective-permute-start.3 = (bf16[16,16,384]{2,1,0:T(8,128)(2,1)S(1)}, bf16[16,16,384]{2,1,0:T(8,128)(2,1)S(1)}, u32[]{:S(2)}, u32[]{:S(2)}) collective-permute-start(bf16[16,16,384]{2,1,0:T(8,128)(2,1)S(1)} %get-tuple-element.40.refs_0_), channel_id=1, source_target_pairs={{0,2},{2,4},{4,6},{6,8},{8,10},{10,12},{12,14},{14,0},{1,3},{3,5},... | collective-permute-start | bytes 589832 | tf_op jit(solution)/shard_map/ppermute | solution.py:457
  33.9 9.3 %collective-permute-start = (bf16[16,16,384]{2,1,0:T(8,128)(2,1)S(1)}, bf16[16,16,384]{2,1,0:T(8,128)(2,1)S(1)}, u32[]{:S(2)}, u32[]{:S(2)}) collective-permute-start(bf16[16,16,384]{2,1,0:T(8,128)(2,1)S(1)} %get-tuple-element.40.refs_0_), channel_id=1, source_target_pairs={{0,14},{2,0},{4,2},{6,4},{8,6},{10,8},{12,10},{14,12},{1,15},{3,1}... | collective-permute-start | bytes 589832 | tf_op jit(solution)/shard_map/ppermute | solution.py:457
  36.6 9.3 %collective-permute-start.14 = (bf16[1,8,32,384]{3,2,1,0:T(8,128)(2,1)}, bf16[1,8,32,384]{3,2,1,0:T(8,128)(2,1)S(1)}, u32[]{:S(2)}, u32[]{:S(2)}) collective-permute-start(bf16[1,8,32,384]{3,2,1,0:T(8,128)(2,1)} %get-tuple-element.39), channel_id=1, source_target_pairs={{0,128},{128,0},{1,129},{129,1},{2,130},{130,2},{3,131},{131,3},{4... | collective-permute-start | bytes 589832 | tf_op jit(solution)/shard_map/ppermute | solution.py:450
  39.0 10.7 %collective-permute-start.12 = (bf16[16,16,384]{2,1,0:T(8,128)(2,1)S(1)}, bf16[16,16,384]{2,1,0:T(8,128)(2,1)S(1)}, u32[]{:S(2)}, u32[]{:S(2)}) collective-permute-start(bf16[16,16,384]{2,1,0:T(8,128)(2,1)S(1)} %collective-permute-done.11.refs_15_), channel_id=1, source_target_pairs={{0,2},{2,4},{4,6},{6,8},{8,10},{10,12},{12,14},{14,0},{1,3},{3,5},... | collective-permute-start | bytes 589832 | tf_op jit(solution)/shard_map/ppermute | solution.py:457
  39.0 10.7 %collective-permute-start.8 = (bf16[16,16,384]{2,1,0:T(8,128)(2,1)S(1)}, bf16[16,16,384]{2,1,0:T(8,128)(2,1)S(1)}, u32[]{:S(2)}, u32[]{:S(2)}) collective-permute-start(bf16[16,16,384]{2,1,0:T(8,128)(2,1)S(1)} %collective-permute-done.7.refs_9_), channel_id=1, source_target_pairs={{0,14},{2,0},{4,2},{6,4},{8,6},{10,8},{12,10},{14,12},{1,15},{3,1}... | collective-permute-start | bytes 589832 | tf_op jit(solution)/shard_map/ppermute | solution.py:457
  43.2 7.8 %collective-permute-start.4 = (bf16[16,16,384]{2,1,0:T(8,128)(2,1)S(1)}, bf16[16,16,384]{2,1,0:T(8,128)(2,1)S(1)}, u32[]{:S(2)}, u32[]{:S(2)}) collective-permute-start(bf16[16,16,384]{2,1,0:T(8,128)(2,1)S(1)} %collective-permute-done.3.refs_7_), channel_id=1, source_target_pairs={{0,2},{2,4},{4,6},{6,8},{8,10},{10,12},{12,14},{14,0},{1,3},{3,5},... | collective-permute-start | bytes 589832 | tf_op jit(solution)/shard_map/ppermute | solution.py:457
  43.2 9.6 %collective-permute-start.1 = (bf16[16,16,384]{2,1,0:T(8,128)(2,1)S(1)}, bf16[16,16,384]{2,1,0:T(8,128)(2,1)S(1)}, u32[]{:S(2)}, u32[]{:S(2)}) collective-permute-start(bf16[16,16,384]{2,1,0:T(8,128)(2,1)S(1)} %collective-permute-done.refs_1_), channel_id=1, source_target_pairs={{0,14},{2,0},{4,2},{6,4},{8,6},{10,8},{12,10},{14,12},{1,15},{3,1}... | collective-permute-start | bytes 589832 | tf_op jit(solution)/shard_map/ppermute | solution.py:457
  47.0 15.1 %collective-permute-start.16 = (bf16[2,8,32,384]{3,2,1,0:T(8,128)(2,1)S(1)}, bf16[2,8,32,384]{3,2,1,0:T(8,128)(2,1)}, u32[]{:S(2)}, u32[]{:S(2)}) collective-permute-start(bf16[2,8,32,384]{3,2,1,0:T(8,128)(2,1)S(1)} %maximum_select_fusion.own), channel_id=1, source_target_pairs={{0,113},{1,112},{16,97},{17,96},{32,81},{33,80},{48,65},{49,64},{6... | collective-permute-start | bytes 1179656 | tf_op jit(solution)/shard_map/ppermute | solution.py:450
  49.7 12.4 %collective-permute-start.15 = (bf16[2,8,32,384]{3,2,1,0:T(8,128)(2,1)S(1)}, bf16[2,8,32,384]{3,2,1,0:T(8,128)(2,1)}, u32[]{:S(2)}, u32[]{:S(2)}) collective-permute-start(bf16[2,8,32,384]{3,2,1,0:T(8,128)(2,1)S(1)} %maximum_select_fusion.own), channel_id=1, source_target_pairs={{0,1},{1,0},{2,3},{3,2},{4,5},{5,4},{6,7},{7,6},{8,9},{9,8},{10,11... | collective-permute-start | bytes 1179656 | tf_op jit(solution)/shard_map/ppermute | solution.py:450
  49.7 7.4 %collective-permute-start.13 = (bf16[16,16,384]{2,1,0:T(8,128)(2,1)S(1)}, bf16[16,16,384]{2,1,0:T(8,128)(2,1)S(1)}, u32[]{:S(2)}, u32[]{:S(2)}) collective-permute-start(bf16[16,16,384]{2,1,0:T(8,128)(2,1)S(1)} %collective-permute-done.12.refs_14_), channel_id=1, source_target_pairs={{0,2},{2,4},{4,6},{6,8},{8,10},{10,12},{12,14},{14,0},{1,3},{3,5},... | collective-permute-start | bytes 589832 | tf_op jit(solution)/shard_map/ppermute | solution.py:457
  51.0 6.2 %collective-permute-start.9 = (bf16[16,16,384]{2,1,0:T(8,128)(2,1)S(1)}, bf16[16,16,384]{2,1,0:T(8,128)(2,1)S(1)}, u32[]{:S(2)}, u32[]{:S(2)}) collective-permute-start(bf16[16,16,384]{2,1,0:T(8,128)(2,1)S(1)} %collective-permute-done.8.refs_10_), channel_id=1, source_target_pairs={{0,14},{2,0},{4,2},{6,4},{8,6},{10,8},{12,10},{14,12},{1,15},{3,1}... | collective-permute-start | bytes 589832 | tf_op jit(solution)/shard_map/ppermute | solution.py:457
  52.9 8.4 %collective-permute-start.5 = (bf16[16,16,384]{2,1,0:T(8,128)(2,1)S(1)}, bf16[16,16,384]{2,1,0:T(8,128)(2,1)S(1)}, u32[]{:S(2)}, u32[]{:S(2)}) collective-permute-start(bf16[16,16,384]{2,1,0:T(8,128)(2,1)S(1)} %collective-permute-done.4.refs_6_), channel_id=1, source_target_pairs={{0,2},{2,4},{4,6},{6,8},{8,10},{10,12},{12,14},{14,0},{1,3},{3,5},... | collective-permute-start | bytes 589832 | tf_op jit(solution)/shard_map/ppermute | solution.py:457
  57.2 4.9 %collective-permute-start.2 = (bf16[16,16,384]{2,1,0:T(8,128)(2,1)S(1)}, bf16[16,16,384]{2,1,0:T(8,128)(2,1)S(1)}, u32[]{:S(2)}, u32[]{:S(2)}) collective-permute-start(bf16[16,16,384]{2,1,0:T(8,128)(2,1)S(1)} %collective-permute-done.1.refs_2_), channel_id=1, source_target_pairs={{0,14},{2,0},{4,2},{6,4},{8,6},{10,8},{12,10},{14,12},{1,15},{3,1}... | collective-permute-start | bytes 589832 | tf_op jit(solution)/shard_map/ppermute | solution.py:457
  57.2 8.6 %collective-permute-start.10 = (bf16[16,16,384]{2,1,0:T(8,128)(2,1)S(1)}, bf16[16,16,384]{2,1,0:T(8,128)(2,1)S(1)}, u32[]{:S(2)}, u32[]{:S(2)}) collective-permute-start(bf16[16,16,384]{2,1,0:T(8,128)(2,1)S(1)} %collective-permute-done.9.refs_11_), channel_id=1, source_target_pairs={{0,14},{2,0},{4,2},{6,4},{8,6},{10,8},{12,10},{14,12},{1,15},{3,1}... | collective-permute-start | bytes 589832 | tf_op jit(solution)/shard_map/ppermute | solution.py:457
  61.3 6.3 %collective-permute-start.6 = (bf16[16,16,384]{2,1,0:T(8,128)(2,1)S(1)}, bf16[16,16,384]{2,1,0:T(8,128)(2,1)S(1)}, u32[]{:S(2)}, u32[]{:S(2)}) collective-permute-start(bf16[16,16,384]{2,1,0:T(8,128)(2,1)S(1)} %collective-permute-done.5.refs_5_), channel_id=1, source_target_pairs={{0,2},{2,4},{4,6},{6,8},{8,10},{10,12},{12,14},{14,0},{1,3},{3,5},... | collective-permute-start | bytes 589832 | tf_op jit(solution)/shard_map/ppermute | solution.py:457
  69.5 30.7 %all-to-all-start.1 = ((bf16[16,128,384]{2,1,0:T(8,128)(2,1)}), bf16[16,128,384]{2,1,0:T(8,128)(2,1)S(1)}, u32[]{:S(2)}, u32[]{:S(2)}) async-start(bf16[16,128,384]{2,1,0:T(8,128)(2,1)} %bitcast.4), calls=%async_computation.1 | async-start | bytes 3145728 | tf_op jit(solution)/shard_map/all_to_all | solution.py:489
  77.2 20.3 %collective-permute-start.17 = (bf16[2,8,32,384]{3,2,1,0:T(8,128)(2,1)}, bf16[2,8,32,384]{3,2,1,0:T(8,128)(2,1)S(1)}, u32[]{:S(2)}, u32[]{:S(2)}) collective-permute-start(bf16[2,8,32,384]{3,2,1,0:T(8,128)(2,1)} %collective-permute-done.16), channel_id=1, source_target_pairs={{0,14},{2,12},{4,10},{6,8},{8,6},{10,4},{12,2},{14,0},{1,15},{3,13... | collective-permute-start | bytes 1179656 | tf_op jit(solution)/shard_map/ppermute | solution.py:450
  83.9 2.7 %copy-start = (bf16[2,3,8,256,256]{4,3,2,1,0:T(8,128)(2,1)}, bf16[2,3,8,256,256]{4,3,2,1,0:T(8,128)(2,1)S(1)}, u32[]{:S(2)}) copy-start(bf16[2,3,8,256,256]{4,3,2,1,0:T(8,128)(2,1)S(1)} %get-tuple-element.63.weights) | copy-start | bytes 18874372
